TPU v7x, 512 devices: a whole 4x8x8 slice. The times are simulated.
512 devices in a mesh: seq: 32 (over y_hi, x, core), section: 2 (over y_lo), tp: 8 (over z).
Axes of the slice: x: 4, y: 8 (y_hi: 4, y_lo: 2; y = y_hi * 2 + y_lo), z: 8, core: 2. Of those that a mesh axis runs over, the one named last changes fastest.
Arguments:
- hidden: bfloat16 [32, 3, 8192], P(None, None, 'seq'), may hold values from -1.796875 to 1.796875
- features: bfloat16 [32, 512, 8192], P('seq', ('section', 'tp')), may hold values from -6 to 6
- tiles: int32 [32], P('seq'), may hold values from 1 to 4, as said below
- key_value_weight: bfloat16 [2, 8192, 8, 256], P('section', 'seq', 'tp'), may hold values from -0.0625 to 0.0625
- k_gain: bfloat16 [2, 128], P('section'), may hold values from 1.5 to 2.5
- q_weight: bfloat16 [2, 8192, 8192], P('section', 'seq', 'tp'), may hold values from -0.0625 to 0.0625
- query_gain: bfloat16 [2, 128], P('section'), may hold values from 1.5 to 2.5
- o_weight: bfloat16 [2, 8192, 8192], P('section', 'tp', 'seq'), may hold values from -0.0625 to 0.0625
- attn_gate: float32 [2], P('section'), may hold values from 0.5 to 2
Outputs:
- key_cache: bfloat16 [2, 32, 512, 8, 128], P('section', 'seq', None, 'tp')
- value_cache: bfloat16 [2, 32, 512, 8, 128], P('section', 'seq', None, 'tp')
- section_out: bfloat16 [2, 32, 3, 8192], P('section', None, None, 'seq')
Inputs may be any that keep to these rules, and one draw needn't show every extreme that they name: Request b's first tiles[b] * 128 image slots are valid. Some request has 4 tiles and some has 1.
All inputs are finite; a program needn't handle non-finite values.
Results may differ from a plain program's by a relative error of at most 0.025.
Values may be sent and summed in bfloat16 or wider, within the bound.
No kernel may reach another device: no remote copies, remote signals or barrier semaphores. Data moves between devices by JAX's collectives and lax.ppermute only.
A program may use at most 64 MiB of HBM per device.

v0:
```python
import math

import jax
import jax.numpy as jnp
from jax import lax
from jax.sharding import PartitionSpec as P

TILE_TOK = 128
STEPS = 3


def shifted(value, axis, steps):
    count = lax.axis_size(axis)
    leading, last = (max(0, -steps), min(count, count - steps))
    return lax.ppermute(value, axis, [(source, source + steps) for source in range(leading, last)])


def norm_per_head(values, gain):
    factor = lax.rsqrt(jnp.mean(values * values, axis=-1, keepdims=True) + 1e-05)
    return values * factor * gain.astype(jnp.float32)


def body(
    hidden, features, tiles, key_value_weight, k_gain, q_weight, query_gain, o_weight, attn_gate
):
    head_size = k_gain.shape[1]
    kv_local = key_value_weight.shape[2]
    heads_local = q_weight.shape[2] // head_size
    group_size = heads_local // kv_local
    req_local = tiles.shape[0]
    section_index = lax.axis_index("section")
    full_weight = lax.all_gather(key_value_weight, "seq", axis=1, tiled=True)
    flat_weight = full_weight.reshape(full_weight.shape[1], kv_local * 2 * head_size)
    piece = lax.all_gather(features, ("section", "tp"), axis=1, tiled=True)
    token_count = piece.shape[1]
    projected_rows = jnp.dot(
        piece.reshape(-1, piece.shape[2]), flat_weight, preferred_element_type=jnp.float32
    )
    projected_rows = projected_rows.reshape(req_local, token_count, kv_local, 2 * head_size)
    keys = norm_per_head(projected_rows[..., :head_size], k_gain[0]).astype(jnp.bfloat16)
    built = jnp.concatenate([keys, projected_rows[..., head_size:].astype(jnp.bfloat16)], axis=-1)
    cache_keys = built[..., :head_size]
    cache_values = built[..., head_size:]
    slot_count = built.shape[1]
    live = jnp.arange(slot_count, dtype=jnp.int32)[None, :] < (tiles * TILE_TOK)[:, None]
    gate = jnp.tanh(attn_gate[0])
    query_weight = q_weight[0]
    output_weight = o_weight[0]
    results = []
    received = jnp.zeros_like(hidden[:, :1])
    for tick in range(STEPS + 1):
        pick = min(tick, STEPS - 1)
        current = jnp.where(section_index == 0, hidden[:, pick : pick + 1], received)
        token_positions = current.shape[1]
        flat_state = current.reshape(-1, current.shape[2])
        query_vector = lax.psum_scatter(
            jnp.dot(flat_state, query_weight, preferred_element_type=jnp.float32),
            "seq",
            scatter_dimension=0,
            tiled=True,
        )
        query_vector = norm_per_head(
            query_vector.reshape(req_local, token_positions, kv_local, group_size, head_size),
            query_gain[0],
        ).astype(jnp.bfloat16)
        scores = jnp.einsum(
            "bsgqd,blgd->bsgql", query_vector, cache_keys, preferred_element_type=jnp.float32
        ) / math.sqrt(head_size)
        weights = jnp.where(live[:, None, None, None, :], jnp.exp(scores), 0.0)
        weights = (weights / jnp.sum(weights, axis=-1, keepdims=True)).astype(jnp.bfloat16)
        attended = jnp.einsum(
            "bsgql,blgd->bsgqd", weights, cache_values, preferred_element_type=jnp.float32
        ).astype(jnp.bfloat16)
        attended = attended.reshape(req_local * token_positions, heads_local * head_size)
        partial_out = jnp.dot(
            lax.all_gather(attended, "seq", axis=0, tiled=True),
            output_weight,
            preferred_element_type=jnp.float32,
        )
        summed = lax.psum(partial_out.astype(jnp.bfloat16), "tp").astype(jnp.float32)
        finished = (current.astype(jnp.float32) + gate * summed.reshape(current.shape)).astype(
            jnp.bfloat16
        )
        results.append(finished)
        if tick < STEPS:
            received = shifted(finished, "section", 1)
    earlier = jnp.concatenate(results[:STEPS], axis=1)
    later = jnp.concatenate(results[1:], axis=1)
    section_out = jnp.where(section_index == 0, earlier, later)
    return (cache_keys[None], cache_values[None], section_out[None])


def solution(mesh):
    return jax.shard_map(
        body,
        mesh=mesh,
        in_specs=(
            P(None, None, "seq"),
            P("seq", ("section", "tp"), None),
            P("seq"),
            P("section", "seq", "tp", None),
            P("section", None),
            P("section", "seq", "tp"),
            P("section", None),
            P("section", "tp", "seq"),
            P("section"),
        ),
        out_specs=(
            P("section", "seq", None, "tp", None),
            P("section", "seq", None, "tp", None),
            P("section", None, None, "seq"),
        ),
        check_vma=False,
    )
```

profile of v0, /device:TPU:1, one launch (start us, length us, event | category | flops | bytes accessed | tf_op | source)
XLA Modules:
  0.0 1568.9 jit_solution(15853297761321611263)
XLA Ops:
  7.2 1.0 copy-done
  8.2 1.6 fusion.34
  12.7 1.3 dynamic-slice
  15.3 268.7 %all-reduce.9.cloned.1.call-done = f32[32,1024]{1,0:T(8,128)} async-done(((f32[32,1024]{1,0:T(8,128)}), f32[32,1024]{1,0:T(8,128)}) %all-reduce.9.cloned.1.call-update) | async-done | bytes 131088
  283.9 1.4 dynamic-slice_multiply_fusion.3
  285.6 1.4 convert_reduce_fusion.3
  287.0 66.7 %all-gather.9.cloned.1.call-done = bf16[1,8192,1,256]{3,1,2,0:T(8,128)(2,1)} async-done(((bf16[1,256,1,256]{3,1,2,0:T(8,128)(2,1)}), bf16[1,8192,1,256]{3,1,2,0:T(8,128)(2,1)}) %all-gather.9.cloned.1.call-update) | async-done | bytes 4194320 | tf_op jit(solution)/shard_map/all_gather | solution.py:32
  353.7 104.1 %all-gather.7.cloned.1.call-done = bf16[1,512,8192]{2,1,0:T(8,128)(2,1)} async-done(((bf16[1,32,8192]{2,1,0:T(8,128)(2,1)}), bf16[1,512,8192]{2,1,0:T(8,128)(2,1)}) %all-gather.7.cloned.1.call-update) | async-done | bytes 8388624 | tf_op jit(solution)/shard_map/all_gather | solution.py:34
  457.8 6.9 fusion.3
  465.4 44.6 %all-gather = bf16[32,1,1024]{2,1,0:T(2,128)(2,1)S(1)} all-gather(bf16[1,1,1024]{2,1,0:T(2,128)(2,1)S(1)} %reshape.498), channel_id=1, replica_groups=mesh['seq'=32,'section'=2,'tp'=8] {'seq'}, dimensions={0}, use_global_device_ids=true | all-gather | bytes 67584 | tf_op jit(solution)/shard_map/all_gather | solution.py:76
  510.2 21.0 %psum.28 = bf16[32,256]{1,0:T(8,128)(2,1)S(1)} all-reduce(bf16[32,256]{1,0:T(8,128)(2,1)S(1)} %convolution_convert_fusion.3), channel_id=1, replica_groups=mesh['seq'=32,'section'=2,'tp'=8] {'tp'}, use_global_device_ids=true, to_apply=%region_4.5 | all-reduce | flops 8192 | bytes 32768 | tf_op jit(solution)/shard_map/psum | solution.py:80
  531.1 2.2 collective-permute-start
  534.2 0.9 fusion.32
  535.2 269.9 %all-reduce.11.cloned.1.call-done = f32[32,1024]{1,0:T(8,128)} async-done(((f32[32,1024]{1,0:T(8,128)}), f32[32,1024]{1,0:T(8,128)}) %all-reduce.11.cloned.1.call-update) | async-done | bytes 131088
  805.1 1.4 dynamic-slice_multiply_fusion.2
  806.7 1.4 convert_reduce_fusion.2
  808.6 42.0 %all-gather.1 = bf16[32,1,1024]{2,1,0:T(2,128)(2,1)S(1)} all-gather(bf16[1,1,1024]{2,1,0:T(2,128)(2,1)S(1)} %reshape.500), channel_id=1, replica_groups=mesh['seq'=32,'section'=2,'tp'=8] {'seq'}, dimensions={0}, use_global_device_ids=true | all-gather | bytes 67584 | tf_op jit(solution)/shard_map/all_gather | solution.py:76
  850.8 22.6 %psum.29 = bf16[32,256]{1,0:T(8,128)(2,1)S(1)} all-reduce(bf16[32,256]{1,0:T(8,128)(2,1)S(1)} %convolution_convert_fusion.2), channel_id=1, replica_groups=mesh['seq'=32,'section'=2,'tp'=8] {'tp'}, use_global_device_ids=true, to_apply=%region_8.9 | all-reduce | flops 8192 | bytes 32768 | tf_op jit(solution)/shard_map/psum | solution.py:80
  873.4 3.1 collective-permute-start.1
  877.4 0.9 fusion.30
  878.4 270.7 %all-reduce.13.cloned.1.call-done = f32[32,1024]{1,0:T(8,128)} async-done(((f32[32,1024]{1,0:T(8,128)}), f32[32,1024]{1,0:T(8,128)}) %all-reduce.13.cloned.1.call-update) | async-done | bytes 131088
  1149.1 1.4 dynamic-slice_multiply_fusion.1
  1150.7 1.4 convert_reduce_fusion.1
  1152.6 42.0 %all-gather.2 = bf16[32,1,1024]{2,1,0:T(2,128)(2,1)S(1)} all-gather(bf16[1,1,1024]{2,1,0:T(2,128)(2,1)S(1)} %reshape.502), channel_id=1, replica_groups=mesh['seq'=32,'section'=2,'tp'=8] {'seq'}, dimensions={0}, use_global_device_ids=true | all-gather | bytes 67584 | tf_op jit(solution)/shard_map/all_gather | solution.py:76
  1194.8 22.6 %psum.30 = bf16[32,256]{1,0:T(8,128)(2,1)S(1)} all-reduce(bf16[32,256]{1,0:T(8,128)(2,1)S(1)} %convolution_convert_fusion.1), channel_id=1, replica_groups=mesh['seq'=32,'section'=2,'tp'=8] {'tp'}, use_global_device_ids=true, to_apply=%region_12.13 | all-reduce | flops 8192 | bytes 32768 | tf_op jit(solution)/shard_map/psum | solution.py:80
  1217.4 3.1 collective-permute-start.2
  1221.4 0.9 fusion.28
  1223.1 270.0 %all-reduce.15.cloned.1.call-done = f32[32,1024]{1,0:T(8,128)} async-done(((f32[32,1024]{1,0:T(8,128)}), f32[32,1024]{1,0:T(8,128)}) %all-reduce.15.cloned.1.call-update) | async-done | bytes 131088
  1493.0 1.4 dynamic-slice_multiply_fusion
  1494.7 1.4 convert_reduce_fusion
  1496.5 42.0 %all-gather.3 = bf16[32,1,1024]{2,1,0:T(2,128)(2,1)S(1)} all-gather(bf16[1,1,1024]{2,1,0:T(2,128)(2,1)S(1)} %reshape.504), channel_id=1, replica_groups=mesh['seq'=32,'section'=2,'tp'=8] {'seq'}, dimensions={0}, use_global_device_ids=true | all-gather | bytes 67584 | tf_op jit(solution)/shard_map/all_gather | solution.py:76
  1538.7 22.6 %psum.31 = bf16[32,256]{1,0:T(8,128)(2,1)S(1)} all-reduce(bf16[32,256]{1,0:T(8,128)(2,1)S(1)} %convolution_convert_fusion), channel_id=1, replica_groups=mesh['seq'=32,'section'=2,'tp'=8] {'tp'}, use_global_device_ids=true, to_apply=%region_16.17 | all-reduce | flops 8192 | bytes 32768 | tf_op jit(solution)/shard_map/psum | solution.py:80
  (64 shorter events, 10.5 us)
Async XLA Ops:
  7.2 1.0 copy-start
  7.2 276.8 %all-reduce.9.cloned.1.call-start = ((), (), s32[]{:S(2)}) async-start(), calls=%async_computation.2 | async-start | bytes 262144
  9.8 343.9 %all-gather.9.cloned.1.call-start = ((), (), s32[]{:S(2)}) async-start(), calls=%async_computation.1 | async-start | bytes 4325376 | tf_op jit(solution)/shard_map/all_gather | solution.py:32
  10.6 447.3 %all-gather.7.cloned.1.call-start = ((), (), s32[]{:S(2)}) async-start(), calls=%async_computation | async-start | bytes 8912896 | tf_op jit(solution)/shard_map/all_gather | solution.py:34
  11.3 793.8 %all-reduce.11.cloned.1.call-start = ((), (), s32[]{:S(2)}) async-start(), calls=%async_computation.3 | async-start | bytes 262144
  287.0 223.0 %copy-start.1 = (bf16[1,1024,256]{2,1,0:T(8,128)(2,1)S(1)}, bf16[1,1024,256]{2,1,0:T(8,128)(2,1)}, u32[]{:S(2)}) copy-start(bf16[1,1024,256]{2,1,0:T(8,128)(2,1)} %param.16) | copy-start | bytes 1572868
  287.0 244.1 %copy-start.2 = (bf16[32,3,256]{2,0,1:T(8,128)(2,1)S(1)}, bf16[32,3,256]{2,0,1:T(8,128)(2,1)}, u32[]{:S(2)}) copy-start(bf16[32,3,256]{2,0,1:T(8,128)(2,1)} %param.9) | copy-start | bytes 147460
  531.1 3.1 collective-permute-start
  535.1 614.0 %all-reduce.13.cloned.1.call-start = ((), (), s32[]{:S(2)}) async-start(), calls=%async_computation.4 | async-start | bytes 262144
  873.4 4.0 collective-permute-start.1
  878.3 614.7 %all-reduce.15.cloned.1.call-start = ((), (), s32[]{:S(2)}) async-start(), calls=%async_computation.5 | async-start | bytes 262144
  1217.4 4.0 collective-permute-start.2
Sparse Core Ops, SparseCore 0:
  11.5 272.3 all-reduce.8
  287.5 66.1 all-gather.8
  356.0 101.7 all-gather.6
  535.2 269.8 all-reduce.10
  878.4 270.5 all-reduce.12
  1222.4 270.5 all-reduce.14
where the time goes:
time: 1580 us; the launch traced here: 1570 us
  waiting for transfers between devices  1250 us (79%)
  blocking collectives  260 us (16%)
    unnamed x10, waiting for transfers between devices  1080 us
    all_gather x4, blocking collectives, body(): lax.all_gather(attended, 'seq', axis=0, tiled=True)  171 us
    all_gather x1, waiting for transfers between devices, body(): piece = lax.all_gather(features, ('section', 'tp'), axis=1, tiled=True)  104 us
    psum x4, blocking collectives, body(): lax.psum(partial_out.astype(jnp.bfloat16), 'tp').astype(jnp.float32)  88.8 us
    all_gather x1, waiting for transfers between devices, body(): full_weight = lax.all_gather(key_value_weight, 'seq', axis=1, tiled=True)  66.7 us
  transfers between devices with their start and end apart: 9, of which 8 were waited for; matrix products, arithmetic and copies ran while one was open for 0% of the time, Pallas kernels for 0%

commit v1 on v0

v1 whole, which is shorter than its diff:
```python
import math

import jax
import jax.numpy as jnp
from jax import lax
from jax.sharding import Mesh, PartitionSpec as P

TILE_TOK = 128
SEQ = ("far", "row", "core")
BF16 = jnp.bfloat16
F32 = jnp.float32


def norm_per_head(values, gain):
    factor = lax.rsqrt(jnp.mean(values * values, axis=-1, keepdims=True) + 1e-05)
    return values * factor * gain.astype(F32)


def exchange(blocks, axis):
    return lax.all_to_all(blocks, axis, 0, 0, tiled=True)


def gathered(block, axis):
    return exchange(jnp.broadcast_to(block[None], (lax.axis_size(axis),) + block.shape), axis)


def gather_weight(weight):
    rows, columns = weight.shape
    by_far = gathered(weight, "far")
    by_row = gathered(by_far, "row")
    by_core = gathered(by_row, "core")
    return jnp.transpose(by_core, (2, 1, 0, 3, 4)).reshape(-1, columns)


def layer(state, weight, query_gain, keys, values, live, output_weight, gate):
    requests, positions, width = state.shape
    head_size = keys.shape[1]
    group = weight.shape[1] // head_size
    partial_query = jnp.dot(
        state.reshape(-1, width), weight, preferred_element_type=F32
    ).astype(BF16)
    pieces = exchange(partial_query.reshape(requests, positions, group * head_size), SEQ)
    query = jnp.sum(pieces.astype(F32), axis=0).reshape(positions * group, head_size)
    query = norm_per_head(query, query_gain).astype(BF16)
    scores = jnp.dot(query, keys.T, preferred_element_type=F32) / math.sqrt(head_size)
    weights = jnp.where(live, jnp.exp(scores), 0.0)
    weights = (weights / jnp.sum(weights, axis=-1, keepdims=True)).astype(BF16)
    attended = jnp.dot(weights, values, preferred_element_type=F32).astype(BF16)
    everyone = gathered(attended.reshape(positions, group * head_size), SEQ)
    partial_out = jnp.dot(
        everyone.reshape(requests * positions, -1), output_weight, preferred_element_type=F32
    )
    return (gate * partial_out).astype(BF16)


def body(
    hidden, features, tiles, key_value_weight, k_gain, q_weight, query_gain, o_weight, attn_gate
):
    head_size = k_gain.shape[1]
    section_index = lax.axis_index("section")
    tensor_count = lax.axis_size("tp")
    gate = jnp.tanh(attn_gate[0])

    tokens = lax.all_gather(features[0], ("section", "tp"), axis=0, tiled=True)
    full_weight = gather_weight(key_value_weight[0, :, 0, :])
    projected = jnp.dot(tokens, full_weight, preferred_element_type=F32)
    keys = norm_per_head(projected[:, :head_size], k_gain[0]).astype(BF16)
    values = projected[:, head_size:].astype(BF16)
    live = jnp.arange(keys.shape[0], dtype=jnp.int32)[None, :] < tiles[0] * TILE_TOK

    def step(state):
        return layer(
            state, q_weight[0], query_gain[0], keys, values, live, o_weight[0], gate
        )

    def added(state, pieces):
        total = jnp.sum(pieces.astype(F32), axis=0).reshape(state.shape)
        return (state.astype(F32) + total).astype(BF16)

    everywhere = gathered(step(hidden), ("section", "tp"))
    first = added(hidden, everywhere[:tensor_count])
    second = added(first, gathered(step(first), "tp"))
    section_out = jnp.where(section_index == 0, first, second)
    return (keys[None, None, :, None, :], values[None, None, :, None, :], section_out[None])


def solution(mesh):
    devices = mesh.devices
    fine = Mesh(
        devices.reshape(4, 4, 2, devices.shape[1], devices.shape[2]),
        ("far", "row", "core", "section", "tp"),
    )
    return jax.shard_map(
        body,
        mesh=fine,
        in_specs=(
            P(None, None, SEQ),
            P(SEQ, ("section", "tp"), None),
            P(SEQ),
            P("section", SEQ, "tp", None),
            P("section", None),
            P("section", SEQ, "tp"),
            P("section", None),
            P("section", "tp", SEQ),
            P("section"),
        ),
        out_specs=(
            P("section", SEQ, None, "tp", None),
            P("section", SEQ, None, "tp", None),
            P("section", None, None, SEQ),
        ),
        check_vma=False,
    )
```

time: 1580 us -> 253 us (0.16)
  waiting for transfers between devices: 1250 us -> 82.4 us
  blocking collectives: 260 us -> 117 us
    unnamed x10 -> x1, waiting for transfers between devices: 1080 us -> 0.68 us
    all_gather x4 -> x0, blocking collectives: 171 us -> none  [body(): lax.all_gather(attended, 'seq', axis=0, tiled=True)]
    all_gather x2 -> x1, waiting for transfers between devices: 171 us -> 32.8 us  [body(): tokens = lax.all_gather(features[0], ('section', 'tp'), axis=0, tiled=True)]
    all_to_all x0 -> x6, blocking collectives: none -> 117 us  [exchange(): return lax.all_to_all(blocks, axis, 0, 0, tiled=True)]
    psum x4 -> x0, blocking collectives: 88.8 us -> none  [body(): lax.psum(partial_out.astype(jnp.bfloat16), 'tp').astype(jnp.float32)]
    all_to_all x0 -> x3, waiting for transfers between devices: none -> 48.9 us  [exchange(): return lax.all_to_all(blocks, axis, 0, 0, tiled=True)]
    all_to_all x0 -> x3, starting transfers between devices: none -> 16.4 us  [exchange(): return lax.all_to_all(blocks, axis, 0, 0, tiled=True)]
  transfers between devices with their start and end apart: 9 -> 4, of which waited for: 8 -> 4; matrix products, arithmetic and copies ran while one was open for 0% -> 3% of each run, Pallas kernels for 0% -> 0%
where the time goes in v1:
time: 253 us; the launch traced here: 252 us
  blocking collectives  117 us (46%)
  waiting for transfers between devices  82.4 us (33%)
  starting transfers between devices  16.5 us (7%)
  between operations  15.6 us (6%)
  local copies, waits for them, and re-layouts  11 us (4%)
  matrix products  8.92 us (4%)
    all_to_all x6, blocking collectives, exchange(): return lax.all_to_all(blocks, axis, 0, 0, tiled=True)  117 us
    all_to_all x3, waiting for transfers between devices, exchange(): return lax.all_to_all(blocks, axis, 0, 0, tiled=True)  48.9 us
    all_gather x1, waiting for transfers between devices, body(): tokens = lax.all_gather(features[0], ('section', 'tp'), axis=0, tiled=True)  32.8 us
    all_to_all x3, starting transfers between devices, exchange(): return lax.all_to_all(blocks, axis, 0, 0, tiled=True)  16.4 us
    dot_general x1, matrix products, body(): projected = jnp.dot(tokens, full_weight, preferred_element_type=F32)  7 us
  transfers between devices with their start and end apart: 4, of which 4 were waited for; matrix products, arithmetic and copies ran while one was open for 3% of the time, Pallas kernels for 0%

profile of v1, /device:TPU:1, one launch (start us, length us, event | category | flops | bytes accessed | tf_op | source)
XLA Modules:
  0.0 252.3 jit_solution(16654641795313391678)
XLA Ops:
  7.2 0.7 all-gather.3.cloned.1.call-update
  7.9 0.8 copy.28
  8.8 0.2 convolution_convert_fusion.1
  9.2 24.1 %all_to_all.45 = bf16[32,3,1024]{2,1,0:T(4,128)(2,1)S(1)} all-to-all(bf16[32,3,1024]{2,1,0:T(4,128)(2,1)S(1)} %reshape.82), channel_id=1, replica_groups=mesh['far'=4,'row'=4,'core'=2,'section'=2,'tp'=8] {'far','row','core'}, dimensions={0} | all-to-all | bytes 393216 | tf_op jit(solution)/shard_map/all_to_all | solution.py:20
  33.3 1.0 broadcast_in_dim.43
  34.2 23.7 %all_to_all.46 = bf16[4,256,256]{2,1,0:T(8,128)(2,1)S(1)} all-to-all(bf16[4,256,256]{2,1,0:T(8,128)(2,1)S(1)} %broadcast_in_dim.43), channel_id=1, replica_groups=mesh['far'=4,'row'=4,'core'=2,'section'=2,'tp'=8] {'far'}, dimensions={0} | all-to-all | bytes 1048576 | tf_op jit(solution)/shard_map/all_to_all | solution.py:20
  58.0 1.6 broadcast_in_dim.44
  59.6 3.6 %all-to-all-start.1 = ((bf16[4,4,256,256]{3,2,1,0:T(8,128)(2,1)}), bf16[4,4,256,256]{3,2,1,0:T(8,128)(2,1)S(1)}, u32[]{:S(2)}, u32[]{:S(2)}) async-start(bf16[4,4,256,256]{3,2,1,0:T(8,128)(2,1)} %broadcast_in_dim.44), calls=%async_computation.1 | async-start | bytes 4194304 | tf_op jit(solution)/shard_map/all_to_all | solution.py:20
  64.2 23.5 %all-to-all-done.1 = bf16[4,4,256,256]{3,2,1,0:T(8,128)(2,1)S(1)} async-done(((bf16[4,4,256,256]{3,2,1,0:T(8,128)(2,1)}), bf16[4,4,256,256]{3,2,1,0:T(8,128)(2,1)S(1)}, u32[]{:S(2)}, u32[]{:S(2)}) %all-to-all-start.1) | async-done | bytes 2097184 | tf_op jit(solution)/shard_map/all_to_all | solution.py:20
  87.8 0.5 broadcast_in_dim.82
  88.3 9.6 %all_to_all.47 = bf16[2,4,4,256,256]{4,3,1,2,0:T(8,128)(2,1)S(1)} all-to-all(bf16[2,4,4,256,256]{4,3,1,2,0:T(8,128)(2,1)S(1)} %broadcast_in_dim.82), channel_id=1, replica_groups=mesh['far'=4,'row'=4,'core'=2,'section'=2,'tp'=8] {'core'}, dimensions={0} | all-to-all | bytes 8388608 | tf_op jit(solution)/shard_map/all_to_all | solution.py:20
  97.8 2.3 copy.27
  100.1 32.8 %all-gather.3.cloned.1.call-done = bf16[1,512,8192]{2,1,0:T(8,128)(2,1)} async-done(((bf16[1,32,8192]{2,1,0:T(8,128)(2,1)}), bf16[1,512,8192]{2,1,0:T(8,128)(2,1)}) %all-gather.3.cloned.1.call-update) | async-done | bytes 8388624 | tf_op jit(solution)/shard_map/all_gather | solution.py:64
  132.9 7.0 %fusion = f32[512,256]{0,1:T(8,128)S(1)} fusion(bf16[8192,256]{1,0:T(8,128)(2,1)} %bitcast.38, bf16[1,512,8192]{2,1,0:T(8,128)(2,1)} %all-gather.3.cloned.1.call-done), kind=kOutput, calls=%fused_computation | convolution fusion | flops 2147483648 | bytes 13107200 | tf_op jit(solution)/shard_map/dot_general | solution.py:66
  140.1 0.3 fusion.21
  140.6 0.8 broadcast_in_dim.88
  141.3 9.4 %all-to-all-start.4 = ((bf16[32,3,1024]{2,1,0:T(4,128)(2,1)}), bf16[32,3,1024]{2,1,0:T(4,128)(2,1)S(1)}, u32[]{:S(2)}, u32[]{:S(2)}) async-start(bf16[32,3,1024]{2,1,0:T(4,128)(2,1)} %broadcast_in_dim.88), calls=%async_computation.4 | async-start | bytes 524288 | tf_op jit(solution)/shard_map/all_to_all | solution.py:20
  151.4 12.3 %all-to-all-done.4 = bf16[32,3,1024]{2,1,0:T(4,128)(2,1)S(1)} async-done(((bf16[32,3,1024]{2,1,0:T(4,128)(2,1)}), bf16[32,3,1024]{2,1,0:T(4,128)(2,1)S(1)}, u32[]{:S(2)}, u32[]{:S(2)}) %all-to-all-start.4) | async-done | bytes 196640 | tf_op jit(solution)/shard_map/all_to_all | solution.py:20
  163.9 0.2 fusion.2
  164.2 23.0 %all_to_all.48 = bf16[16,96,256]{2,1,0:T(8,128)(2,1)S(1)} all-to-all(bf16[16,96,256]{2,1,0:T(8,128)(2,1)S(1)} %broadcast_in_dim.89), channel_id=1, replica_groups=mesh['far'=4,'row'=4,'core'=2,'section'=2,'tp'=8] {'section','tp'}, dimensions={0} | all-to-all | bytes 1572864 | tf_op jit(solution)/shard_map/all_to_all | solution.py:20
  187.5 0.2 convolution_convert_fusion
  187.9 19.8 %all_to_all.49 = bf16[32,3,1024]{2,1,0:T(4,128)(2,1)S(1)} all-to-all(bf16[32,3,1024]{2,1,0:T(4,128)(2,1)S(1)} %reshape.87), channel_id=1, replica_groups=mesh['far'=4,'row'=4,'core'=2,'section'=2,'tp'=8] {'far','row','core'}, dimensions={0} | all-to-all | bytes 393216 | tf_op jit(solution)/shard_map/all_to_all | solution.py:20
  208.0 0.3 fusion.22
  208.3 0.2 convolution_convert_fusion.2
  208.6 16.7 %all_to_all.50 = bf16[32,3,1024]{2,1,0:T(4,128)(2,1)S(1)} all-to-all(bf16[32,3,1024]{2,1,0:T(4,128)(2,1)S(1)} %broadcast_in_dim.91), channel_id=1, replica_groups=mesh['far'=4,'row'=4,'core'=2,'section'=2,'tp'=8] {'far','row','core'}, dimensions={0} | all-to-all | bytes 393216 | tf_op jit(solution)/shard_map/all_to_all | solution.py:20
  225.4 0.2 fusion.3
  225.7 0.8 broadcast_in_dim.92
  226.4 3.5 %all-to-all-start.8 = ((bf16[8,96,256]{2,1,0:T(8,128)(2,1)}), bf16[8,96,256]{2,1,0:T(8,128)(2,1)S(1)}, u32[]{:S(2)}, u32[]{:S(2)}) async-start(bf16[8,96,256]{2,1,0:T(8,128)(2,1)} %broadcast_in_dim.92), calls=%async_computation.8 | async-start | bytes 786432 | tf_op jit(solution)/shard_map/all_to_all | solution.py:20
  230.0 0.8 copy.30
  230.8 0.8 copy.31
  231.5 13.1 %all-to-all-done.8 = bf16[8,96,256]{2,1,0:T(8,128)(2,1)S(1)} async-done(((bf16[8,96,256]{2,1,0:T(8,128)(2,1)}), bf16[8,96,256]{2,1,0:T(8,128)(2,1)S(1)}, u32[]{:S(2)}, u32[]{:S(2)}) %all-to-all-start.8) | async-done | bytes 393248 | tf_op jit(solution)/shard_map/all_to_all | solution.py:20
  244.8 0.6 copy.32
  (45 shorter events, 2.3 us)
Async XLA Ops:
  7.2 1.6 copy-start
  7.2 125.7 %all-gather.3.cloned.1.call-start = ((), (), s32[]{:S(2)}) async-start(), calls=%async_computation.9 | async-start | bytes 8912896 | tf_op jit(solution)/shard_map/all_gather | solution.py:64
  33.3 30.6 %copy-start.3 = (bf16[1,128]{1,0:T(2,128)(2,1)S(1)}, bf16[1,128]{1,0:T(2,128)(2,1)}, u32[]{:S(2)}) copy-start(bf16[1,128]{1,0:T(2,128)(2,1)} %param.13) | copy-start | bytes 772
  33.3 30.6 %copy-start.4 = (bf16[1,128]{1,0:T(2,128)(2,1)S(1)}, bf16[1,128]{1,0:T(2,128)(2,1)}, u32[]{:S(2)}) copy-start(bf16[1,128]{1,0:T(2,128)(2,1)} %param.15) | copy-start | bytes 772
  59.6 28.0 %all-to-all-start.1 = ((bf16[4,4,256,256]{3,2,1,0:T(8,128)(2,1)}), bf16[4,4,256,256]{3,2,1,0:T(8,128)(2,1)S(1)}, u32[]{:S(2)}, u32[]{:S(2)}) async-start(bf16[4,4,256,256]{3,2,1,0:T(8,128)(2,1)} %broadcast_in_dim.44), calls=%async_computation.1 | async-start | bytes 4194304 | tf_op jit(solution)/shard_map/all_to_all | solution.py:20
  132.9 31.0 %copy-start.1 = (bf16[1,1024,256]{2,1,0:T(8,128)(2,1)S(1)}, bf16[1,1024,256]{2,1,0:T(8,128)(2,1)}, u32[]{:S(2)}) copy-start(bf16[1,1024,256]{2,1,0:T(8,128)(2,1)} %param.16) | copy-start | bytes 1572868
  139.9 47.5 %copy-start.2 = (bf16[32,3,256]{2,0,1:T(8,128)(2,1)S(1)}, bf16[32,3,256]{2,0,1:T(8,128)(2,1)}, u32[]{:S(2)}) copy-start(bf16[32,3,256]{2,0,1:T(8,128)(2,1)} %param.9) | copy-start | bytes 147460
  141.3 22.4 %all-to-all-start.4 = ((bf16[32,3,1024]{2,1,0:T(4,128)(2,1)}), bf16[32,3,1024]{2,1,0:T(4,128)(2,1)S(1)}, u32[]{:S(2)}, u32[]{:S(2)}) async-start(bf16[32,3,1024]{2,1,0:T(4,128)(2,1)} %broadcast_in_dim.88), calls=%async_computation.4 | async-start | bytes 524288 | tf_op jit(solution)/shard_map/all_to_all | solution.py:20
  226.4 18.2 %all-to-all-start.8 = ((bf16[8,96,256]{2,1,0:T(8,128)(2,1)}), bf16[8,96,256]{2,1,0:T(8,128)(2,1)S(1)}, u32[]{:S(2)}, u32[]{:S(2)}) async-start(bf16[8,96,256]{2,1,0:T(8,128)(2,1)} %broadcast_in_dim.92), calls=%async_computation.8 | async-start | bytes 786432 | tf_op jit(solution)/shard_map/all_to_all | solution.py:20
Sparse Core Ops, SparseCore 0:
  10.1 122.7 all-gather.2

commit v2 on v1

v2 whole, which is shorter than its diff:
```python
import math

import jax
import jax.numpy as jnp
from jax import lax
from jax.sharding import Mesh, PartitionSpec as P

TILE_TOK = 128
SEQ = ("far", "row", "core")
BF16 = jnp.bfloat16
F32 = jnp.float32


def norm_per_head(values, gain):
    factor = lax.rsqrt(jnp.mean(values * values, axis=-1, keepdims=True) + 1e-05)
    return values * factor * gain.astype(F32)


def exchange(blocks, axis):
    return lax.all_to_all(blocks, axis, 0, 0, tiled=True)


def gathered(block, axis):
    return exchange(jnp.broadcast_to(block[None], (lax.axis_size(axis),) + block.shape), axis)


def after(value, *earlier):
    return lax.optimization_barrier((value, *earlier))[0]


def to_query(state, weight):
    requests, positions, width = state.shape
    partial_query = jnp.dot(
        state.reshape(-1, width), weight, preferred_element_type=F32
    ).astype(BF16)
    pieces = exchange(partial_query.reshape(requests, positions, -1), SEQ)
    return jnp.sum(pieces.astype(F32), axis=0)


def attend(query, query_gain, keys, values, live, output_weight, gate):
    positions = query.shape[0]
    head_size = keys.shape[1]
    query = norm_per_head(query.reshape(-1, head_size), query_gain).astype(BF16)
    scores = jnp.dot(query, keys.T, preferred_element_type=F32) / math.sqrt(head_size)
    weights = jnp.where(live, jnp.exp(scores), 0.0)
    weights = (weights / jnp.sum(weights, axis=-1, keepdims=True)).astype(BF16)
    attended = jnp.dot(weights, values, preferred_element_type=F32).astype(BF16)
    everyone = gathered(attended.reshape(positions, -1), SEQ)
    partial_out = jnp.dot(
        everyone.reshape(-1, output_weight.shape[0]), output_weight, preferred_element_type=F32
    )
    return (gate * partial_out).astype(BF16)


def body(
    hidden, features, tiles, key_value_weight, k_gain, q_weight, query_gain, o_weight, attn_gate
):
    head_size = k_gain.shape[1]
    section = lax.axis_index("section")
    tensor_count = lax.axis_size("tp")
    fars, rows, cores = (lax.axis_size(name) for name in SEQ)
    gate = jnp.tanh(attn_gate[0])

    tokens = features.shape[1]
    halves = features.reshape(tokens, fars * rows, cores, -1)
    first_half = halves[:, :, 0].reshape(tokens, -1)
    second_half = halves[:, :, 1].reshape(tokens, -1)
    kept = jnp.where(section == 0, first_half, second_half)
    given = jnp.where(section == 0, second_half, first_half)
    received = lax.ppermute(given, "section", [(0, 1), (1, 0)])
    pair = jnp.where(
        section == 0,
        jnp.stack([kept, received]),
        jnp.stack([received, kept]),
    ).reshape(2 * tokens, -1)

    own_weight = key_value_weight[0, :, 0, :]
    columns = own_weight.shape[1]
    part_rows = own_weight.shape[0] // cores
    parts = jnp.broadcast_to(
        own_weight.reshape(1, cores, part_rows, columns), (2, cores, part_rows, columns)
    )
    parts = exchange(parts.reshape(2 * cores, part_rows, columns), ("section", "core"))
    parts = parts.reshape(2, cores, part_rows, columns)
    parts = jnp.where(section == 0, parts[:, 0], parts[:, 1])
    first_part, second_part = parts[0], parts[1]

    gathered_tokens = lax.all_gather(pair, "tp", axis=0, tiled=True)
    by_core = gathered(gathered(gathered(first_part, "far"), "row"), "core")
    first_weight = jnp.transpose(by_core, (2, 1, 0, 3, 4)).reshape(-1, columns)
    first_query = to_query(after(hidden, by_core), q_weight[0])

    def projected(weight):
        return jnp.dot(gathered_tokens, weight, preferred_element_type=F32)

    def handed(partial_sum, direction):
        return lax.ppermute(partial_sum.astype(BF16), "section", [direction])

    def cache(partial_sum, other):
        total = partial_sum + other.astype(F32)
        keys = norm_per_head(total[:, :head_size], k_gain[0]).astype(BF16)
        return keys, total[:, head_size:].astype(BF16)

    def added(state, pieces):
        total = jnp.sum(pieces.astype(F32), axis=0).reshape(state.shape)
        return (state.astype(F32) + total).astype(BF16)

    slots = jnp.arange(2 * tensor_count * tokens, dtype=jnp.int32)
    place = slots // tokens
    slots = (place % 2 * tensor_count + place // 2) * tokens + slots % tokens
    live = slots[None, :] < tiles[0] * TILE_TOK

    first_partial = projected(first_weight)
    first_keys, first_values = cache(first_partial, handed(first_partial, (1, 0)))
    second_weight = lax.all_gather(
        after(second_part, gathered_tokens), SEQ, axis=0, tiled=True
    )
    first_sum = attend(
        first_query, query_gain[0], first_keys, first_values, live, o_weight[0], gate
    )
    everywhere = gathered(first_sum, ("section", "tp"))
    second_partial = projected(after(second_weight, first_sum))
    second_other = handed(second_partial, (0, 1))
    first = added(hidden, everywhere[:tensor_count])
    second_query = to_query(after(first, second_partial), q_weight[0])
    second_keys, second_values = cache(second_partial, second_other)
    second_sum = attend(
        second_query, query_gain[0], second_keys, second_values, live, o_weight[0], gate
    )
    second = added(first, gathered(second_sum, "tp"))

    def placed(ours, theirs):
        chosen = jnp.where(section == 0, ours, theirs)
        chosen = chosen.reshape(tensor_count, 2, tokens, head_size)
        return jnp.transpose(chosen, (1, 0, 2, 3)).reshape(1, 1, -1, 1, head_size)

    keys = placed(first_keys, second_keys)
    values = placed(first_values, second_values)
    section_out = jnp.where(section == 0, first, second)
    return (keys, values, section_out[None])


def solution(mesh):
    devices = mesh.devices
    fine = Mesh(
        devices.reshape(4, 4, 2, devices.shape[1], devices.shape[2]),
        ("far", "row", "core", "section", "tp"),
    )
    return jax.shard_map(
        body,
        mesh=fine,
        in_specs=(
            P(None, None, SEQ),
            P(SEQ, ("section", "tp"), None),
            P(SEQ),
            P("section", SEQ, "tp", None),
            P("section", None),
            P("section", SEQ, "tp"),
            P("section", None),
            P("section", "tp", SEQ),
            P("section"),
        ),
        out_specs=(
            P("section", SEQ, None, "tp", None),
            P("section", SEQ, None, "tp", None),
            P("section", None, None, SEQ),
        ),
        check_vma=False,
    )
```

time: 253 us -> 231 us (0.913)
  waiting for transfers between devices: 82.4 us -> 61.6 us
  blocking collectives: 117 us -> 99 us
  starting transfers between devices: 16.5 us -> 29.6 us
    all_gather x1 -> x2, waiting for transfers between devices: 32.8 us -> 0.03 us  [the longest x1 0.02 us: body(): lax.all_gather(after(second_part, gathered_tokens), SEQ, axis=0, tiled=True)]
    all_to_all x6, blocking collectives: 117 us -> 99 us  [exchange(): return lax.all_to_all(blocks, axis, 0, 0, tiled=True)]
    ppermute x0 -> x3, waiting for transfers between devices: none -> 12 us  [the longest x2 8.4 us: handed(): return lax.ppermute(partial_sum.astype(BF16), 'section', [direction])]
    ppermute x0 -> x3, starting transfers between devices: none -> 6.94 us  [the longest x1 4.03 us: body(): received = lax.ppermute(given, 'section', [(0, 1), (1, 0)])]
    all_to_all x3 -> x4, starting transfers between devices: 16.4 us -> 22.6 us  [exchange(): return lax.all_to_all(blocks, axis, 0, 0, tiled=True)]
    reshape x8 -> x9, local copies, waits for them, and re-layouts: 0.72 us -> 3.58 us  [the longest x2 1.65 us: to_query(): pieces = exchange(partial_query.reshape(requests, positions, -1), SEQ)]
    broadcast_in_dim x9, local copies, waits for them, and re-layouts: 4.75 us -> 2.1 us  [gathered(): jnp.broadcast_to(block[None], (lax.axis_size(axis),) + block.shape)]
    dot_general x9 -> x10, matrix products: 8.92 us -> 10.3 us  [the longest x2 8.24 us: projected(): return jnp.dot(gathered_tokens, weight, preferred_element_type=F32)]
  transfers between devices with their start and end apart: 4 -> 9, of which waited for: 4 -> 6; matrix products, arithmetic and copies ran while one was open for 3% -> 6% of each run, Pallas kernels for 0% -> 0%
where the time goes in v2:
time: 231 us; the launch traced here: 230 us
  blocking collectives  99 us (43%)
  waiting for transfers between devices  61.6 us (27%)
  starting transfers between devices  29.6 us (13%)
  between operations  15.8 us (7%)
  local copies, waits for them, and re-layouts  11.4 us (5%)
  matrix products  10.3 us (4%)
  other arithmetic  2.31 us (1%)
    all_to_all x6, blocking collectives, exchange(): return lax.all_to_all(blocks, axis, 0, 0, tiled=True)  99 us
    all_to_all x4, waiting for transfers between devices, exchange(): return lax.all_to_all(blocks, axis, 0, 0, tiled=True)  49.5 us
    all_to_all x4, starting transfers between devices, exchange(): return lax.all_to_all(blocks, axis, 0, 0, tiled=True)  22.6 us
    ppermute x2, waiting for transfers between devices, handed(): return lax.ppermute(partial_sum.astype(BF16), 'section', [direction])  8.4 us
    dot_general x2, matrix products, projected(): return jnp.dot(gathered_tokens, weight, preferred_element_type=F32)  8.24 us
  transfers between devices with their start and end apart: 9, of which 6 were waited for; matrix products, arithmetic and copies ran while one was open for 6% of the time, Pallas kernels for 0%

profile of v2, /device:TPU:1, one launch (start us, length us, event | category | flops | bytes accessed | tf_op | source)
XLA Modules:
  0.0 230.0 jit_solution(15920900011219830696)
XLA Ops:
  7.2 1.5 reshape.188
  8.7 1.2 fusion.35
  10.1 4.0 %collective-permute-start = (bf16[32,4096]{1,0:T(8,128)(2,1)S(1)}, bf16[32,4096]{1,0:T(8,128)(2,1)S(1)}, u32[]{:S(2)}, u32[]{:S(2)}) collective-permute-start(bf16[32,4096]{1,0:T(8,128)(2,1)S(1)} %bitcast.63), channel_id=1, source_target_pairs={{0,8},{8,0},{1,9},{9,1},{2,10},{10,2},{3,11},{11,3},{4,12},{12,4},... | collective-permute-start | bytes 786440 | tf_op jit(solution)/shard_map/ppermute | solution.py:70
  14.3 3.6 %collective-permute-done = bf16[32,4096]{1,0:T(8,128)(2,1)S(1)} collective-permute-done((bf16[32,4096]{1,0:T(8,128)(2,1)S(1)}, bf16[32,4096]{1,0:T(8,128)(2,1)S(1)}, u32[]{:S(2)}, u32[]{:S(2)}) %collective-permute-start) | collective-permute-done | bytes 262176 | tf_op jit(solution)/shard_map/ppermute | solution.py:70
  17.9 0.9 maximum_select_fusion
  18.8 14.7 %all_to_all.50 = bf16[4,128,256]{2,1,0:T(8,128)(2,1)S(1)} all-to-all(bf16[4,128,256]{2,1,0:T(8,128)(2,1)S(1)} %bitcast.59), channel_id=1, replica_groups=mesh['far'=4,'row'=4,'core'=2,'section'=2,'tp'=8] {'section','core'}, dimensions={0} | all-to-all | bytes 524288 | tf_op jit(solution)/shard_map/all_to_all | solution.py:20
  33.6 0.6 slice_bitcast_fusion
  34.2 11.3 %all_to_all.51 = bf16[4,128,256]{2,1,0:T(8,128)(2,1)S(1)} all-to-all(bf16[4,128,256]{2,1,0:T(8,128)(2,1)S(1)} %broadcast_in_dim.45), channel_id=1, replica_groups=mesh['far'=4,'row'=4,'core'=2,'section'=2,'tp'=8] {'far'}, dimensions={0} | all-to-all | bytes 524288 | tf_op jit(solution)/shard_map/all_to_all | solution.py:20
  45.6 15.2 %all_to_all.52 = bf16[4,4,128,256]{3,2,1,0:T(8,128)(2,1)S(1)} all-to-all(bf16[4,4,128,256]{3,2,1,0:T(8,128)(2,1)S(1)} %broadcast_in_dim.46), channel_id=1, replica_groups=mesh['far'=4,'row'=4,'core'=2,'section'=2,'tp'=8] {'row'}, dimensions={0} | all-to-all | bytes 2097152 | tf_op jit(solution)/shard_map/all_to_all | solution.py:20
  61.2 9.8 %all_to_all.53 = bf16[2,4,4,128,256]{4,3,1,2,0:T(8,128)(2,1)S(1)} all-to-all(bf16[2,4,4,128,256]{4,3,1,2,0:T(8,128)(2,1)S(1)} %broadcast_in_dim.47), channel_id=1, replica_groups=mesh['far'=4,'row'=4,'core'=2,'section'=2,'tp'=8] {'core'}, dimensions={0} | all-to-all | bytes 4194304 | tf_op jit(solution)/shard_map/all_to_all | solution.py:20
  71.4 0.8 reshape.193
  72.2 6.5 %all-to-all-start.4 = ((bf16[32,3,1024]{2,1,0:T(4,128)(2,1)}), bf16[32,3,1024]{2,1,0:T(4,128)(2,1)S(1)}, u32[]{:S(2)}, u32[]{:S(2)}) async-start(bf16[32,3,1024]{2,1,0:T(4,128)(2,1)} %reshape.193), calls=%async_computation.4 | async-start | bytes 524288 | tf_op jit(solution)/shard_map/all_to_all | solution.py:20
  79.4 1.5 copy.33
  80.9 10.5 %all-to-all-done.4 = bf16[32,3,1024]{2,1,0:T(4,128)(2,1)S(1)} async-done(((bf16[32,3,1024]{2,1,0:T(4,128)(2,1)}), bf16[32,3,1024]{2,1,0:T(4,128)(2,1)S(1)}, u32[]{:S(2)}, u32[]{:S(2)}) %all-to-all-start.4) | async-done | bytes 196640 | tf_op jit(solution)/shard_map/all_to_all | solution.py:20
  91.6 4.1 %fusion.36 = (bf16[512,256]{1,0:T(8,128)(2,1)S(1)}, f32[512,256]{1,0:T(8,128)S(1)}) fusion(bf16[512,4096]{1,0:T(8,128)(2,1)} %all-gather.3.cloned.1.call-done, bf16[4096,256]{1,0:T(8,128)(2,1)} %bitcast.56), kind=kOutput, calls=%fused_computation.87 | convolution fusion | flops 1073872896 | bytes 7077888 | tf_op jit(solution)/shard_map/dot_general | solution.py:94
  95.8 1.4 collective-permute-start.1
  97.3 8.4 %collective-permute-done.1 = bf16[512,256]{1,0:T(8,128)(2,1)S(1)} collective-permute-done((bf16[512,256]{1,0:T(8,128)(2,1)S(1)}, bf16[512,256]{1,0:T(8,128)(2,1)S(1)}, u32[]{:S(2)}, u32[]{:S(2)}) %collective-permute-start.1) | collective-permute-done | bytes 262176 | tf_op jit(solution)/shard_map/ppermute | solution.py:97
  106.6 0.8 broadcast_in_dim.91
  107.3 4.3 %all-to-all-start.5 = ((bf16[32,3,1024]{2,1,0:T(4,128)(2,1)}), bf16[32,3,1024]{2,1,0:T(4,128)(2,1)S(1)}, u32[]{:S(2)}, u32[]{:S(2)}) async-start(bf16[32,3,1024]{2,1,0:T(4,128)(2,1)} %broadcast_in_dim.91), calls=%async_computation.5 | async-start | bytes 524288 | tf_op jit(solution)/shard_map/all_to_all | solution.py:20
  112.4 12.8 %all-to-all-done.5 = bf16[32,3,1024]{2,1,0:T(4,128)(2,1)S(1)} async-done(((bf16[32,3,1024]{2,1,0:T(4,128)(2,1)}), bf16[32,3,1024]{2,1,0:T(4,128)(2,1)S(1)}, u32[]{:S(2)}, u32[]{:S(2)}) %all-to-all-start.5) | async-done | bytes 196640 | tf_op jit(solution)/shard_map/all_to_all | solution.py:20
  125.6 31.7 %all_to_all.54 = bf16[16,96,256]{2,1,0:T(8,128)(2,1)S(1)} all-to-all(bf16[16,96,256]{2,1,0:T(8,128)(2,1)S(1)} %broadcast_in_dim.92), channel_id=1, replica_groups=mesh['far'=4,'row'=4,'core'=2,'section'=2,'tp'=8] {'section','tp'}, dimensions={0} | all-to-all | bytes 1572864 | tf_op jit(solution)/shard_map/all_to_all | solution.py:20
  157.5 4.1 %fusion.38 = (bf16[512,256]{1,0:T(8,128)(2,1)S(1)}, f32[512,256]{1,0:T(8,128)S(1)}) fusion(bf16[512,4096]{1,0:T(8,128)(2,1)} %all-gather.3.cloned.1.call-done, bf16[4096,256]{1,0:T(8,128)(2,1)} %all-gather.5.cloned.1.call-done), kind=kOutput, calls=%fused_computation.89 | convolution fusion | flops 1073872896 | bytes 7077888 | tf_op jit(solution)/shard_map/dot_general | solution.py:94
  161.6 1.5 collective-permute-start.2
  163.4 0.8 reshape.202
  164.2 6.5 %all-to-all-start.7 = ((bf16[32,3,1024]{2,1,0:T(4,128)(2,1)}), bf16[32,3,1024]{2,1,0:T(4,128)(2,1)S(1)}, u32[]{:S(2)}, u32[]{:S(2)}) async-start(bf16[32,3,1024]{2,1,0:T(4,128)(2,1)} %reshape.202), calls=%async_computation.7 | async-start | bytes 524288 | tf_op jit(solution)/shard_map/all_to_all | solution.py:20
  170.9 12.5 %all-to-all-done.7 = bf16[32,3,1024]{2,1,0:T(4,128)(2,1)S(1)} async-done(((bf16[32,3,1024]{2,1,0:T(4,128)(2,1)}), bf16[32,3,1024]{2,1,0:T(4,128)(2,1)S(1)}, u32[]{:S(2)}, u32[]{:S(2)}) %all-to-all-start.7) | async-done | bytes 196640 | tf_op jit(solution)/shard_map/all_to_all | solution.py:20
  184.4 16.2 %all_to_all.55 = bf16[32,3,1024]{2,1,0:T(4,128)(2,1)S(1)} all-to-all(bf16[32,3,1024]{2,1,0:T(4,128)(2,1)S(1)} %broadcast_in_dim.94), channel_id=1, replica_groups=mesh['far'=4,'row'=4,'core'=2,'section'=2,'tp'=8] {'far','row','core'}, dimensions={0} | all-to-all | bytes 393216 | tf_op jit(solution)/shard_map/all_to_all | solution.py:20
  201.1 0.8 broadcast_in_dim.95
  201.9 5.4 %all-to-all-start.9 = ((bf16[8,96,256]{2,1,0:T(8,128)(2,1)}), bf16[8,96,256]{2,1,0:T(8,128)(2,1)S(1)}, u32[]{:S(2)}, u32[]{:S(2)}) async-start(bf16[8,96,256]{2,1,0:T(8,128)(2,1)} %broadcast_in_dim.95), calls=%async_computation.9 | async-start | bytes 786432 | tf_op jit(solution)/shard_map/all_to_all | solution.py:20
  207.5 0.7 copy.35
  208.1 0.7 copy.36
  208.8 13.6 %all-to-all-done.9 = bf16[8,96,256]{2,1,0:T(8,128)(2,1)S(1)} async-done(((bf16[8,96,256]{2,1,0:T(8,128)(2,1)}), bf16[8,96,256]{2,1,0:T(8,128)(2,1)S(1)}, u32[]{:S(2)}, u32[]{:S(2)}) %all-to-all-start.9) | async-done | bytes 393248 | tf_op jit(solution)/shard_map/all_to_all | solution.py:20
  (69 shorter events, 5.7 us)
Async XLA Ops:
  7.2 64.0 %copy-start = (bf16[1,256,1024]{2,1,0:T(8,128)(2,1)S(1)}, bf16[1,256,1024]{2,1,0:T(8,128)(2,1)}, u32[]{:S(2)}) copy-start(bf16[1,256,1024]{2,1,0:T(8,128)(2,1)} %param.14) | copy-start | bytes 1572868
  7.2 84.4 %all-gather.3.cloned.1.call-start = ((), (), s32[]{:S(2)}) async-start(), calls=%async_computation.10 | async-start | bytes 4718592 | tf_op jit(solution)/shard_map/all_gather | solution.py:88
  9.9 8.9 %copy-start.3 = (bf16[1,256,1,256]{3,1,2,0:T(8,128)(2,1)S(1)}, bf16[1,256,1,256]{3,1,2,0:T(8,128)(2,1)}, u32[]{:S(2)}) copy-start(bf16[1,256,1,256]{3,1,2,0:T(8,128)(2,1)} %param.12) | copy-start | bytes 393220
  10.1 7.8 %collective-permute-start = (bf16[32,4096]{1,0:T(8,128)(2,1)S(1)}, bf16[32,4096]{1,0:T(8,128)(2,1)S(1)}, u32[]{:S(2)}, u32[]{:S(2)}) collective-permute-start(bf16[32,4096]{1,0:T(8,128)(2,1)S(1)} %bitcast.63), channel_id=1, source_target_pairs={{0,8},{8,0},{1,9},{9,1},{2,10},{10,2},{3,11},{11,3},{4,12},{12,4},... | collective-permute-start | bytes 786440 | tf_op jit(solution)/shard_map/ppermute | solution.py:70
  61.2 9.8 %copy-start.2 = (bf16[32,3,256]{2,0,1:T(8,128)(2,1)S(1)}, bf16[32,3,256]{2,0,1:T(8,128)(2,1)}, u32[]{:S(2)}) copy-start(bf16[32,3,256]{2,0,1:T(8,128)(2,1)} %param.9) | copy-start | bytes 147460
  61.2 18.2 %copy-start.4 = (bf16[1,128]{1,0:T(2,128)(2,1)S(1)}, bf16[1,128]{1,0:T(2,128)(2,1)}, u32[]{:S(2)}) copy-start(bf16[1,128]{1,0:T(2,128)(2,1)} %param.15) | copy-start | bytes 772
  61.2 18.2 %copy-start.5 = (bf16[1,128]{1,0:T(2,128)(2,1)S(1)}, bf16[1,128]{1,0:T(2,128)(2,1)}, u32[]{:S(2)}) copy-start(bf16[1,128]{1,0:T(2,128)(2,1)} %param.13) | copy-start | bytes 772
  72.2 19.3 %all-to-all-start.4 = ((bf16[32,3,1024]{2,1,0:T(4,128)(2,1)}), bf16[32,3,1024]{2,1,0:T(4,128)(2,1)S(1)}, u32[]{:S(2)}, u32[]{:S(2)}) async-start(bf16[32,3,1024]{2,1,0:T(4,128)(2,1)} %reshape.193), calls=%async_computation.4 | async-start | bytes 524288 | tf_op jit(solution)/shard_map/all_to_all | solution.py:20
  78.7 78.8 %all-gather.5.cloned.1.call-start = ((), (), s32[]{:S(2)}) async-start(), calls=%async_computation.11 | async-start | bytes 2162688 | tf_op jit(solution)/shard_map/all_gather | solution.py:115
  95.8 29.5 %copy-start.1 = (bf16[1,1024,256]{2,1,0:T(8,128)(2,1)S(1)}, bf16[1,1024,256]{2,1,0:T(8,128)(2,1)}, u32[]{:S(2)}) copy-start(bf16[1,1024,256]{2,1,0:T(8,128)(2,1)} %param.16) | copy-start | bytes 1572868
  95.8 9.9 %collective-permute-start.1 = (bf16[512,256]{1,0:T(8,128)(2,1)S(1)}, bf16[512,256]{1,0:T(8,128)(2,1)S(1)}, u32[]{:S(2)}, u32[]{:S(2)}) collective-permute-start(bf16[512,256]{1,0:T(8,128)(2,1)S(1)} %get-tuple-element.28), channel_id=1, source_target_pairs={{8,0},{9,1},{10,2},{11,3},{12,4},{13,5},{14,6},{15,7},{24,16},{25,... | collective-permute-start | bytes 786440 | tf_op jit(solution)/shard_map/ppermute | solution.py:97
  107.3 17.8 %all-to-all-start.5 = ((bf16[32,3,1024]{2,1,0:T(4,128)(2,1)}), bf16[32,3,1024]{2,1,0:T(4,128)(2,1)S(1)}, u32[]{:S(2)}, u32[]{:S(2)}) async-start(bf16[32,3,1024]{2,1,0:T(4,128)(2,1)} %broadcast_in_dim.91), calls=%async_computation.5 | async-start | bytes 524288 | tf_op jit(solution)/shard_map/all_to_all | solution.py:20
  161.6 9.1 %collective-permute-start.2 = (bf16[512,256]{1,0:T(8,128)(2,1)S(1)}, bf16[512,256]{1,0:T(8,128)(2,1)S(1)}, u32[]{:S(2)}, u32[]{:S(2)}) collective-permute-start(bf16[512,256]{1,0:T(8,128)(2,1)S(1)} %get-tuple-element.32), channel_id=1, source_target_pairs={{0,8},{1,9},{2,10},{3,11},{4,12},{5,13},{6,14},{7,15},{16,24},{17,... | collective-permute-start | bytes 786440 | tf_op jit(solution)/shard_map/ppermute | solution.py:97
  164.2 19.2 %all-to-all-start.7 = ((bf16[32,3,1024]{2,1,0:T(4,128)(2,1)}), bf16[32,3,1024]{2,1,0:T(4,128)(2,1)S(1)}, u32[]{:S(2)}, u32[]{:S(2)}) async-start(bf16[32,3,1024]{2,1,0:T(4,128)(2,1)} %reshape.202), calls=%async_computation.7 | async-start | bytes 524288 | tf_op jit(solution)/shard_map/all_to_all | solution.py:20
  201.9 20.6 %all-to-all-start.9 = ((bf16[8,96,256]{2,1,0:T(8,128)(2,1)}), bf16[8,96,256]{2,1,0:T(8,128)(2,1)S(1)}, u32[]{:S(2)}, u32[]{:S(2)}) async-start(bf16[8,96,256]{2,1,0:T(8,128)(2,1)} %broadcast_in_dim.95), calls=%async_computation.9 | async-start | bytes 786432 | tf_op jit(solution)/shard_map/all_to_all | solution.py:20
Sparse Core Ops, SparseCore 0:
  18.9 65.8 all-gather.2
  91.8 62.8 all-gather.4

commit v3 on v2

--- a/solution.py
+++ b/solution.py
@@ -3,6 +3,8 @@
 import jax
 import jax.numpy as jnp
 from jax import lax
+from jax.experimental import pallas as pl
+from jax.experimental.pallas import tpu as pltpu
 from jax.sharding import Mesh, PartitionSpec as P
 
 TILE_TOK = 128
@@ -26,6 +28,28 @@
 
 def after(value, *earlier):
     return lax.optimization_barrier((value, *earlier))[0]
+
+
+def halved(rows, run):
+    count, width = rows.shape
+
+    def deal(rows_ref, halves_ref):
+        for column in range(0, width, 2 * run):
+            to = pl.ds(column // 2, run)
+            halves_ref[0, :, to] = rows_ref[:, pl.ds(column, run)]
+            halves_ref[1, :, to] = rows_ref[:, pl.ds(column + run, run)]
+
+    return pl.pallas_call(
+        deal,
+        out_shape=jax.ShapeDtypeStruct((2, count, width // 2), rows.dtype),
+        in_specs=[pl.BlockSpec(memory_space=pltpu.VMEM)],
+        out_specs=pl.BlockSpec(memory_space=pltpu.VMEM),
+        compiler_params=pltpu.CompilerParams(vmem_limit_bytes=4 * 1024 * 1024),
+        cost_estimate=pl.CostEstimate(
+            flops=0, bytes_accessed=4 * count * width, transcendentals=0
+        ),
+        name="deal_halves",
+    )(rows)
 
 
 def to_query(state, weight):
@@ -61,28 +85,13 @@
     fars, rows, cores = (lax.axis_size(name) for name in SEQ)
     gate = jnp.tanh(attn_gate[0])
 
-    tokens = features.shape[1]
-    halves = features.reshape(tokens, fars * rows, cores, -1)
-    first_half = halves[:, :, 0].reshape(tokens, -1)
-    second_half = halves[:, :, 1].reshape(tokens, -1)
-    kept = jnp.where(section == 0, first_half, second_half)
-    given = jnp.where(section == 0, second_half, first_half)
-    received = lax.ppermute(given, "section", [(0, 1), (1, 0)])
-    pair = jnp.where(
-        section == 0,
-        jnp.stack([kept, received]),
-        jnp.stack([received, kept]),
-    ).reshape(2 * tokens, -1)
+    tokens, width = features.shape[1:]
+    run = width // (fars * rows * cores * 2)
+    pair = exchange(halved(features[0], run), "section").reshape(2 * tokens, -1)
 
     own_weight = key_value_weight[0, :, 0, :]
     columns = own_weight.shape[1]
-    part_rows = own_weight.shape[0] // cores
-    parts = jnp.broadcast_to(
-        own_weight.reshape(1, cores, part_rows, columns), (2, cores, part_rows, columns)
-    )
-    parts = exchange(parts.reshape(2 * cores, part_rows, columns), ("section", "core"))
-    parts = parts.reshape(2, cores, part_rows, columns)
-    parts = jnp.where(section == 0, parts[:, 0], parts[:, 1])
+    parts = exchange(after(own_weight, pair).reshape(2, run, columns), "section")
     first_part, second_part = parts[0], parts[1]
 
     gathered_tokens = lax.all_gather(pair, "tp", axis=0, tiled=True)
@@ -101,9 +110,8 @@
         keys = norm_per_head(total[:, :head_size], k_gain[0]).astype(BF16)
         return keys, total[:, head_size:].astype(BF16)
 
-    def added(state, pieces):
-        total = jnp.sum(pieces.astype(F32), axis=0).reshape(state.shape)
-        return (state.astype(F32) + total).astype(BF16)
+    def added(state, total):
+        return (state.astype(F32) + total.reshape(state.shape)).astype(BF16)
 
     slots = jnp.arange(2 * tensor_count * tokens, dtype=jnp.int32)
     place = slots // tokens
@@ -118,16 +126,17 @@
     first_sum = attend(
         first_query, query_gain[0], first_keys, first_values, live, o_weight[0], gate
     )
-    everywhere = gathered(first_sum, ("section", "tp"))
-    second_partial = projected(after(second_weight, first_sum))
+    first_sum = first_sum.reshape(tensor_count, -1, first_sum.shape[1])
+    summed = jnp.sum(exchange(first_sum, "tp").astype(F32), axis=0).astype(BF16)
+    first = added(hidden, gathered(summed, ("section", "tp"))[:tensor_count].astype(F32))
+    second_partial = projected(after(second_weight, first))
     second_other = handed(second_partial, (0, 1))
-    first = added(hidden, everywhere[:tensor_count])
-    second_query = to_query(after(first, second_partial), q_weight[0])
+    second_query = to_query(first, q_weight[0])
     second_keys, second_values = cache(second_partial, second_other)
     second_sum = attend(
         second_query, query_gain[0], second_keys, second_values, live, o_weight[0], gate
     )
-    second = added(first, gathered(second_sum, "tp"))
+    second = added(first, jnp.sum(gathered(second_sum, "tp").astype(F32), axis=0))
 
     def placed(ours, theirs):
         chosen = jnp.where(section == 0, ours, theirs)

time: 231 us -> 225 us (0.974)
  blocking collectives: 99 us -> 119 us
  waiting for transfers between devices: 61.6 us -> 50.4 us
  starting transfers between devices: 29.6 us -> 19.3 us
    all_to_all x4 -> x3, waiting for transfers between devices: 49.5 us -> 26.9 us  [exchange(): return lax.all_to_all(blocks, axis, 0, 0, tiled=True)]
    all_to_all x6 -> x9, blocking collectives: 99 us -> 119 us  [exchange(): return lax.all_to_all(blocks, axis, 0, 0, tiled=True)]
    all_gather x1, waiting for transfers between devices: 0.01 us -> 9.53 us  [body(): gathered_tokens = lax.all_gather(pair, 'tp', axis=0, tiled=True)]
    all_to_all x4 -> x3, starting transfers between devices: 22.6 us -> 16.2 us  [exchange(): return lax.all_to_all(blocks, axis, 0, 0, tiled=True)]
    ppermute x2, waiting for transfers between devices: 8.4 us -> 14 us  [handed(): return lax.ppermute(partial_sum.astype(BF16), 'section', [direction])]
    ppermute x1 -> x0, starting transfers between devices: 4.03 us -> none  [body(): received = lax.ppermute(given, 'section', [(0, 1), (1, 0)])]
    ppermute x1 -> x0, waiting for transfers between devices: 3.61 us -> none  [body(): received = lax.ppermute(given, 'section', [(0, 1), (1, 0)])]
  transfers between devices with their start and end apart: 9 -> 7, of which waited for: 6 -> 6; matrix products, arithmetic and copies ran while one was open for 6% -> 6% of each run, Pallas kernels for 0% -> 0%
where the time goes in v3:
time: 225 us; the launch traced here: 224 us
  blocking collectives  119 us (53%)
  waiting for transfers between devices  50.4 us (22%)
  starting transfers between devices  19.3 us (9%)
  between operations  15.7 us (7%)
  matrix products  10.2 us (5%)
  local copies, waits for them, and re-layouts  9.1 us (4%)
    all_to_all x9, blocking collectives, exchange(): return lax.all_to_all(blocks, axis, 0, 0, tiled=True)  119 us
    all_to_all x3, waiting for transfers between devices, exchange(): return lax.all_to_all(blocks, axis, 0, 0, tiled=True)  26.9 us
    all_to_all x3, starting transfers between devices, exchange(): return lax.all_to_all(blocks, axis, 0, 0, tiled=True)  16.2 us
    ppermute x2, waiting for transfers between devices, handed(): return lax.ppermute(partial_sum.astype(BF16), 'section', [direction])  14 us
    all_gather x1, waiting for transfers between devices, body(): gathered_tokens = lax.all_gather(pair, 'tp', axis=0, tiled=True)  9.53 us
    dot_general x2, matrix products, projected(): return jnp.dot(gathered_tokens, weight, preferred_element_type=F32)  8.24 us
  transfers between devices with their start and end apart: 7, of which 6 were waited for; matrix products, arithmetic and copies ran while one was open for 6% of the time, Pallas kernels for 0%

profile of v3, /device:TPU:1, one launch (start us, length us, event | category | flops | bytes accessed | tf_op | source)
XLA Modules:
  0.0 224.4 jit_solution(3940293053100446729)
XLA Ops:
  7.2 1.1 copy-done.1
  8.4 9.2 %all_to_all.60 = bf16[2,32,4096]{2,1,0:T(8,128)(2,1)} all-to-all(bf16[2,32,4096]{2,1,0:T(8,128)(2,1)S(1)} %deal_halves.1), channel_id=1, replica_groups=mesh['far'=4,'row'=4,'core'=2,'section'=2,'tp'=8] {'section'}, dimensions={0} | all-to-all | bytes 1048576 | tf_op jit(solution)/shard_map/all_to_all | solution.py:22
  17.7 6.8 %all_to_all.61 = bf16[2,128,256]{2,1,0:T(8,128)(2,1)S(1)} all-to-all(bf16[2,128,256]{2,1,0:T(8,128)(2,1)S(1)} %bitcast.56), channel_id=1, replica_groups=mesh['far'=4,'row'=4,'core'=2,'section'=2,'tp'=8] {'section'}, dimensions={0} | all-to-all | bytes 262144 | tf_op jit(solution)/shard_map/all_to_all | solution.py:22
  24.5 0.6 slice_bitcast_fusion
  25.2 15.9 %all_to_all.62 = bf16[4,128,256]{2,1,0:T(8,128)(2,1)S(1)} all-to-all(bf16[4,128,256]{2,1,0:T(8,128)(2,1)S(1)} %broadcast_in_dim.39), channel_id=1, replica_groups=mesh['far'=4,'row'=4,'core'=2,'section'=2,'tp'=8] {'far'}, dimensions={0} | all-to-all | bytes 524288 | tf_op jit(solution)/shard_map/all_to_all | solution.py:22
  41.1 13.8 %all_to_all.63 = bf16[4,4,128,256]{3,2,1,0:T(8,128)(2,1)S(1)} all-to-all(bf16[4,4,128,256]{3,2,1,0:T(8,128)(2,1)S(1)} %broadcast_in_dim.40), channel_id=1, replica_groups=mesh['far'=4,'row'=4,'core'=2,'section'=2,'tp'=8] {'row'}, dimensions={0} | all-to-all | bytes 2097152 | tf_op jit(solution)/shard_map/all_to_all | solution.py:22
  55.3 11.2 %all_to_all.64 = bf16[2,4,4,128,256]{4,3,1,2,0:T(8,128)(2,1)S(1)} all-to-all(bf16[2,4,4,128,256]{4,3,1,2,0:T(8,128)(2,1)S(1)} %broadcast_in_dim.41), channel_id=1, replica_groups=mesh['far'=4,'row'=4,'core'=2,'section'=2,'tp'=8] {'core'}, dimensions={0} | all-to-all | bytes 4194304 | tf_op jit(solution)/shard_map/all_to_all | solution.py:22
  66.9 0.8 reshape.162
  67.7 4.2 %all-to-all-start.5 = ((bf16[32,3,1024]{2,1,0:T(4,128)(2,1)}), bf16[32,3,1024]{2,1,0:T(4,128)(2,1)S(1)}, u32[]{:S(2)}, u32[]{:S(2)}) async-start(bf16[32,3,1024]{2,1,0:T(4,128)(2,1)} %reshape.162), calls=%async_computation.5 | async-start | bytes 524288 | tf_op jit(solution)/shard_map/all_to_all | solution.py:22
  72.7 1.5 copy.36
  74.2 9.5 %all-gather.3.cloned.1.call-done = bf16[512,4096]{1,0:T(8,128)(2,1)} async-done(((bf16[64,4096]{1,0:T(8,128)(2,1)}), bf16[512,4096]{1,0:T(8,128)(2,1)}) %all-gather.3.cloned.1.call-update) | async-done | bytes 4194320 | tf_op jit(solution)/shard_map/all_gather | solution.py:97
  83.7 1.4 all-to-all-done.5
  85.3 4.1 %fusion.35 = (bf16[512,256]{0,1:T(8,128)(2,1)S(1)}, f32[512,256]{0,1:T(8,128)S(1)}) fusion(bf16[4096,256]{1,0:T(8,128)(2,1)} %bitcast.52, bf16[512,4096]{1,0:T(8,128)(2,1)} %all-gather.3.cloned.1.call-done), kind=kOutput, calls=%fused_computation.84 | convolution fusion | flops 1073872896 | bytes 7077888 | tf_op jit(solution)/shard_map/dot_general | solution.py:103
  89.4 1.4 collective-permute-start
  91.0 8.5 %collective-permute-done = bf16[512,256]{0,1:T(8,128)(2,1)S(1)} collective-permute-done((bf16[512,256]{0,1:T(8,128)(2,1)S(1)}, bf16[512,256]{0,1:T(8,128)(2,1)S(1)}, u32[]{:S(2)}, u32[]{:S(2)}) %collective-permute-start) | collective-permute-done | bytes 262176 | tf_op jit(solution)/shard_map/ppermute | solution.py:106
  99.6 0.3 fusion.36
  100.2 0.8 broadcast_in_dim.82
  101.0 8.6 %all-to-all-start.6 = ((bf16[32,3,1024]{2,1,0:T(4,128)(2,1)}), bf16[32,3,1024]{2,1,0:T(4,128)(2,1)S(1)}, u32[]{:S(2)}, u32[]{:S(2)}) async-start(bf16[32,3,1024]{2,1,0:T(4,128)(2,1)} %broadcast_in_dim.82), calls=%async_computation.6 | async-start | bytes 524288 | tf_op jit(solution)/shard_map/all_to_all | solution.py:22
  110.2 12.2 %all-to-all-done.6 = bf16[32,3,1024]{2,1,0:T(4,128)(2,1)S(1)} async-done(((bf16[32,3,1024]{2,1,0:T(4,128)(2,1)}), bf16[32,3,1024]{2,1,0:T(4,128)(2,1)S(1)}, u32[]{:S(2)}, u32[]{:S(2)}) %all-to-all-start.6) | async-done | bytes 196640 | tf_op jit(solution)/shard_map/all_to_all | solution.py:22
  122.9 13.3 %all_to_all.65 = bf16[8,12,256]{2,1,0:T(8,128)(2,1)S(1)} all-to-all(bf16[8,12,256]{2,1,0:T(8,128)(2,1)S(1)} %reshape.165), channel_id=1, replica_groups=mesh['far'=4,'row'=4,'core'=2,'section'=2,'tp'=8] {'tp'}, dimensions={0} | all-to-all | bytes 98304 | tf_op jit(solution)/shard_map/all_to_all | solution.py:22
  136.2 12.3 %all_to_all.66 = bf16[16,12,256]{2,1,0:T(8,128)(2,1)S(1)} all-to-all(bf16[16,12,256]{2,1,0:T(8,128)(2,1)S(1)} %broadcast_in_dim.83), channel_id=1, replica_groups=mesh['far'=4,'row'=4,'core'=2,'section'=2,'tp'=8] {'section','tp'}, dimensions={0} | all-to-all | bytes 196608 | tf_op jit(solution)/shard_map/all_to_all | solution.py:22
  149.0 18.0 %all_to_all.67 = bf16[32,3,1024]{2,1,0:T(4,128)(2,1)S(1)} all-to-all(bf16[32,3,1024]{2,1,0:T(4,128)(2,1)S(1)} %reshape.173), channel_id=1, replica_groups=mesh['far'=4,'row'=4,'core'=2,'section'=2,'tp'=8] {'far','row','core'}, dimensions={0} | all-to-all | bytes 393216 | tf_op jit(solution)/shard_map/all_to_all | solution.py:22
  167.2 4.1 %fusion.37 = (bf16[512,256]{0,1:T(8,128)(2,1)S(1)}, f32[512,256]{0,1:T(8,128)S(1)}) fusion(bf16[4096,256]{1,0:T(8,128)(2,1)} %all-gather.5.cloned.1.call-done, bf16[512,4096]{1,0:T(8,128)(2,1)} %all-gather.3.cloned.1.call-done), kind=kOutput, calls=%fused_computation.86 | convolution fusion | flops 1073872896 | bytes 7077888 | tf_op jit(solution)/shard_map/dot_general | solution.py:103
  171.3 1.5 collective-permute-start.1
  172.9 5.5 %collective-permute-done.1 = bf16[512,256]{0,1:T(8,128)(2,1)S(1)} collective-permute-done((bf16[512,256]{0,1:T(8,128)(2,1)S(1)}, bf16[512,256]{0,1:T(8,128)(2,1)S(1)}, u32[]{:S(2)}, u32[]{:S(2)}) %collective-permute-start.1) | collective-permute-done | bytes 262176 | tf_op jit(solution)/shard_map/ppermute | solution.py:106
  179.2 18.1 %all_to_all.68 = bf16[32,3,1024]{2,1,0:T(4,128)(2,1)S(1)} all-to-all(bf16[32,3,1024]{2,1,0:T(4,128)(2,1)S(1)} %broadcast_in_dim.85), channel_id=1, replica_groups=mesh['far'=4,'row'=4,'core'=2,'section'=2,'tp'=8] {'far','row','core'}, dimensions={0} | all-to-all | bytes 393216 | tf_op jit(solution)/shard_map/all_to_all | solution.py:22
  197.7 0.8 broadcast_in_dim.86
  198.4 3.5 %all-to-all-start.11 = ((bf16[8,96,256]{2,1,0:T(8,128)(2,1)}), bf16[8,96,256]{2,1,0:T(8,128)(2,1)S(1)}, u32[]{:S(2)}, u32[]{:S(2)}) async-start(bf16[8,96,256]{2,1,0:T(8,128)(2,1)} %broadcast_in_dim.86), calls=%async_computation.11 | async-start | bytes 786432 | tf_op jit(solution)/shard_map/all_to_all | solution.py:22
  202.2 0.7 copy.40
  202.9 0.7 copy.42
  203.6 13.2 %all-to-all-done.11 = bf16[8,96,256]{2,1,0:T(8,128)(2,1)S(1)} async-done(((bf16[8,96,256]{2,1,0:T(8,128)(2,1)}), bf16[8,96,256]{2,1,0:T(8,128)(2,1)S(1)}, u32[]{:S(2)}, u32[]{:S(2)}) %all-to-all-start.11) | async-done | bytes 393248 | tf_op jit(solution)/shard_map/all_to_all | solution.py:22
  217.0 0.6 copy.43
  (67 shorter events, 4.5 us)
Async XLA Ops:
  7.2 59.5 %copy-start = (bf16[1,256,1024]{2,1,0:T(8,128)(2,1)S(1)}, bf16[1,256,1024]{2,1,0:T(8,128)(2,1)}, u32[]{:S(2)}) copy-start(bf16[1,256,1024]{2,1,0:T(8,128)(2,1)} %param.14) | copy-start | bytes 1572868
  7.2 76.5 %all-gather.3.cloned.1.call-start = ((), (), s32[]{:S(2)}) async-start(), calls=%async_computation.12 | async-start | bytes 4718592 | tf_op jit(solution)/shard_map/all_gather | solution.py:97
  7.2 1.1 copy-start.1
  8.3 9.4 %copy-start.4 = (bf16[1,256,1,256]{3,1,2,0:T(8,128)(2,1)S(1)}, bf16[1,256,1,256]{3,1,2,0:T(8,128)(2,1)}, u32[]{:S(2)}) copy-start(bf16[1,256,1,256]{3,1,2,0:T(8,128)(2,1)} %param.12) | copy-start | bytes 393220
  55.3 11.3 %copy-start.3 = (bf16[32,3,256]{2,0,1:T(8,128)(2,1)S(1)}, bf16[32,3,256]{2,0,1:T(8,128)(2,1)}, u32[]{:S(2)}) copy-start(bf16[32,3,256]{2,0,1:T(8,128)(2,1)} %param.9) | copy-start | bytes 147460
  55.3 17.4 %copy-start.5 = (bf16[1,128]{1,0:T(2,128)(2,1)S(1)}, bf16[1,128]{1,0:T(2,128)(2,1)}, u32[]{:S(2)}) copy-start(bf16[1,128]{1,0:T(2,128)(2,1)} %param.15) | copy-start | bytes 772
  55.3 17.4 %copy-start.6 = (bf16[1,128]{1,0:T(2,128)(2,1)S(1)}, bf16[1,128]{1,0:T(2,128)(2,1)}, u32[]{:S(2)}) copy-start(bf16[1,128]{1,0:T(2,128)(2,1)} %param.13) | copy-start | bytes 772
  67.7 17.4 %all-to-all-start.5 = ((bf16[32,3,1024]{2,1,0:T(4,128)(2,1)}), bf16[32,3,1024]{2,1,0:T(4,128)(2,1)S(1)}, u32[]{:S(2)}, u32[]{:S(2)}) async-start(bf16[32,3,1024]{2,1,0:T(4,128)(2,1)} %reshape.162), calls=%async_computation.5 | async-start | bytes 524288 | tf_op jit(solution)/shard_map/all_to_all | solution.py:22
  71.9 95.2 %all-gather.5.cloned.1.call-start = ((), (), s32[]{:S(2)}) async-start(), calls=%async_computation.13 | async-start | bytes 2162688 | tf_op jit(solution)/shard_map/all_gather | solution.py:123
  89.4 33.2 %copy-start.2 = (bf16[1,1024,256]{2,1,0:T(8,128)(2,1)S(1)}, bf16[1,1024,256]{2,1,0:T(8,128)(2,1)}, u32[]{:S(2)}) copy-start(bf16[1,1024,256]{2,1,0:T(8,128)(2,1)} %param.16) | copy-start | bytes 1572868
  89.4 10.1 %collective-permute-start = (bf16[512,256]{0,1:T(8,128)(2,1)S(1)}, bf16[512,256]{0,1:T(8,128)(2,1)S(1)}, u32[]{:S(2)}, u32[]{:S(2)}) collective-permute-start(bf16[512,256]{0,1:T(8,128)(2,1)S(1)} %get-tuple-element.27), channel_id=1, source_target_pairs={{8,0},{9,1},{10,2},{11,3},{12,4},{13,5},{14,6},{15,7},{24,16},{25,... | collective-permute-start | bytes 786440 | tf_op jit(solution)/shard_map/ppermute | solution.py:106
  101.0 21.5 %all-to-all-start.6 = ((bf16[32,3,1024]{2,1,0:T(4,128)(2,1)}), bf16[32,3,1024]{2,1,0:T(4,128)(2,1)S(1)}, u32[]{:S(2)}, u32[]{:S(2)}) async-start(bf16[32,3,1024]{2,1,0:T(4,128)(2,1)} %broadcast_in_dim.82), calls=%async_computation.6 | async-start | bytes 524288 | tf_op jit(solution)/shard_map/all_to_all | solution.py:22
  171.3 7.1 %collective-permute-start.1 = (bf16[512,256]{0,1:T(8,128)(2,1)S(1)}, bf16[512,256]{0,1:T(8,128)(2,1)S(1)}, u32[]{:S(2)}, u32[]{:S(2)}) collective-permute-start(bf16[512,256]{0,1:T(8,128)(2,1)S(1)} %get-tuple-element.31), channel_id=1, source_target_pairs={{0,8},{1,9},{2,10},{3,11},{4,12},{5,13},{6,14},{7,15},{16,24},{17,... | collective-permute-start | bytes 786440 | tf_op jit(solution)/shard_map/ppermute | solution.py:106
  198.4 18.4 %all-to-all-start.11 = ((bf16[8,96,256]{2,1,0:T(8,128)(2,1)}), bf16[8,96,256]{2,1,0:T(8,128)(2,1)S(1)}, u32[]{:S(2)}, u32[]{:S(2)}) async-start(bf16[8,96,256]{2,1,0:T(8,128)(2,1)} %broadcast_in_dim.86), calls=%async_computation.11 | async-start | bytes 786432 | tf_op jit(solution)/shard_map/all_to_all | solution.py:22
Sparse Core Ops, SparseCore 0:
  17.8 65.8 all-gather.2
  87.4 60.8 all-gather.4

commit v4 on v3

--- a/solution.py
+++ b/solution.py
@@ -30,26 +30,42 @@
     return lax.optimization_barrier((value, *earlier))[0]
 
 
-def halved(rows, run):
+def dealt(rows, weight, section):
     count, width = rows.shape
-
-    def deal(rows_ref, halves_ref):
-        for column in range(0, width, 2 * run):
-            to = pl.ds(column // 2, run)
-            halves_ref[0, :, to] = rows_ref[:, pl.ds(column, run)]
-            halves_ref[1, :, to] = rows_ref[:, pl.ds(column + run, run)]
-
+    run = weight.shape[0] // 2
+    columns = weight.shape[1]
+
+    def deal(section_ref, rows_ref, weight_ref, kept_ref, given_ref, kept_weight_ref, given_weight_ref):
+        def split(first_ref, second_ref, first_weight_ref, second_weight_ref):
+            for column in range(0, width, 2 * run):
+                to = pl.ds(column // 2, run)
+                first_ref[:, to] = rows_ref[:, pl.ds(column, run)]
+                second_ref[:, to] = rows_ref[:, pl.ds(column + run, run)]
+            first_weight_ref[...] = weight_ref[pl.ds(0, run), :]
+            second_weight_ref[...] = weight_ref[pl.ds(run, run), :]
+
+        @pl.when(section_ref[0] == 0)
+        def _():
+            split(kept_ref, given_ref, kept_weight_ref, given_weight_ref)
+
+        @pl.when(section_ref[0] != 0)
+        def _():
+            split(given_ref, kept_ref, given_weight_ref, kept_weight_ref)
+
+    half = jax.ShapeDtypeStruct((count, width // 2), rows.dtype)
+    half_weight = jax.ShapeDtypeStruct((run, columns), weight.dtype)
+    vmem = pl.BlockSpec(memory_space=pltpu.VMEM)
     return pl.pallas_call(
         deal,
-        out_shape=jax.ShapeDtypeStruct((2, count, width // 2), rows.dtype),
-        in_specs=[pl.BlockSpec(memory_space=pltpu.VMEM)],
-        out_specs=pl.BlockSpec(memory_space=pltpu.VMEM),
+        out_shape=(half, half, half_weight, half_weight),
+        in_specs=[pl.BlockSpec(memory_space=pltpu.SMEM), vmem, vmem],
+        out_specs=(vmem, vmem, vmem, vmem),
         compiler_params=pltpu.CompilerParams(vmem_limit_bytes=4 * 1024 * 1024),
         cost_estimate=pl.CostEstimate(
             flops=0, bytes_accessed=4 * count * width, transcendentals=0
         ),
         name="deal_halves",
-    )(rows)
+    )(section.reshape(1), rows, weight)
 
 
 def to_query(state, weight):
@@ -85,28 +101,29 @@
     fars, rows, cores = (lax.axis_size(name) for name in SEQ)
     gate = jnp.tanh(attn_gate[0])
 
-    tokens, width = features.shape[1:]
-    run = width // (fars * rows * cores * 2)
-    pair = exchange(halved(features[0], run), "section").reshape(2 * tokens, -1)
-
-    own_weight = key_value_weight[0, :, 0, :]
-    columns = own_weight.shape[1]
-    parts = exchange(after(own_weight, pair).reshape(2, run, columns), "section")
-    first_part, second_part = parts[0], parts[1]
-
-    gathered_tokens = lax.all_gather(pair, "tp", axis=0, tiled=True)
-    by_core = gathered(gathered(gathered(first_part, "far"), "row"), "core")
+    tokens = features.shape[1]
+    swap = [(0, 1), (1, 0)]
+    kept, given, kept_weight, given_weight = dealt(
+        features[0], key_value_weight[0, :, 0, :], section.astype(jnp.int32)
+    )
+    columns = kept_weight.shape[1]
+    near_tokens = lax.all_gather(kept, "tp", axis=0, tiled=True)
+    got_weight = lax.ppermute(given_weight, "section", swap)
+    got = lax.ppermute(after(given, given_weight), "section", swap)
+    far_tokens = lax.all_gather(got, "tp", axis=0, tiled=True)
+    first_part = jnp.where(section == 0, kept_weight, got_weight)
+    second_part = jnp.where(section == 0, got_weight, kept_weight)
+    by_far = gathered(first_part, "far")
+    by_core = gathered(gathered(after(by_far, got), "row"), "core")
     first_weight = jnp.transpose(by_core, (2, 1, 0, 3, 4)).reshape(-1, columns)
-    first_query = to_query(after(hidden, by_core), q_weight[0])
-
-    def projected(weight):
-        return jnp.dot(gathered_tokens, weight, preferred_element_type=F32)
+
+    def projected(rows, weight):
+        return jnp.dot(rows, weight, preferred_element_type=F32)
 
     def handed(partial_sum, direction):
-        return lax.ppermute(partial_sum.astype(BF16), "section", [direction])
-
-    def cache(partial_sum, other):
-        total = partial_sum + other.astype(F32)
+        return lax.ppermute(partial_sum, "section", [direction]).astype(F32)
+
+    def cache(total):
         keys = norm_per_head(total[:, :head_size], k_gain[0]).astype(BF16)
         return keys, total[:, head_size:].astype(BF16)
 
@@ -114,14 +131,20 @@
         return (state.astype(F32) + total.reshape(state.shape)).astype(BF16)
 
     slots = jnp.arange(2 * tensor_count * tokens, dtype=jnp.int32)
-    place = slots // tokens
-    slots = (place % 2 * tensor_count + place // 2) * tokens + slots % tokens
+    slots = (slots + section * tensor_count * tokens) % slots.shape[0]
     live = slots[None, :] < tiles[0] * TILE_TOK
 
-    first_partial = projected(first_weight)
-    first_keys, first_values = cache(first_partial, handed(first_partial, (1, 0)))
+    first_near = projected(near_tokens, first_weight)
+    given_near, early_hidden = lax.optimization_barrier((first_near.astype(BF16), hidden))
+    for_far = handed(given_near, (1, 0))
+    first_query = to_query(early_hidden, q_weight[0])
+    first_far = projected(after(far_tokens, first_query), first_weight)
+    for_near = handed(first_far.astype(BF16), (1, 0))
+    first_keys, first_values = cache(
+        jnp.concatenate([first_near + for_near, first_far + for_far])
+    )
     second_weight = lax.all_gather(
-        after(second_part, gathered_tokens), SEQ, axis=0, tiled=True
+        after(second_part, far_tokens), SEQ, axis=0, tiled=True
     )
     first_sum = attend(
         first_query, query_gain[0], first_keys, first_values, live, o_weight[0], gate
@@ -129,19 +152,25 @@
     first_sum = first_sum.reshape(tensor_count, -1, first_sum.shape[1])
     summed = jnp.sum(exchange(first_sum, "tp").astype(F32), axis=0).astype(BF16)
     first = added(hidden, gathered(summed, ("section", "tp"))[:tensor_count].astype(F32))
-    second_partial = projected(after(second_weight, first))
-    second_other = handed(second_partial, (0, 1))
-    second_query = to_query(first, q_weight[0])
-    second_keys, second_values = cache(second_partial, second_other)
+    second_weight = after(second_weight, first)
+    second_near = projected(near_tokens, second_weight)
+    second_far = projected(far_tokens, second_weight)
+    given_second = jnp.concatenate([second_far.astype(BF16), second_near.astype(BF16)])
+    given_second, late_first = lax.optimization_barrier((given_second, first))
+    second_other = handed(given_second, (0, 1))
+    second_query = to_query(late_first, q_weight[0])
+    second_keys, second_values = cache(
+        jnp.concatenate([second_near, second_far]) + second_other
+    )
     second_sum = attend(
         second_query, query_gain[0], second_keys, second_values, live, o_weight[0], gate
     )
     second = added(first, jnp.sum(gathered(second_sum, "tp").astype(F32), axis=0))
 
     def placed(ours, theirs):
-        chosen = jnp.where(section == 0, ours, theirs)
-        chosen = chosen.reshape(tensor_count, 2, tokens, head_size)
-        return jnp.transpose(chosen, (1, 0, 2, 3)).reshape(1, 1, -1, 1, head_size)
+        near = theirs.shape[0] // 2
+        turned = jnp.concatenate([theirs[near:], theirs[:near]])
+        return jnp.where(section == 0, ours, turned)[None, None, :, None, :]
 
     keys = placed(first_keys, second_keys)
     values = placed(first_values, second_values)

time: 225 us -> 263 us (1.17)
  waiting for transfers between devices: 50.4 us -> 96 us
  blocking collectives: 119 us -> 78 us
  starting transfers between devices: 19.3 us -> 46.8 us
  other arithmetic: 1.08 us -> 4.46 us
    all_to_all x9 -> x6, blocking collectives: 119 us -> 78 us  [exchange(): return lax.all_to_all(blocks, axis, 0, 0, tiled=True)]
    all_to_all x3 -> x4, waiting for transfers between devices: 26.9 us -> 52 us  [exchange(): return lax.all_to_all(blocks, axis, 0, 0, tiled=True)]
    all_gather x2 -> x3, waiting for transfers between devices: 9.54 us -> 31.7 us  [the longest x1 31.6 us: body(): far_tokens = lax.all_gather(got, 'tp', axis=0, tiled=True)]
    all_to_all x3 -> x4, starting transfers between devices: 16.2 us -> 34.4 us  [exchange(): return lax.all_to_all(blocks, axis, 0, 0, tiled=True)]
    ppermute x2 -> x5, starting transfers between devices: 2.93 us -> 12.3 us  [the longest x3 4.94 us: handed(): return lax.ppermute(partial_sum, 'section', [direction]).astype(F32)]
    ppermute x2 -> x5, waiting for transfers between devices: 14 us -> 12.2 us  [the longest x3 5.81 us: handed(): return lax.ppermute(partial_sum, 'section', [direction]).astype(F32)]
    dot_general x2 -> x4, matrix products: 8.24 us -> 9.1 us  [projected(): return jnp.dot(rows, weight, preferred_element_type=F32)]
  transfers between devices with their start and end apart: 7 -> 12, of which waited for: 6 -> 8; matrix products, arithmetic and copies ran while one was open for 6% -> 5% of each run, Pallas kernels for 0% -> 0%
where the time goes in v4:
time: 263 us; the launch traced here: 262 us
  waiting for transfers between devices  96 us (37%)
  blocking collectives  78 us (30%)
  starting transfers between devices  46.8 us (18%)
  between operations  15.6 us (6%)
  matrix products  11 us (4%)
  local copies, waits for them, and re-layouts  9.32 us (4%)
  other arithmetic  4.46 us (2%)
    all_to_all x6, blocking collectives, exchange(): return lax.all_to_all(blocks, axis, 0, 0, tiled=True)  78 us
    all_to_all x4, waiting for transfers between devices, exchange(): return lax.all_to_all(blocks, axis, 0, 0, tiled=True)  52 us
    all_to_all x4, starting transfers between devices, exchange(): return lax.all_to_all(blocks, axis, 0, 0, tiled=True)  34.4 us
    all_gather x1, waiting for transfers between devices, body(): far_tokens = lax.all_gather(got, 'tp', axis=0, tiled=True)  31.6 us
    dot_general x4, matrix products, projected(): return jnp.dot(rows, weight, preferred_element_type=F32)  9.1 us
    ppermute x3, waiting for transfers between devices, handed(): return lax.ppermute(partial_sum, 'section', [direction]).astype(F32)  5.81 us
  transfers between devices with their start and end apart: 12, of which 8 were waited for; matrix products, arithmetic and copies ran while one was open for 5% of the time, Pallas kernels for 0%

profile of v4, /device:TPU:1, one launch (start us, length us, event | category | flops | bytes accessed | tf_op | source)
XLA Modules:
  0.0 262.0 jit_solution(18193089701230987794)
XLA Ops:
  7.2 1.1 copy-done.1
  8.3 0.9 copy-done.2
  10.1 4.0 %collective-permute-start.1 = (bf16[32,4096]{1,0:T(8,128)(2,1)S(1)}, bf16[32,4096]{1,0:T(8,128)(2,1)S(1)}, u32[]{:S(2)}, u32[]{:S(2)}) collective-permute-start(bf16[32,4096]{1,0:T(8,128)(2,1)S(1)} %get-tuple-element.20), channel_id=1, source_target_pairs={{0,8},{8,0},{1,9},{9,1},{2,10},{10,2},{3,11},{11,3},{4,12},{12,4},... | collective-permute-start | bytes 786440 | tf_op jit(solution)/shard_map/ppermute | solution.py:112
  14.2 3.7 %collective-permute-done.1 = bf16[32,4096]{1,0:T(8,128)(2,1)S(1)} collective-permute-done((bf16[32,4096]{1,0:T(8,128)(2,1)S(1)}, bf16[32,4096]{1,0:T(8,128)(2,1)S(1)}, u32[]{:S(2)}, u32[]{:S(2)}) %collective-permute-start.1) | collective-permute-done | bytes 262176 | tf_op jit(solution)/shard_map/ppermute | solution.py:112
  18.7 3.4 %collective-permute-start = (bf16[128,256]{1,0:T(8,128)(2,1)S(1)}, bf16[128,256]{1,0:T(8,128)(2,1)S(1)}, u32[]{:S(2)}, u32[]{:S(2)}) collective-permute-start(bf16[128,256]{1,0:T(8,128)(2,1)S(1)} %get-tuple-element.18), channel_id=1, source_target_pairs={{0,8},{8,0},{1,9},{9,1},{2,10},{10,2},{3,11},{11,3},{4,12},{12,4},... | collective-permute-start | bytes 196616 | tf_op jit(solution)/shard_map/ppermute | solution.py:111
  22.1 2.7 %collective-permute-done = bf16[128,256]{1,0:T(8,128)(2,1)S(1)} collective-permute-done((bf16[128,256]{1,0:T(8,128)(2,1)S(1)}, bf16[128,256]{1,0:T(8,128)(2,1)S(1)}, u32[]{:S(2)}, u32[]{:S(2)}) %collective-permute-start) | collective-permute-done | bytes 65568 | tf_op jit(solution)/shard_map/ppermute | solution.py:111
  25.4 16.1 %all_to_all.50 = bf16[4,128,256]{2,1,0:T(8,128)(2,1)S(1)} all-to-all(bf16[4,128,256]{2,1,0:T(8,128)(2,1)S(1)} %broadcast_in_dim.40), channel_id=1, replica_groups=mesh['far'=4,'row'=4,'core'=2,'section'=2,'tp'=8] {'far'}, dimensions={0} | all-to-all | bytes 524288 | tf_op jit(solution)/shard_map/all_to_all | solution.py:22
  41.6 14.3 %all_to_all.51 = bf16[4,4,128,256]{3,2,1,0:T(8,128)(2,1)S(1)} all-to-all(bf16[4,4,128,256]{3,2,1,0:T(8,128)(2,1)S(1)} %broadcast_in_dim.41), channel_id=1, replica_groups=mesh['far'=4,'row'=4,'core'=2,'section'=2,'tp'=8] {'row'}, dimensions={0} | all-to-all | bytes 2097152 | tf_op jit(solution)/shard_map/all_to_all | solution.py:22
  56.2 10.6 %all_to_all.52 = bf16[2,4,4,128,256]{4,3,1,2,0:T(8,128)(2,1)S(1)} all-to-all(bf16[2,4,4,128,256]{4,3,1,2,0:T(8,128)(2,1)S(1)} %broadcast_in_dim.42), channel_id=1, replica_groups=mesh['far'=4,'row'=4,'core'=2,'section'=2,'tp'=8] {'core'}, dimensions={0} | all-to-all | bytes 4194304 | tf_op jit(solution)/shard_map/all_to_all | solution.py:22
  67.0 2.3 fusion.29
  69.5 31.6 %all-gather.6.cloned.1.call-done = bf16[256,4096]{1,0:T(8,128)(2,1)} async-done(((bf16[32,4096]{1,0:T(8,128)(2,1)}), bf16[256,4096]{1,0:T(8,128)(2,1)}) %all-gather.6.cloned.1.call-update) | async-done | bytes 2097168 | tf_op jit(solution)/shard_map/all_gather | solution.py:113
  101.4 0.8 reshape.112
  102.2 14.0 %all-to-all-start.3 = ((bf16[32,3,1024]{2,1,0:T(4,128)(2,1)}), bf16[32,3,1024]{2,1,0:T(4,128)(2,1)S(1)}, u32[]{:S(2)}, u32[]{:S(2)}) async-start(bf16[32,3,1024]{2,1,0:T(4,128)(2,1)} %reshape.112), calls=%async_computation.3 | async-start | bytes 524288 | tf_op jit(solution)/shard_map/all_to_all | solution.py:22
  118.0 1.3 collective-permute-start.3
  119.3 10.0 %all-to-all-done.3 = bf16[32,3,1024]{2,1,0:T(4,128)(2,1)S(1)} async-done(((bf16[32,3,1024]{2,1,0:T(4,128)(2,1)}), bf16[32,3,1024]{2,1,0:T(4,128)(2,1)S(1)}, u32[]{:S(2)}, u32[]{:S(2)}) %all-to-all-start.3) | async-done | bytes 196640 | tf_op jit(solution)/shard_map/all_to_all | solution.py:22
  129.4 2.3 fusion.27
  131.7 1.3 collective-permute-start.2
  133.2 5.8 %collective-permute-done.2 = bf16[256,256]{1,0:T(8,128)(2,1)S(1)} collective-permute-done((bf16[256,256]{1,0:T(8,128)(2,1)S(1)}, bf16[256,256]{1,0:T(8,128)(2,1)S(1)}, u32[]{:S(2)}, u32[]{:S(2)}) %collective-permute-start.2) | collective-permute-done | bytes 131104 | tf_op jit(solution)/shard_map/ppermute | solution.py:124
  140.8 7.8 %all-to-all-start.4 = ((bf16[32,3,1024]{2,1,0:T(4,128)(2,1)}), bf16[32,3,1024]{2,1,0:T(4,128)(2,1)S(1)}, u32[]{:S(2)}, u32[]{:S(2)}) async-start(bf16[32,3,1024]{2,1,0:T(4,128)(2,1)} %broadcast_in_dim.46), calls=%async_computation.4 | async-start | bytes 524288 | tf_op jit(solution)/shard_map/all_to_all | solution.py:22
  149.3 15.4 %all-to-all-done.4 = bf16[32,3,1024]{2,1,0:T(4,128)(2,1)S(1)} async-done(((bf16[32,3,1024]{2,1,0:T(4,128)(2,1)}), bf16[32,3,1024]{2,1,0:T(4,128)(2,1)S(1)}, u32[]{:S(2)}, u32[]{:S(2)}) %all-to-all-start.4) | async-done | bytes 196640 | tf_op jit(solution)/shard_map/all_to_all | solution.py:22
  165.1 10.8 %all_to_all.53 = bf16[8,12,256]{2,1,0:T(8,128)(2,1)S(1)} all-to-all(bf16[8,12,256]{2,1,0:T(8,128)(2,1)S(1)} %reshape.115), channel_id=1, replica_groups=mesh['far'=4,'row'=4,'core'=2,'section'=2,'tp'=8] {'tp'}, dimensions={0} | all-to-all | bytes 98304 | tf_op jit(solution)/shard_map/all_to_all | solution.py:22
  175.9 10.0 %all_to_all.54 = bf16[16,12,256]{2,1,0:T(8,128)(2,1)S(1)} all-to-all(bf16[16,12,256]{2,1,0:T(8,128)(2,1)S(1)} %broadcast_in_dim.47), channel_id=1, replica_groups=mesh['far'=4,'row'=4,'core'=2,'section'=2,'tp'=8] {'section','tp'}, dimensions={0} | all-to-all | bytes 196608 | tf_op jit(solution)/shard_map/all_to_all | solution.py:22
  186.7 3.1 %fusion.32 = (bf16[256,256]{1,0:T(8,128)(2,1)S(1)}, f32[256,256]{1,0:T(8,128)S(1)}) fusion(bf16[256,4096]{1,0:T(8,128)(2,1)} %all-gather.6.cloned.1.call-done, bf16[4096,256]{1,0:T(8,128)(2,1)} %all-gather.8.cloned.1.call-done), kind=kOutput, calls=%fused_computation.76 | convolution fusion | flops 536936448 | bytes 4587520 | tf_op jit(solution)/shard_map/dot_general | solution.py:121
  190.2 1.4 fusion.31
  191.6 2.4 collective-permute-start.4
  194.0 0.9 reshape.118
  195.1 0.8 reshape.119
  196.0 9.1 %all-to-all-start.7 = ((bf16[32,3,1024]{2,1,0:T(4,128)(2,1)}), bf16[32,3,1024]{2,1,0:T(4,128)(2,1)S(1)}, u32[]{:S(2)}, u32[]{:S(2)}) async-start(bf16[32,3,1024]{2,1,0:T(4,128)(2,1)} %reshape.119), calls=%async_computation.7 | async-start | bytes 524288 | tf_op jit(solution)/shard_map/all_to_all | solution.py:22
  205.4 12.4 %all-to-all-done.7 = bf16[32,3,1024]{2,1,0:T(4,128)(2,1)S(1)} async-done(((bf16[32,3,1024]{2,1,0:T(4,128)(2,1)}), bf16[32,3,1024]{2,1,0:T(4,128)(2,1)S(1)}, u32[]{:S(2)}, u32[]{:S(2)}) %all-to-all-start.7) | async-done | bytes 196640 | tf_op jit(solution)/shard_map/all_to_all | solution.py:22
  218.7 16.2 %all_to_all.55 = bf16[32,3,1024]{2,1,0:T(4,128)(2,1)S(1)} all-to-all(bf16[32,3,1024]{2,1,0:T(4,128)(2,1)S(1)} %broadcast_in_dim.91), channel_id=1, replica_groups=mesh['far'=4,'row'=4,'core'=2,'section'=2,'tp'=8] {'far','row','core'}, dimensions={0} | all-to-all | bytes 393216 | tf_op jit(solution)/shard_map/all_to_all | solution.py:22
  236.1 3.5 %all-to-all-start.9 = ((bf16[8,96,256]{2,1,0:T(8,128)(2,1)}), bf16[8,96,256]{2,1,0:T(8,128)(2,1)S(1)}, u32[]{:S(2)}, u32[]{:S(2)}) async-start(bf16[8,96,256]{2,1,0:T(8,128)(2,1)} %broadcast_in_dim.92), calls=%async_computation.9 | async-start | bytes 786432 | tf_op jit(solution)/shard_map/all_to_all | solution.py:22
  240.4 14.3 %all-to-all-done.9 = bf16[8,96,256]{2,1,0:T(8,128)(2,1)S(1)} async-done(((bf16[8,96,256]{2,1,0:T(8,128)(2,1)}), bf16[8,96,256]{2,1,0:T(8,128)(2,1)S(1)}, u32[]{:S(2)}, u32[]{:S(2)}) %all-to-all-start.9) | async-done | bytes 393248 | tf_op jit(solution)/shard_map/all_to_all | solution.py:22
  (104 shorter events, 12.1 us)
Async XLA Ops:
  7.2 94.0 %copy-start = (bf16[1,256,1024]{2,1,0:T(8,128)(2,1)S(1)}, bf16[1,256,1024]{2,1,0:T(8,128)(2,1)}, u32[]{:S(2)}) copy-start(bf16[1,256,1024]{2,1,0:T(8,128)(2,1)} %param.14) | copy-start | bytes 1572868
  7.2 59.8 %all-gather.4.cloned.1.call-start = ((), (), s32[]{:S(2)}) async-start(), calls=%async_computation.10 | async-start | bytes 2359296 | tf_op jit(solution)/shard_map/all_gather | solution.py:110
  7.2 1.1 copy-start.1
  8.3 0.9 copy-start.2
  10.1 91.1 %all-gather.6.cloned.1.call-start = ((), (), s32[]{:S(2)}) async-start(), calls=%async_computation.11 | async-start | bytes 2359296 | tf_op jit(solution)/shard_map/all_gather | solution.py:113
  10.1 7.8 %collective-permute-start.1 = (bf16[32,4096]{1,0:T(8,128)(2,1)S(1)}, bf16[32,4096]{1,0:T(8,128)(2,1)S(1)}, u32[]{:S(2)}, u32[]{:S(2)}) collective-permute-start(bf16[32,4096]{1,0:T(8,128)(2,1)S(1)} %get-tuple-element.20), channel_id=1, source_target_pairs={{0,8},{8,0},{1,9},{9,1},{2,10},{10,2},{3,11},{11,3},{4,12},{12,4},... | collective-permute-start | bytes 786440 | tf_op jit(solution)/shard_map/ppermute | solution.py:112
  17.9 0.7 copy-start.10
  18.6 168.1 %all-gather.8.cloned.1.call-start = ((), (), s32[]{:S(2)}) async-start(), calls=%async_computation.12 | async-start | bytes 2162688 | tf_op jit(solution)/shard_map/all_gather | solution.py:146
  18.7 6.0 %collective-permute-start = (bf16[128,256]{1,0:T(8,128)(2,1)S(1)}, bf16[128,256]{1,0:T(8,128)(2,1)S(1)}, u32[]{:S(2)}, u32[]{:S(2)}) collective-permute-start(bf16[128,256]{1,0:T(8,128)(2,1)S(1)} %get-tuple-element.18), channel_id=1, source_target_pairs={{0,8},{8,0},{1,9},{9,1},{2,10},{10,2},{3,11},{11,3},{4,12},{12,4},... | collective-permute-start | bytes 196616 | tf_op jit(solution)/shard_map/ppermute | solution.py:111
  67.0 2.4 copy-start.11
  67.0 49.3 %copy-start.17 = (bf16[1,128]{1,0:T(2,128)(2,1)S(1)}, bf16[1,128]{1,0:T(2,128)(2,1)}, u32[]{:S(2)}) copy-start(bf16[1,128]{1,0:T(2,128)(2,1)} %param.13) | copy-start | bytes 772
  67.0 50.5 %copy-start.18 = (bf16[1,128]{1,0:T(2,128)(2,1)S(1)}, bf16[1,128]{1,0:T(2,128)(2,1)}, u32[]{:S(2)}) copy-start(bf16[1,128]{1,0:T(2,128)(2,1)} %param.15) | copy-start | bytes 772
  102.2 27.0 %all-to-all-start.3 = ((bf16[32,3,1024]{2,1,0:T(4,128)(2,1)}), bf16[32,3,1024]{2,1,0:T(4,128)(2,1)S(1)}, u32[]{:S(2)}, u32[]{:S(2)}) async-start(bf16[32,3,1024]{2,1,0:T(4,128)(2,1)} %reshape.112), calls=%async_computation.3 | async-start | bytes 524288 | tf_op jit(solution)/shard_map/all_to_all | solution.py:22
  118.0 11.4 %collective-permute-start.3 = (bf16[256,256]{1,0:T(8,128)(2,1)S(1)}, bf16[256,256]{1,0:T(8,128)(2,1)S(1)}, u32[]{:S(2)}, u32[]{:S(2)}) collective-permute-start(bf16[256,256]{1,0:T(8,128)(2,1)S(1)} %get-tuple-element.24), channel_id=1, source_target_pairs={{8,0},{9,1},{10,2},{11,3},{12,4},{13,5},{14,6},{15,7},{24,16},{25,... | collective-permute-start | bytes 393224 | tf_op jit(solution)/shard_map/ppermute | solution.py:124
  129.4 9.8 %copy-start.15 = (f32[128]{0:T(128)S(1)}, f32[128]{0:T(128)}, u32[]{:S(2)}) copy-start(f32[128]{0:T(128)} %bitcast_convert_fusion.1) | copy-start | bytes 1540
  131.7 7.6 %copy-start.13 = (f32[128]{0:T(128)S(1)}, f32[128]{0:T(128)}, u32[]{:S(2)}) copy-start(f32[128]{0:T(128)} %bitcast_convert_fusion) | copy-start | bytes 1540
  131.7 7.2 %collective-permute-start.2 = (bf16[256,256]{1,0:T(8,128)(2,1)S(1)}, bf16[256,256]{1,0:T(8,128)(2,1)S(1)}, u32[]{:S(2)}, u32[]{:S(2)}) collective-permute-start(bf16[256,256]{1,0:T(8,128)(2,1)S(1)} %get-tuple-element.42), channel_id=1, source_target_pairs={{8,0},{9,1},{10,2},{11,3},{12,4},{13,5},{14,6},{15,7},{24,16},{25,... | collective-permute-start | bytes 393224 | tf_op jit(solution)/shard_map/ppermute | solution.py:124
  139.0 25.9 %copy-start.5 = (bf16[1,1024,256]{2,1,0:T(8,128)(2,1)S(1)}, bf16[1,1024,256]{2,1,0:T(8,128)(2,1)}, u32[]{:S(2)}) copy-start(bf16[1,1024,256]{2,1,0:T(8,128)(2,1)} %param.16) | copy-start | bytes 1572868
  139.2 0.7 copy-start.8
  139.2 46.8 %copy-start.12 = (bf16[32,3,256]{2,0,1:T(8,128)(2,1)S(1)}, bf16[32,3,256]{2,0,1:T(8,128)(2,1)}, u32[]{:S(2)}) copy-start(bf16[32,3,256]{2,0,1:T(8,128)(2,1)} %param.9) | copy-start | bytes 147460
  140.8 23.9 %all-to-all-start.4 = ((bf16[32,3,1024]{2,1,0:T(4,128)(2,1)}), bf16[32,3,1024]{2,1,0:T(4,128)(2,1)S(1)}, u32[]{:S(2)}, u32[]{:S(2)}) async-start(bf16[32,3,1024]{2,1,0:T(4,128)(2,1)} %broadcast_in_dim.46), calls=%async_computation.4 | async-start | bytes 524288 | tf_op jit(solution)/shard_map/all_to_all | solution.py:22
  186.7 3.1 %copy-start.3 = (bf16[256,4096]{1,0:T(8,128)(2,1)S(1)}, bf16[256,4096]{1,0:T(8,128)(2,1)}, u32[]{:S(2)}) copy-start(bf16[256,4096]{1,0:T(8,128)(2,1)} %all-gather.4.cloned.1.call-done) | copy-start | bytes 6291460
  186.7 3.5 %copy-start.4 = (bf16[4096,256]{1,0:T(8,128)(2,1)S(1)}, bf16[4096,256]{1,0:T(8,128)(2,1)}, u32[]{:S(2)}) copy-start(bf16[4096,256]{1,0:T(8,128)(2,1)} %all-gather.8.cloned.1.call-done) | copy-start | bytes 6291460
  191.6 13.4 %copy-start.6 = (f32[256,256]{1,0:T(8,128)S(1)}, f32[256,256]{1,0:T(8,128)}, u32[]{:S(2)}) copy-start(f32[256,256]{1,0:T(8,128)} %get-tuple-element.53) | copy-start | bytes 786436
  191.6 13.7 %copy-start.16 = (f32[128]{0:T(128)S(1)}, f32[128]{0:T(128)}, u32[]{:S(2)}) copy-start(f32[128]{0:T(128)} %bitcast_convert_fusion.1) | copy-start | bytes 1540
  191.6 13.4 %collective-permute-start.4 = (bf16[512,256]{1,0:T(8,128)(2,1)S(1)}, bf16[512,256]{1,0:T(8,128)(2,1)S(1)}, u32[]{:S(2)}, u32[]{:S(2)}) collective-permute-start(bf16[512,256]{1,0:T(8,128)(2,1)S(1)} %pad_maximum_fusion.1), channel_id=1, source_target_pairs={{0,8},{1,9},{2,10},{3,11},{4,12},{5,13},{6,14},{7,15},{16,24},{17,... | collective-permute-start | bytes 786440 | tf_op jit(solution)/shard_map/ppermute | solution.py:124
  194.9 23.2 %copy-start.14 = (f32[128]{0:T(128)S(1)}, f32[128]{0:T(128)}, u32[]{:S(2)}) copy-start(f32[128]{0:T(128)} %bitcast_convert_fusion) | copy-start | bytes 1540
  196.0 21.8 %all-to-all-start.7 = ((bf16[32,3,1024]{2,1,0:T(4,128)(2,1)}), bf16[32,3,1024]{2,1,0:T(4,128)(2,1)S(1)}, u32[]{:S(2)}, u32[]{:S(2)}) async-start(bf16[32,3,1024]{2,1,0:T(4,128)(2,1)} %reshape.119), calls=%async_computation.7 | async-start | bytes 524288 | tf_op jit(solution)/shard_map/all_to_all | solution.py:22
  218.4 21.2 %copy-start.9 = (bf16[512,128]{1,0:T(8,128)(2,1)S(1)}, bf16[512,128]{1,0:T(8,128)(2,1)}, u32[]{:S(2)}) copy-start(bf16[512,128]{1,0:T(8,128)(2,1)} %copy-done.8) | copy-start | bytes 393220
  235.1 19.7 %copy-start.7 = (bf16[32,3,256]{2,1,0:T(4,128)(2,1)S(1)}, bf16[32,3,256]{2,1,0:T(4,128)(2,1)}, u32[]{:S(2)}) copy-start(bf16[32,3,256]{2,1,0:T(4,128)(2,1)} %add_convert_fusion.1) | copy-start | bytes 147460
  236.1 18.6 %all-to-all-start.9 = ((bf16[8,96,256]{2,1,0:T(8,128)(2,1)}), bf16[8,96,256]{2,1,0:T(8,128)(2,1)S(1)}, u32[]{:S(2)}, u32[]{:S(2)}) async-start(bf16[8,96,256]{2,1,0:T(8,128)(2,1)} %broadcast_in_dim.92), calls=%async_computation.9 | async-start | bytes 786432 | tf_op jit(solution)/shard_map/all_to_all | solution.py:22
Sparse Core Ops, SparseCore 0:
  10.2 46.0 all-gather.3
  58.4 42.7 all-gather.5
  104.8 67.8 all-gather.7

commit v5 on v3

v5 whole, which is shorter than its diff:
```python
import math

import jax
import jax.numpy as jnp
from jax import lax
from jax.experimental import pallas as pl
from jax.experimental.pallas import tpu as pltpu
from jax.sharding import Mesh, PartitionSpec as P

TILE_TOK = 128
SEQ = ("far", "row", "core")
CHIP = ("far", "row")
SWAP = [(0, 1), (1, 0)]
BF16 = jnp.bfloat16
F32 = jnp.float32


def norm_per_head(values, gain):
    factor = lax.rsqrt(jnp.mean(values * values, axis=-1, keepdims=True) + 1e-05)
    return values * factor * gain.astype(F32)


def exchange(blocks, axis):
    return lax.all_to_all(blocks, axis, 0, 0, tiled=True)


def gathered(block, axis):
    return exchange(jnp.broadcast_to(block[None], (lax.axis_size(axis),) + block.shape), axis)


def after(value, *earlier):
    return lax.optimization_barrier((value, *earlier))[0]


def dealt(rows, run, order):
    count, width = rows.shape

    def deal(rows_ref, halves_ref):
        for place, pair in enumerate(order):
            to = pl.ds(place * run, run)
            halves_ref[0, :, to] = rows_ref[:, pl.ds(2 * pair * run, run)]
            halves_ref[1, :, to] = rows_ref[:, pl.ds((2 * pair + 1) * run, run)]

    return pl.pallas_call(
        deal,
        out_shape=jax.ShapeDtypeStruct((2, count, width // 2), rows.dtype),
        in_specs=[pl.BlockSpec(memory_space=pltpu.VMEM)],
        out_specs=pl.BlockSpec(memory_space=pltpu.VMEM),
        compiler_params=pltpu.CompilerParams(vmem_limit_bytes=4 * 1024 * 1024),
        cost_estimate=pl.CostEstimate(
            flops=0, bytes_accessed=4 * count * width, transcendentals=0
        ),
        name="deal_halves",
    )(rows)


def to_query(state, weights):
    partial_query = sum(
        jnp.dot(block, weight, preferred_element_type=F32)
        for block, weight in zip(state, weights, strict=True)
    ).astype(BF16)
    chips = lax.axis_size(CHIP)
    pieces = exchange(partial_query.reshape(chips, -1, partial_query.shape[1]), CHIP)
    return jnp.sum(pieces.astype(F32), axis=0)


def attend(query, query_gain, keys, values, live, weights, gate):
    positions = query.shape[0]
    head_size = keys.shape[1]
    query = norm_per_head(query.reshape(-1, head_size), query_gain).astype(BF16)
    scores = jnp.dot(query, keys.T, preferred_element_type=F32) / math.sqrt(head_size)
    shares = jnp.where(live, jnp.exp(scores), 0.0)
    shares = (shares / jnp.sum(shares, axis=-1, keepdims=True)).astype(BF16)
    attended = jnp.dot(shares, values, preferred_element_type=F32).astype(BF16)
    everyone = gathered(attended.reshape(positions, -1), CHIP).reshape(-1, weights[0].shape[0])
    return [
        (gate * jnp.dot(everyone, weight, preferred_element_type=F32)).astype(BF16)
        for weight in weights
    ]


def body(
    hidden, features, tiles, key_value_weight, k_gain, q_weight, query_gain, o_weight, attn_gate
):
    head_size = k_gain.shape[1]
    section = lax.axis_index("section")
    core = lax.axis_index("core")
    tensor_count = lax.axis_size("tp")
    fars, rows, cores = (lax.axis_size(name) for name in SEQ)
    chips = fars * rows
    gate = jnp.tanh(attn_gate[0])

    def by_index(index, first, second):
        return jnp.where(index == 0, first, second)

    def to_other_core(block):
        return lax.ppermute(block, "core", SWAP)

    tokens, width = features.shape[1:]
    run = width // (chips * cores * 2)
    order = [
        (far * rows + row) * cores + each
        for each in range(cores)
        for row in range(rows)
        for far in range(fars)
    ]
    pair = exchange(dealt(features[0], run, order), "section").reshape(2 * tokens, -1)
    gathered_tokens = lax.all_gather(pair, "tp", axis=0, tiled=True)

    parts = after(key_value_weight, pair)[0, :, 0, :].reshape(2, run, -1)
    columns = parts.shape[2]
    kept_weight = by_index(section, parts[0], parts[1])
    got_weight = lax.ppermute(by_index(section, parts[1], parts[0]), "section", SWAP)
    both_parts = by_index(
        section, jnp.stack([kept_weight, got_weight]), jnp.stack([got_weight, kept_weight])
    )

    positions = hidden.shape[1]
    by_parity = after(hidden, pair).reshape(chips, cores, positions, -1)
    own = by_index(core, by_parity[:, 0], by_parity[:, 1]).reshape(chips * positions, -1)
    others = by_index(core, by_parity[:, 1], by_parity[:, 0]).reshape(chips * positions, -1)
    state = [own, to_other_core(others)]
    query_weights = [q_weight[0], to_other_core(after(q_weight, pair)[0])]
    output_weights = [o_weight[0], to_other_core(after(o_weight, pair)[0])]

    by_far = gathered(both_parts, "far")
    first_weight = gathered(gathered(by_far[:, 0], "row"), "core").reshape(-1, columns)
    first_query = to_query([after(state[0], first_weight), state[1]], query_weights)

    def projected(weight):
        return jnp.dot(gathered_tokens, weight, preferred_element_type=F32)

    def handed(partial_sum, direction):
        return lax.ppermute(partial_sum, "section", [direction]).astype(F32)

    def cache(total):
        keys = norm_per_head(total[:, :head_size], k_gain[0]).astype(BF16)
        return keys, total[:, head_size:].astype(BF16)

    slots = jnp.arange(2 * tensor_count * tokens, dtype=jnp.int32)
    place = slots // tokens
    slots = (place % 2 * tensor_count + place // 2) * tokens + slots % tokens
    live = slots[None, :] < tiles[0] * TILE_TOK

    first_partial = projected(first_weight)
    first_keys, first_values = cache(
        first_partial + handed(first_partial.astype(BF16), (1, 0))
    )
    second_weight = lax.all_gather(
        after(by_far[:, 1], gathered_tokens), ("core", "row"), axis=0, tiled=False
    ).reshape(-1, columns)
    first_sum = attend(
        first_query, query_gain[0], first_keys, first_values, live, output_weights, gate
    )
    first_sum = jnp.concatenate(first_sum).reshape(tensor_count, -1, columns)
    summed = jnp.sum(exchange(first_sum, "tp").astype(F32), axis=0).astype(BF16)
    everywhere = gathered(summed, ("section", "tp"))[:tensor_count]
    everywhere = everywhere.reshape(2, chips * positions, -1).astype(F32)
    first = [
        (block.astype(F32) + total).astype(BF16)
        for block, total in zip(state, everywhere, strict=True)
    ]

    second_partial = projected(after(second_weight, summed))
    given, late = lax.optimization_barrier((second_partial.astype(BF16), first[0]))
    second_other = handed(given, (0, 1))
    second_query = to_query([late, first[1]], query_weights)
    second_keys, second_values = cache(second_partial + second_other)
    second_sum = attend(
        second_query, query_gain[0], second_keys, second_values, live, output_weights, gate
    )
    second_sum = by_index(core, jnp.stack(second_sum), jnp.stack(second_sum[::-1]))
    shape = (cores, tensor_count) + second_sum.shape[1:]
    second_sum = jnp.broadcast_to(second_sum[:, None], shape).reshape((-1,) + shape[2:])
    second_sum = exchange(second_sum, ("core", "tp")).reshape(shape)

    returned = to_other_core(after(first[1], second_query))
    first = by_index(core, jnp.stack([first[0], returned]), jnp.stack([returned, first[0]]))
    second = (first.astype(F32) + jnp.sum(second_sum.astype(F32), axis=1)).astype(BF16)
    section_out = by_index(section, first, second).reshape(cores, chips, positions, -1)
    section_out = jnp.transpose(section_out, (1, 0, 2, 3)).reshape((1,) + hidden.shape)

    def placed(ours, theirs):
        chosen = by_index(section, ours, theirs).reshape(tensor_count, 2, tokens, head_size)
        return jnp.transpose(chosen, (1, 0, 2, 3)).reshape(1, 1, -1, 1, head_size)

    return (
        placed(first_keys, second_keys),
        placed(first_values, second_values),
        section_out,
    )


def solution(mesh):
    devices = mesh.devices
    fine = Mesh(
        devices.reshape(4, 4, 2, devices.shape[1], devices.shape[2]),
        ("far", "row", "core", "section", "tp"),
    )
    return jax.shard_map(
        body,
        mesh=fine,
        in_specs=(
            P(None, None, SEQ),
            P(SEQ, ("section", "tp"), None),
            P(SEQ),
            P("section", SEQ, "tp", None),
            P("section", None),
            P("section", SEQ, "tp"),
            P("section", None),
            P("section", "tp", SEQ),
            P("section"),
        ),
        out_specs=(
            P("section", SEQ, None, "tp", None),
            P("section", SEQ, None, "tp", None),
            P("section", None, None, SEQ),
        ),
        check_vma=False,
    )
```

time: 225 us -> 215 us (0.956)
  blocking collectives: 119 us -> 82.1 us
  starting transfers between devices: 19.3 us -> 47.1 us
  waiting for transfers between devices: 50.4 us -> 44 us
  matrix products: 10.2 us -> 14.4 us
    all_to_all x9 -> x6, blocking collectives: 119 us -> 82.1 us  [exchange(): return lax.all_to_all(blocks, axis, 0, 0, tiled=True)]
    ppermute x2 -> x7, starting transfers between devices: 2.93 us -> 17.5 us  [the longest x4 12 us: to_other_core(): return lax.ppermute(block, 'core', SWAP)]
    all_to_all x3 -> x5, starting transfers between devices: 16.2 us -> 29.5 us  [exchange(): return lax.all_to_all(blocks, axis, 0, 0, tiled=True)]
    all_gather x1, waiting for transfers between devices: 9.53 us -> 0.01 us  [body(): gathered_tokens = lax.all_gather(pair, 'tp', axis=0, tiled=True)]
    all_to_all x3 -> x5, waiting for transfers between devices: 26.9 us -> 32.5 us  [exchange(): return lax.all_to_all(blocks, axis, 0, 0, tiled=True)]
    dot_general x6 -> x10, matrix products: 1.3 us -> 6.19 us  [the longest x4 2.9 us: attend(): jnp.dot(everyone, weight, preferred_element_type=F32)]
    ppermute x2 -> x7, waiting for transfers between devices: 14 us -> 11.4 us  [the longest x2 6.46 us: handed(): return lax.ppermute(partial_sum, 'section', [direction]).astype(F32)]
  transfers between devices with their start and end apart: 7 -> 14, of which waited for: 6 -> 8; matrix products, arithmetic and copies ran while one was open for 6% -> 6% of each run, Pallas kernels for 0% -> 0%
where the time goes in v5:
time: 215 us; the launch traced here: 214 us
  blocking collectives  82.1 us (38%)
  starting transfers between devices  47.1 us (22%)
  waiting for transfers between devices  44 us (20%)
  between operations  15.9 us (7%)
  matrix products  14.4 us (7%)
  local copies, waits for them, and re-layouts  9.01 us (4%)
    all_to_all x6, blocking collectives, exchange(): return lax.all_to_all(blocks, axis, 0, 0, tiled=True)  82.1 us
    all_to_all x5, waiting for transfers between devices, exchange(): return lax.all_to_all(blocks, axis, 0, 0, tiled=True)  32.5 us
    all_to_all x5, starting transfers between devices, exchange(): return lax.all_to_all(blocks, axis, 0, 0, tiled=True)  29.5 us
    ppermute x4, starting transfers between devices, to_other_core(): return lax.ppermute(block, 'core', SWAP)  12 us
    dot_general x2, matrix products, projected(): return jnp.dot(gathered_tokens, weight, preferred_element_type=F32)  7.6 us
    ppermute x2, waiting for transfers between devices, handed(): return lax.ppermute(partial_sum, 'section', [direction]).astype(F32)  6.46 us
  transfers between devices with their start and end apart: 14, of which 8 were waited for; matrix products, arithmetic and copies ran while one was open for 6% of the time, Pallas kernels for 0%

profile of v5, /device:TPU:1, one launch (start us, length us, event | category | flops | bytes accessed | tf_op | source)
XLA Modules:
  0.0 214.0 jit_solution(15031382622273462330)
XLA Ops:
  8.3 9.3 %all_to_all.55 = bf16[2,32,4096]{2,1,0:T(8,128)(2,1)} all-to-all(bf16[2,32,4096]{2,1,0:T(8,128)(2,1)S(1)} %deal_halves.1), channel_id=1, replica_groups=mesh['far'=4,'row'=4,'core'=2,'section'=2,'tp'=8] {'section'}, dimensions={0} | all-to-all | bytes 1048576 | tf_op jit(solution)/shard_map/all_to_all | solution.py:24
  17.7 1.9 collective-permute-start
  19.6 4.1 %collective-permute-done = bf16[128,256]{1,0:T(8,128)(2,1)S(1)} collective-permute-done((bf16[128,256]{1,0:T(8,128)(2,1)S(1)}, bf16[128,256]{1,0:T(8,128)(2,1)S(1)}, u32[]{:S(2)}, u32[]{:S(2)}) %collective-permute-start) | collective-permute-done | bytes 65568 | tf_op jit(solution)/shard_map/ppermute | solution.py:113
  23.8 21.7 %all_to_all.56 = bf16[4,2,128,256]{3,2,1,0:T(8,128)(2,1)S(1)} all-to-all(bf16[4,2,128,256]{3,2,1,0:T(8,128)(2,1)S(1)} %broadcast_in_dim.36), channel_id=1, replica_groups=mesh['far'=4,'row'=4,'core'=2,'section'=2,'tp'=8] {'far'}, dimensions={0} | all-to-all | bytes 1048576 | tf_op jit(solution)/shard_map/all_to_all | solution.py:24
  46.2 1.1 broadcast_in_dim.38
  47.3 4.0 %all-to-all-start.2 = ((bf16[4,4,128,256]{3,2,1,0:T(8,128)(2,1)}), bf16[4,4,128,256]{3,2,1,0:T(8,128)(2,1)S(1)}, u32[]{:S(2)}, u32[]{:S(2)}) async-start(bf16[4,4,128,256]{3,2,1,0:T(8,128)(2,1)} %broadcast_in_dim.38), calls=%async_computation.2 | async-start | bytes 2097152 | tf_op jit(solution)/shard_map/all_to_all | solution.py:24
  52.0 5.4 %collective-permute-start.3 = (bf16[256,1024]{1,0:T(8,128)(2,1)S(1)}, bf16[256,1024]{1,0:T(8,128)(2,1)}, u32[]{:S(2)}, u32[]{:S(2)}) collective-permute-start(bf16[256,1024]{1,0:T(8,128)(2,1)S(1)} %bitcast.81), channel_id=1, source_target_pairs={{0,16},{16,0},{1,17},{17,1},{2,18},{18,2},{3,19},{19,3},{4,20},{20... | collective-permute-start | bytes 1572872 | tf_op jit(solution)/shard_map/ppermute | solution.py:97
  57.9 1.9 collective-permute-start.2
  59.8 2.9 %all-to-all-done.2 = bf16[4,4,128,256]{3,2,1,0:T(8,128)(2,1)S(1)} async-done(((bf16[4,4,128,256]{3,2,1,0:T(8,128)(2,1)}), bf16[4,4,128,256]{3,2,1,0:T(8,128)(2,1)S(1)}, u32[]{:S(2)}, u32[]{:S(2)}) %all-to-all-start.2) | async-done | bytes 1048608 | tf_op jit(solution)/shard_map/all_to_all | solution.py:24
  62.9 9.9 %all_to_all.57 = bf16[2,4,4,128,256]{4,3,2,1,0:T(8,128)(2,1)S(1)} all-to-all(bf16[2,4,4,128,256]{4,3,2,1,0:T(8,128)(2,1)S(1)} %broadcast_in_dim.39), channel_id=1, replica_groups=mesh['far'=4,'row'=4,'core'=2,'section'=2,'tp'=8] {'core'}, dimensions={0} | all-to-all | bytes 4194304 | tf_op jit(solution)/shard_map/all_to_all | solution.py:24
  73.0 1.2 fusion
  75.0 5.9 %all-to-all-start.4 = ((bf16[16,3,1024]{2,1,0:T(4,128)(2,1)}), bf16[16,3,1024]{2,1,0:T(4,128)(2,1)S(1)}, u32[]{:S(2)}, u32[]{:S(2)}) async-start(bf16[16,3,1024]{2,1,0:T(4,128)(2,1)} %reshape.297), calls=%async_computation.4 | async-start | bytes 262144 | tf_op jit(solution)/shard_map/all_to_all | solution.py:24
  81.0 2.6 %collective-permute-start.4 = (bf16[1024,256]{1,0:T(8,128)(2,1)S(1)}, bf16[1024,256]{1,0:T(8,128)(2,1)}, u32[]{:S(2)}, u32[]{:S(2)}) collective-permute-start(bf16[1024,256]{1,0:T(8,128)(2,1)S(1)} %bitcast.82), channel_id=1, source_target_pairs={{0,16},{16,0},{1,17},{17,1},{2,18},{18,2},{3,19},{19,3},{4,20},{20... | collective-permute-start | bytes 1572872 | tf_op jit(solution)/shard_map/ppermute | solution.py:97
  83.6 6.6 %all-to-all-done.4 = bf16[16,3,1024]{2,1,0:T(4,128)(2,1)S(1)} async-done(((bf16[16,3,1024]{2,1,0:T(4,128)(2,1)}), bf16[16,3,1024]{2,1,0:T(4,128)(2,1)S(1)}, u32[]{:S(2)}, u32[]{:S(2)}) %all-to-all-start.4) | async-done | bytes 98336 | tf_op jit(solution)/shard_map/all_to_all | solution.py:24
  90.3 3.5 %fusion.50 = (bf16[512,256]{0,1:T(8,128)(2,1)S(1)}, f32[512,256]{0,1:T(8,128)S(1)}) fusion(bf16[4096,256]{1,0:T(8,128)(2,1)S(1)} %bitcast.80, bf16[512,4096]{1,0:T(8,128)(2,1)} %all-gather.4.cloned.1.call-done), kind=kOutput, calls=%fused_computation.111 | convolution fusion | flops 1073872896 | bytes 7077888 | tf_op jit(solution)/shard_map/dot_general | solution.py:131
  93.8 1.3 collective-permute-start.1
  95.2 6.5 %collective-permute-done.1 = bf16[512,256]{0,1:T(8,128)(2,1)S(1)} collective-permute-done((bf16[512,256]{0,1:T(8,128)(2,1)S(1)}, bf16[512,256]{0,1:T(8,128)(2,1)S(1)}, u32[]{:S(2)}, u32[]{:S(2)}) %collective-permute-start.1) | collective-permute-done | bytes 262176 | tf_op jit(solution)/shard_map/ppermute | solution.py:134
  103.0 3.5 %all-to-all-start.5 = ((bf16[16,3,1024]{2,1,0:T(4,128)(2,1)}), bf16[16,3,1024]{2,1,0:T(4,128)(2,1)S(1)}, u32[]{:S(2)}, u32[]{:S(2)}) async-start(bf16[16,3,1024]{2,1,0:T(4,128)(2,1)} %broadcast_in_dim.43), calls=%async_computation.5 | async-start | bytes 262144 | tf_op jit(solution)/shard_map/all_to_all | solution.py:24
  107.2 8.6 %all-to-all-done.5 = bf16[16,3,1024]{2,1,0:T(4,128)(2,1)S(1)} async-done(((bf16[16,3,1024]{2,1,0:T(4,128)(2,1)}), bf16[16,3,1024]{2,1,0:T(4,128)(2,1)S(1)}, u32[]{:S(2)}, u32[]{:S(2)}) %all-to-all-start.5) | async-done | bytes 98336 | tf_op jit(solution)/shard_map/all_to_all | solution.py:24
  116.1 1.2 fusion.7
  117.4 17.1 %all_to_all.58 = bf16[8,12,256]{2,1,0:T(8,128)(2,1)S(1)} all-to-all(bf16[8,12,256]{2,1,0:T(8,128)(2,1)S(1)} %reshape.300), channel_id=1, replica_groups=mesh['far'=4,'row'=4,'core'=2,'section'=2,'tp'=8] {'tp'}, dimensions={0} | all-to-all | bytes 98304 | tf_op jit(solution)/shard_map/all_to_all | solution.py:24
  134.6 10.0 %all_to_all.59 = bf16[16,12,256]{2,1,0:T(8,128)(2,1)S(1)} all-to-all(bf16[16,12,256]{2,1,0:T(8,128)(2,1)S(1)} %broadcast_in_dim.80), channel_id=1, replica_groups=mesh['far'=4,'row'=4,'core'=2,'section'=2,'tp'=8] {'section','tp'}, dimensions={0} | all-to-all | bytes 196608 | tf_op jit(solution)/shard_map/all_to_all | solution.py:24
  144.7 4.1 %fusion.52 = (bf16[512,256]{0,1:T(8,128)(2,1)S(1)}, f32[512,256]{0,1:T(8,128)S(1)}) fusion(bf16[4096,256]{1,0:T(8,128)(2,1)} %bitcast.90, bf16[512,4096]{1,0:T(8,128)(2,1)} %all-gather.4.cloned.1.call-done), kind=kOutput, calls=%fused_computation.113 | convolution fusion | flops 1073872896 | bytes 7077888 | tf_op jit(solution)/shard_map/dot_general | solution.py:131
  149.0 1.3 fusion.1
  151.0 3.5 %all-to-all-start.8 = ((bf16[16,3,1024]{2,1,0:T(4,128)(2,1)}), bf16[16,3,1024]{2,1,0:T(4,128)(2,1)S(1)}, u32[]{:S(2)}, u32[]{:S(2)}) async-start(bf16[16,3,1024]{2,1,0:T(4,128)(2,1)} %reshape.305), calls=%async_computation.8 | async-start | bytes 262144 | tf_op jit(solution)/shard_map/all_to_all | solution.py:24
  154.5 2.3 %collective-permute-start.5 = (bf16[512,256]{0,1:T(8,128)(2,1)S(1)}, bf16[512,256]{0,1:T(8,128)(2,1)S(1)}, u32[]{:S(2)}, u32[]{:S(2)}) collective-permute-start(bf16[512,256]{0,1:T(8,128)(2,1)S(1)} %get-tuple-element.20), channel_id=1, source_target_pairs={{0,8},{1,9},{2,10},{3,11},{4,12},{5,13},{6,14},{7,15},{16,24},{17,... | collective-permute-start | bytes 786440 | tf_op jit(solution)/shard_map/ppermute | solution.py:134
  156.8 6.9 %all-to-all-done.8 = bf16[16,3,1024]{2,1,0:T(4,128)(2,1)S(1)} async-done(((bf16[16,3,1024]{2,1,0:T(4,128)(2,1)}), bf16[16,3,1024]{2,1,0:T(4,128)(2,1)S(1)}, u32[]{:S(2)}, u32[]{:S(2)}) %all-to-all-start.8) | async-done | bytes 98336 | tf_op jit(solution)/shard_map/all_to_all | solution.py:24
  164.6 14.2 %all_to_all.60 = bf16[16,3,1024]{2,1,0:T(4,128)(2,1)S(1)} all-to-all(bf16[16,3,1024]{2,1,0:T(4,128)(2,1)S(1)} %broadcast_in_dim.82), channel_id=1, replica_groups=mesh['far'=4,'row'=4,'core'=2,'section'=2,'tp'=8] {'far','row'}, dimensions={0} | all-to-all | bytes 196608 | tf_op jit(solution)/shard_map/all_to_all | solution.py:24
  179.1 1.2 fusion.10
  181.2 12.6 %all-to-all-start.10 = ((bf16[16,48,256]{2,1,0:T(8,128)(2,1)}), bf16[16,48,256]{2,1,0:T(8,128)(2,1)S(1)}, u32[]{:S(2)}, u32[]{:S(2)}) async-start(bf16[16,48,256]{2,1,0:T(8,128)(2,1)} %bitcast.28), calls=%async_computation.10 | async-start | bytes 786432 | tf_op jit(solution)/shard_map/all_to_all | solution.py:24
  193.8 2.1 collective-permute-start.6
  198.6 7.6 %all-to-all-done.10 = bf16[16,48,256]{2,1,0:T(8,128)(2,1)S(1)} async-done(((bf16[16,48,256]{2,1,0:T(8,128)(2,1)}), bf16[16,48,256]{2,1,0:T(8,128)(2,1)S(1)}, u32[]{:S(2)}, u32[]{:S(2)}) %all-to-all-start.10) | async-done | bytes 393248 | tf_op jit(solution)/shard_map/all_to_all | solution.py:24
  (94 shorter events, 12.2 us)
Async XLA Ops:
  7.2 83.1 %all-gather.4.cloned.1.call-start = ((), (), s32[]{:S(2)}) async-start(), calls=%async_computation.11 | async-start | bytes 4718592 | tf_op jit(solution)/shard_map/all_gather | solution.py:108
  7.2 1.0 copy-start
  8.3 9.4 %copy-start.3 = (bf16[1,256,1,256]{3,1,2,0:T(8,128)(2,1)S(1)}, bf16[1,256,1,256]{3,1,2,0:T(8,128)(2,1)}, u32[]{:S(2)}) copy-start(bf16[1,256,1,256]{3,1,2,0:T(8,128)(2,1)} %param.12) | copy-start | bytes 393220
  17.7 6.1 %collective-permute-start = (bf16[128,256]{1,0:T(8,128)(2,1)S(1)}, bf16[128,256]{1,0:T(8,128)(2,1)S(1)}, u32[]{:S(2)}, u32[]{:S(2)}) collective-permute-start(bf16[128,256]{1,0:T(8,128)(2,1)S(1)} %get-tuple-element.32), channel_id=1, source_target_pairs={{0,8},{8,0},{1,9},{9,1},{2,10},{10,2},{3,11},{11,3},{4,12},{12,4},... | collective-permute-start | bytes 196616 | tf_op jit(solution)/shard_map/ppermute | solution.py:113
  45.5 6.5 %copy-start.4 = (bf16[32,3,256]{2,0,1:T(8,128)(2,1)S(1)}, bf16[32,3,256]{2,0,1:T(8,128)(2,1)}, u32[]{:S(2)}) copy-start(bf16[32,3,256]{2,0,1:T(8,128)(2,1)} %param.9) | copy-start | bytes 147460
  45.5 6.6 %copy-start.1 = (bf16[1,256,1024]{2,1,0:T(8,128)(2,1)S(1)}, bf16[1,256,1024]{2,1,0:T(8,128)(2,1)}, u32[]{:S(2)}) copy-start(bf16[1,256,1024]{2,1,0:T(8,128)(2,1)} %param.14) | copy-start | bytes 1572868
  47.3 15.4 %all-to-all-start.2 = ((bf16[4,4,128,256]{3,2,1,0:T(8,128)(2,1)}), bf16[4,4,128,256]{3,2,1,0:T(8,128)(2,1)S(1)}, u32[]{:S(2)}, u32[]{:S(2)}) async-start(bf16[4,4,128,256]{3,2,1,0:T(8,128)(2,1)} %broadcast_in_dim.38), calls=%async_computation.2 | async-start | bytes 2097152 | tf_op jit(solution)/shard_map/all_to_all | solution.py:24
  52.0 21.0 %collective-permute-start.3 = (bf16[256,1024]{1,0:T(8,128)(2,1)S(1)}, bf16[256,1024]{1,0:T(8,128)(2,1)}, u32[]{:S(2)}, u32[]{:S(2)}) collective-permute-start(bf16[256,1024]{1,0:T(8,128)(2,1)S(1)} %bitcast.81), channel_id=1, source_target_pairs={{0,16},{16,0},{1,17},{17,1},{2,18},{18,2},{3,19},{19,3},{4,20},{20... | collective-permute-start | bytes 1572872 | tf_op jit(solution)/shard_map/ppermute | solution.py:97
  57.9 15.1 %collective-permute-start.2 = (bf16[48,256]{1,0:T(8,128)(2,1)S(1)}, bf16[48,256]{1,0:T(8,128)(2,1)S(1)}, u32[]{:S(2)}, u32[]{:S(2)}) collective-permute-start(bf16[48,256]{1,0:T(8,128)(2,1)S(1)} %select_n.164), channel_id=1, source_target_pairs={{0,16},{16,0},{1,17},{17,1},{2,18},{18,2},{3,19},{19,3},{4,20},{20... | collective-permute-start | bytes 73736 | tf_op jit(solution)/shard_map/ppermute | solution.py:97
  62.9 18.1 %copy-start.5 = (bf16[1,128]{1,0:T(2,128)(2,1)S(1)}, bf16[1,128]{1,0:T(2,128)(2,1)}, u32[]{:S(2)}) copy-start(bf16[1,128]{1,0:T(2,128)(2,1)} %param.15) | copy-start | bytes 772
  62.9 18.1 %copy-start.6 = (bf16[1,128]{1,0:T(2,128)(2,1)S(1)}, bf16[1,128]{1,0:T(2,128)(2,1)}, u32[]{:S(2)}) copy-start(bf16[1,128]{1,0:T(2,128)(2,1)} %param.13) | copy-start | bytes 772
  62.9 18.1 %copy-start.2 = (bf16[1,1024,256]{2,1,0:T(8,128)(2,1)S(1)}, bf16[1,1024,256]{2,1,0:T(8,128)(2,1)}, u32[]{:S(2)}) copy-start(bf16[1,1024,256]{2,1,0:T(8,128)(2,1)} %param.16) | copy-start | bytes 1572868
  75.0 15.1 %all-to-all-start.4 = ((bf16[16,3,1024]{2,1,0:T(4,128)(2,1)}), bf16[16,3,1024]{2,1,0:T(4,128)(2,1)S(1)}, u32[]{:S(2)}, u32[]{:S(2)}) async-start(bf16[16,3,1024]{2,1,0:T(4,128)(2,1)} %reshape.297), calls=%async_computation.4 | async-start | bytes 262144 | tf_op jit(solution)/shard_map/all_to_all | solution.py:24
  80.9 63.8 %all-gather.6.cloned.1.call-start = ((), (), s32[]{:S(2)}) async-start(), calls=%async_computation.12 | async-start | bytes 2359296 | tf_op jit(solution)/shard_map/all_gather | solution.py:149
  81.0 35.1 %collective-permute-start.4 = (bf16[1024,256]{1,0:T(8,128)(2,1)S(1)}, bf16[1024,256]{1,0:T(8,128)(2,1)}, u32[]{:S(2)}, u32[]{:S(2)}) collective-permute-start(bf16[1024,256]{1,0:T(8,128)(2,1)S(1)} %bitcast.82), channel_id=1, source_target_pairs={{0,16},{16,0},{1,17},{17,1},{2,18},{18,2},{3,19},{19,3},{4,20},{20... | collective-permute-start | bytes 1572872 | tf_op jit(solution)/shard_map/ppermute | solution.py:97
  93.8 7.9 %collective-permute-start.1 = (bf16[512,256]{0,1:T(8,128)(2,1)S(1)}, bf16[512,256]{0,1:T(8,128)(2,1)S(1)}, u32[]{:S(2)}, u32[]{:S(2)}) collective-permute-start(bf16[512,256]{0,1:T(8,128)(2,1)S(1)} %get-tuple-element.36), channel_id=1, source_target_pairs={{8,0},{9,1},{10,2},{11,3},{12,4},{13,5},{14,6},{15,7},{24,16},{25,... | collective-permute-start | bytes 786440 | tf_op jit(solution)/shard_map/ppermute | solution.py:134
  103.0 12.8 %all-to-all-start.5 = ((bf16[16,3,1024]{2,1,0:T(4,128)(2,1)}), bf16[16,3,1024]{2,1,0:T(4,128)(2,1)S(1)}, u32[]{:S(2)}, u32[]{:S(2)}) async-start(bf16[16,3,1024]{2,1,0:T(4,128)(2,1)} %broadcast_in_dim.43), calls=%async_computation.5 | async-start | bytes 262144 | tf_op jit(solution)/shard_map/all_to_all | solution.py:24
  151.0 12.7 %all-to-all-start.8 = ((bf16[16,3,1024]{2,1,0:T(4,128)(2,1)}), bf16[16,3,1024]{2,1,0:T(4,128)(2,1)S(1)}, u32[]{:S(2)}, u32[]{:S(2)}) async-start(bf16[16,3,1024]{2,1,0:T(4,128)(2,1)} %reshape.305), calls=%async_computation.8 | async-start | bytes 262144 | tf_op jit(solution)/shard_map/all_to_all | solution.py:24
  154.5 9.4 %collective-permute-start.5 = (bf16[512,256]{0,1:T(8,128)(2,1)S(1)}, bf16[512,256]{0,1:T(8,128)(2,1)S(1)}, u32[]{:S(2)}, u32[]{:S(2)}) collective-permute-start(bf16[512,256]{0,1:T(8,128)(2,1)S(1)} %get-tuple-element.20), channel_id=1, source_target_pairs={{0,8},{1,9},{2,10},{3,11},{4,12},{5,13},{6,14},{7,15},{16,24},{17,... | collective-permute-start | bytes 786440 | tf_op jit(solution)/shard_map/ppermute | solution.py:134
  181.2 25.0 %all-to-all-start.10 = ((bf16[16,48,256]{2,1,0:T(8,128)(2,1)}), bf16[16,48,256]{2,1,0:T(8,128)(2,1)S(1)}, u32[]{:S(2)}, u32[]{:S(2)}) async-start(bf16[16,48,256]{2,1,0:T(8,128)(2,1)} %bitcast.28), calls=%async_computation.10 | async-start | bytes 786432 | tf_op jit(solution)/shard_map/all_to_all | solution.py:24
  193.8 3.1 %collective-permute-start.6 = (bf16[48,256]{1,0:T(8,128)(2,1)S(1)}, bf16[48,256]{1,0:T(8,128)(2,1)S(1)}, u32[]{:S(2)}, u32[]{:S(2)}) collective-permute-start(bf16[48,256]{1,0:T(8,128)(2,1)S(1)} %add_convert_fusion), channel_id=1, source_target_pairs={{0,16},{16,0},{1,17},{17,1},{2,18},{18,2},{3,19},{19,3},{4,20},{20... | collective-permute-start | bytes 73736 | tf_op jit(solution)/shard_map/ppermute | solution.py:97
Sparse Core Ops, SparseCore 0:
  17.8 65.8 all-gather.3
  90.4 30.9 all-gather.5

commit v6 on v5

--- a/solution.py
+++ b/solution.py
@@ -54,17 +54,60 @@
     )(rows)
 
 
-def to_query(state, weights):
-    partial_query = sum(
-        jnp.dot(block, weight, preferred_element_type=F32)
-        for block, weight in zip(state, weights, strict=True)
-    ).astype(BF16)
+def projected(rows, weight, steps=4):
+    count, depth = rows.shape
+    columns = weight.shape[1]
+    part = depth // steps
+
+    def project(rows_ref, weight_ref, sum_ref, rounded_ref):
+        step = pl.program_id(0)
+        product = jnp.dot(rows_ref[...], weight_ref[...], preferred_element_type=F32)
+
+        @pl.when(step == 0)
+        def _():
+            sum_ref[...] = product
+
+        @pl.when(step > 0)
+        def _():
+            sum_ref[...] += product
+
+        @pl.when(step == steps - 1)
+        def _():
+            rounded_ref[...] = sum_ref[...].astype(rounded_ref.dtype)
+
+    whole = pl.BlockSpec((count, columns), lambda step: (0, 0))
+    return pl.pallas_call(
+        project,
+        grid=(steps,),
+        out_shape=(
+            jax.ShapeDtypeStruct((count, columns), F32),
+            jax.ShapeDtypeStruct((count, columns), BF16),
+        ),
+        in_specs=[
+            pl.BlockSpec((count, part), lambda step: (0, step)),
+            pl.BlockSpec((part, columns), lambda step: (step, 0)),
+        ],
+        out_specs=(whole, whole),
+        compiler_params=pltpu.CompilerParams(
+            dimension_semantics=("arbitrary",), vmem_limit_bytes=59 * 1024 * 1024
+        ),
+        cost_estimate=pl.CostEstimate(
+            flops=2 * count * depth * columns,
+            bytes_accessed=2 * (count + columns) * depth,
+            transcendentals=0,
+        ),
+        name="project",
+    )(rows, weight)
+
+
+def to_query(state, weight):
+    partial_query = jnp.dot(state, weight, preferred_element_type=F32).astype(BF16)
     chips = lax.axis_size(CHIP)
     pieces = exchange(partial_query.reshape(chips, -1, partial_query.shape[1]), CHIP)
     return jnp.sum(pieces.astype(F32), axis=0)
 
 
-def attend(query, query_gain, keys, values, live, weights, gate):
+def attend(query, query_gain, keys, values, live, weight, gate):
     positions = query.shape[0]
     head_size = keys.shape[1]
     query = norm_per_head(query.reshape(-1, head_size), query_gain).astype(BF16)
@@ -72,11 +115,8 @@
     shares = jnp.where(live, jnp.exp(scores), 0.0)
     shares = (shares / jnp.sum(shares, axis=-1, keepdims=True)).astype(BF16)
     attended = jnp.dot(shares, values, preferred_element_type=F32).astype(BF16)
-    everyone = gathered(attended.reshape(positions, -1), CHIP).reshape(-1, weights[0].shape[0])
-    return [
-        (gate * jnp.dot(everyone, weight, preferred_element_type=F32)).astype(BF16)
-        for weight in weights
-    ]
+    everyone = gathered(attended.reshape(positions, -1), CHIP).reshape(-1, weight.shape[0])
+    return (gate * jnp.dot(everyone, weight, preferred_element_type=F32)).astype(BF16)
 
 
 def body(
@@ -105,12 +145,11 @@
         for far in range(fars)
     ]
     pair = exchange(dealt(features[0], run, order), "section").reshape(2 * tokens, -1)
-    gathered_tokens = lax.all_gather(pair, "tp", axis=0, tiled=True)
-
-    parts = after(key_value_weight, pair)[0, :, 0, :].reshape(2, run, -1)
+    parts = key_value_weight[0, :, 0, :].reshape(2, run, -1)
     columns = parts.shape[2]
     kept_weight = by_index(section, parts[0], parts[1])
     got_weight = lax.ppermute(by_index(section, parts[1], parts[0]), "section", SWAP)
+    gathered_tokens = lax.all_gather(after(pair, got_weight), "tp", axis=0, tiled=True)
     both_parts = by_index(
         section, jnp.stack([kept_weight, got_weight]), jnp.stack([got_weight, kept_weight])
     )
@@ -119,16 +158,20 @@
     by_parity = after(hidden, pair).reshape(chips, cores, positions, -1)
     own = by_index(core, by_parity[:, 0], by_parity[:, 1]).reshape(chips * positions, -1)
     others = by_index(core, by_parity[:, 1], by_parity[:, 0]).reshape(chips * positions, -1)
-    state = [own, to_other_core(others)]
-    query_weights = [q_weight[0], to_other_core(after(q_weight, pair)[0])]
-    output_weights = [o_weight[0], to_other_core(after(o_weight, pair)[0])]
+    state = jnp.concatenate([own, to_other_core(others)], axis=1)
+    query_weight = jnp.concatenate([q_weight[0], to_other_core(after(q_weight, pair)[0])])
+    output_weight = jnp.concatenate(
+        [o_weight[0], to_other_core(after(o_weight, pair)[0])], axis=1
+    )
 
     by_far = gathered(both_parts, "far")
     first_weight = gathered(gathered(by_far[:, 0], "row"), "core").reshape(-1, columns)
-    first_query = to_query([after(state[0], first_weight), state[1]], query_weights)
-
-    def projected(weight):
-        return jnp.dot(gathered_tokens, weight, preferred_element_type=F32)
+    state, query_weight, first_weight = lax.optimization_barrier(
+        (state, query_weight, first_weight)
+    )
+    first_query, output_weight = lax.optimization_barrier(
+        (to_query(state, query_weight), output_weight)
+    )
 
     def handed(partial_sum, direction):
         return lax.ppermute(partial_sum, "section", [direction]).astype(F32)
@@ -142,40 +185,48 @@
     slots = (place % 2 * tensor_count + place // 2) * tokens + slots % tokens
     live = slots[None, :] < tiles[0] * TILE_TOK
 
-    first_partial = projected(first_weight)
-    first_keys, first_values = cache(
-        first_partial + handed(first_partial.astype(BF16), (1, 0))
-    )
+    first_partial, given = projected(gathered_tokens, first_weight)
+    first_keys, first_values = cache(first_partial + handed(given, (1, 0)))
     second_weight = lax.all_gather(
         after(by_far[:, 1], gathered_tokens), ("core", "row"), axis=0, tiled=False
     ).reshape(-1, columns)
     first_sum = attend(
-        first_query, query_gain[0], first_keys, first_values, live, output_weights, gate
-    )
-    first_sum = jnp.concatenate(first_sum).reshape(tensor_count, -1, columns)
+        first_query,
+        query_gain[0],
+        first_keys,
+        first_values,
+        live,
+        output_weight,
+        gate,
+    )
+    first_sum = jnp.concatenate([first_sum[:, :columns], first_sum[:, columns:]])
+    first_sum = first_sum.reshape(tensor_count, -1, columns)
     summed = jnp.sum(exchange(first_sum, "tp").astype(F32), axis=0).astype(BF16)
     everywhere = gathered(summed, ("section", "tp"))[:tensor_count]
     everywhere = everywhere.reshape(2, chips * positions, -1).astype(F32)
-    first = [
-        (block.astype(F32) + total).astype(BF16)
-        for block, total in zip(state, everywhere, strict=True)
-    ]
-
-    second_partial = projected(after(second_weight, summed))
-    given, late = lax.optimization_barrier((second_partial.astype(BF16), first[0]))
+    everywhere = jnp.concatenate([everywhere[0], everywhere[1]], axis=1)
+    first = (state.astype(F32) + everywhere).astype(BF16)
+
+    second_partial, given = projected(gathered_tokens, after(second_weight, summed))
+    given, late = lax.optimization_barrier((given, first))
     second_other = handed(given, (0, 1))
-    second_query = to_query([late, first[1]], query_weights)
+    second_query = to_query(late, query_weight)
     second_keys, second_values = cache(second_partial + second_other)
     second_sum = attend(
-        second_query, query_gain[0], second_keys, second_values, live, output_weights, gate
-    )
-    second_sum = by_index(core, jnp.stack(second_sum), jnp.stack(second_sum[::-1]))
+        second_query, query_gain[0], second_keys, second_values, live, output_weight, gate
+    )
+    second_sum = by_index(
+        core,
+        jnp.stack([second_sum[:, :columns], second_sum[:, columns:]]),
+        jnp.stack([second_sum[:, columns:], second_sum[:, :columns]]),
+    )
     shape = (cores, tensor_count) + second_sum.shape[1:]
     second_sum = jnp.broadcast_to(second_sum[:, None], shape).reshape((-1,) + shape[2:])
     second_sum = exchange(second_sum, ("core", "tp")).reshape(shape)
 
-    returned = to_other_core(after(first[1], second_query))
-    first = by_index(core, jnp.stack([first[0], returned]), jnp.stack([returned, first[0]]))
+    ours, others = first[:, :columns], after(first, second_query)[:, columns:]
+    returned = to_other_core(others)
+    first = by_index(core, jnp.stack([ours, returned]), jnp.stack([returned, ours]))
     second = (first.astype(F32) + jnp.sum(second_sum.astype(F32), axis=1)).astype(BF16)
     section_out = by_index(section, first, second).reshape(cores, chips, positions, -1)
     section_out = jnp.transpose(section_out, (1, 0, 2, 3)).reshape((1,) + hidden.shape)

time: 215 us -> 227 us (1.056)
  blocking collectives: 82.1 us -> 43.5 us
  waiting for transfers between devices: 44 us -> 72.6 us
  starting transfers between devices: 47.1 us -> 64 us
  matrix products: 14.4 us -> 2.33 us
  Pallas kernels: 0.09 us -> 11.5 us
  other arithmetic: 1.39 us -> 4.58 us
    all_to_all x6 -> x4, blocking collectives: 82.1 us -> 43.5 us  [exchange(): return lax.all_to_all(blocks, axis, 0, 0, tiled=True)]
    all_to_all x5 -> x7, starting transfers between devices: 29.5 us -> 46.5 us  [exchange(): return lax.all_to_all(blocks, axis, 0, 0, tiled=True)]
    all_to_all x5 -> x7, waiting for transfers between devices: 32.5 us -> 49.3 us  [exchange(): return lax.all_to_all(blocks, axis, 0, 0, tiled=True)]
    all_gather x1, waiting for transfers between devices: 0.01 us -> 13.3 us  [body(): lax.all_gather(after(pair, got_weight), 'tp', axis=0, tiled=True)]
    pallas_call x0 -> x2, Pallas kernels: none -> 10.6 us  [projected(): pl.pallas_call(project, grid=(steps,), out_shape=(jax.ShapeDtypeStruct((c...]
    dot_general x6 -> x2, matrix products: 10.5 us -> 0.59 us  [to_query(): jnp.dot(state, weight, preferred_element_type=F32).astype(BF16)]
    dot_general x4 -> x2, matrix products: 2.9 us -> 0.57 us  [attend(): jnp.dot(everyone, weight, preferred_element_type=F32)]
  transfers between devices with their start and end apart: 14 -> 16, of which waited for: 8 -> 10; matrix products, arithmetic and copies ran while one was open for 6% -> 5% of each run, Pallas kernels for 0% -> 2%
where the time goes in v6:
time: 227 us; the launch traced here: 226 us
  waiting for transfers between devices  72.6 us (32%)
  starting transfers between devices  64 us (28%)
  blocking collectives  43.5 us (19%)
  between operations  15.9 us (7%)
  Pallas kernels  11.5 us (5%)
  local copies, waits for them, and re-layouts  11.1 us (5%)
  other arithmetic  4.58 us (2%)
  matrix products  2.33 us (1%)
    all_to_all x7, waiting for transfers between devices, exchange(): return lax.all_to_all(blocks, axis, 0, 0, tiled=True)  49.3 us
    all_to_all x7, starting transfers between devices, exchange(): return lax.all_to_all(blocks, axis, 0, 0, tiled=True)  46.5 us
    all_to_all x4, blocking collectives, exchange(): return lax.all_to_all(blocks, axis, 0, 0, tiled=True)  43.5 us
    all_gather x1, waiting for transfers between devices, body(): lax.all_gather(after(pair, got_weight), 'tp', axis=0, tiled=True)  13.3 us
    pallas_call x2, Pallas kernels, projected(): pl.pallas_call(project, grid=(steps,), out_shape=(jax.ShapeDtypeStruct((c...  10.6 us
    ppermute x4, starting transfers between devices, to_other_core(): return lax.ppermute(block, 'core', SWAP)  9.87 us
    ppermute x2, waiting for transfers between devices, handed(): return lax.ppermute(partial_sum, 'section', [direction]).astype(F32)  6.41 us
  transfers between devices with their start and end apart: 16, of which 10 were waited for; matrix products, arithmetic and copies ran while one was open for 5% of the time, Pallas kernels for 2%

profile of v6, /device:TPU:1, one launch (start us, length us, event | category | flops | bytes accessed | tf_op | source)
XLA Modules:
  0.0 225.5 jit_solution(15311247599897083200)
XLA Ops:
  9.1 3.6 %all-to-all-start = ((bf16[2,32,4096]{2,1,0:T(8,128)(2,1)}), bf16[2,32,4096]{2,1,0:T(8,128)(2,1)S(1)}, u32[]{:S(2)}, u32[]{:S(2)}) async-start(bf16[2,32,4096]{2,1,0:T(8,128)(2,1)} %deal_halves.1), calls=%async_computation | async-start | bytes 1048576 | tf_op jit(solution)/shard_map/all_to_all | solution.py:24
  12.8 4.0 %collective-permute-start = (bf16[128,256]{1,0:T(8,128)(2,1)S(1)}, bf16[128,256]{1,0:T(8,128)(2,1)S(1)}, u32[]{:S(2)}, u32[]{:S(2)}) collective-permute-start(bf16[128,256]{1,0:T(8,128)(2,1)S(1)} %get-tuple-element.46), channel_id=1, source_target_pairs={{0,8},{8,0},{1,9},{9,1},{2,10},{10,2},{3,11},{11,3},{4,12},{12,4},... | collective-permute-start | bytes 196616 | tf_op jit(solution)/shard_map/ppermute | solution.py:151
  16.8 2.7 %collective-permute-done = bf16[128,256]{1,0:T(8,128)(2,1)S(1)} collective-permute-done((bf16[128,256]{1,0:T(8,128)(2,1)S(1)}, bf16[128,256]{1,0:T(8,128)(2,1)S(1)}, u32[]{:S(2)}, u32[]{:S(2)}) %collective-permute-start) | collective-permute-done | bytes 65568 | tf_op jit(solution)/shard_map/ppermute | solution.py:151
  21.2 9.6 %all-to-all-start.1 = ((bf16[4,2,128,256]{3,2,1,0:T(8,128)(2,1)}), bf16[4,2,128,256]{3,2,1,0:T(8,128)(2,1)S(1)}, u32[]{:S(2)}, u32[]{:S(2)}) async-start(bf16[4,2,128,256]{3,2,1,0:T(8,128)(2,1)} %broadcast_in_dim.36), calls=%async_computation.1 | async-start | bytes 1048576 | tf_op jit(solution)/shard_map/all_to_all | solution.py:24
  30.9 14.9 %all-to-all-done.1 = bf16[4,2,128,256]{3,2,1,0:T(8,128)(2,1)S(1)} async-done(((bf16[4,2,128,256]{3,2,1,0:T(8,128)(2,1)}), bf16[4,2,128,256]{3,2,1,0:T(8,128)(2,1)S(1)}, u32[]{:S(2)}, u32[]{:S(2)}) %all-to-all-start.1) | async-done | bytes 524320 | tf_op jit(solution)/shard_map/all_to_all | solution.py:24
  47.6 4.0 %all-to-all-start.2 = ((bf16[4,4,128,256]{3,2,1,0:T(8,128)(2,1)}), bf16[4,4,128,256]{3,2,1,0:T(8,128)(2,1)S(1)}, u32[]{:S(2)}, u32[]{:S(2)}) async-start(bf16[4,4,128,256]{3,2,1,0:T(8,128)(2,1)} %broadcast_in_dim.38), calls=%async_computation.2 | async-start | bytes 2097152 | tf_op jit(solution)/shard_map/all_to_all | solution.py:24
  51.7 3.5 %collective-permute-start.2 = (bf16[256,1024]{1,0:T(8,128)(2,1)S(1)}, bf16[256,1024]{1,0:T(8,128)(2,1)S(1)}, u32[]{:S(2)}, u32[]{:S(2)}) collective-permute-start(bf16[256,1024]{1,0:T(8,128)(2,1)S(1)} %bitcast.66), channel_id=1, source_target_pairs={{0,16},{16,0},{1,17},{17,1},{2,18},{18,2},{3,19},{19,3},{4,20},{20... | collective-permute-start | bytes 1572872 | tf_op jit(solution)/shard_map/ppermute | solution.py:137
  55.3 1.9 collective-permute-start.1
  57.9 2.4 %collective-permute-start.4 = (bf16[1024,256]{1,0:T(8,128)(2,1)S(1)}, bf16[1024,256]{1,0:T(8,128)(2,1)}, u32[]{:S(2)}, u32[]{:S(2)}) collective-permute-start(bf16[1024,256]{1,0:T(8,128)(2,1)S(1)} %bitcast.68), channel_id=1, source_target_pairs={{0,16},{16,0},{1,17},{17,1},{2,18},{18,2},{3,19},{19,3},{4,20},{20... | collective-permute-start | bytes 1572872 | tf_op jit(solution)/shard_map/ppermute | solution.py:137
  61.2 1.1 pad_maximum_fusion
  62.3 2.9 %all-to-all-done.2 = bf16[4,4,128,256]{3,2,1,0:T(8,128)(2,1)S(1)} async-done(((bf16[4,4,128,256]{3,2,1,0:T(8,128)(2,1)}), bf16[4,4,128,256]{3,2,1,0:T(8,128)(2,1)S(1)}, u32[]{:S(2)}, u32[]{:S(2)}) %all-to-all-start.2) | async-done | bytes 1048608 | tf_op jit(solution)/shard_map/all_to_all | solution.py:24
  65.4 8.4 %all_to_all.55 = bf16[2,4,4,128,256]{4,3,2,1,0:T(8,128)(2,1)} all-to-all(bf16[2,4,4,128,256]{4,3,2,1,0:T(8,128)(2,1)S(1)} %broadcast_in_dim.39), channel_id=1, replica_groups=mesh['far'=4,'row'=4,'core'=2,'section'=2,'tp'=8] {'core'}, dimensions={0} | all-to-all | bytes 4194304 | tf_op jit(solution)/shard_map/all_to_all | solution.py:24
  73.8 13.3 %all-gather.4.cloned.1.call-done.rows_ref = bf16[512,4096]{1,0:T(8,128)(2,1)} async-done(((bf16[64,4096]{1,0:T(8,128)(2,1)}), bf16[512,4096]{1,0:T(8,128)(2,1)}) %all-gather.4.cloned.1.call-update) | async-done | bytes 4194320 | tf_op jit(solution)/shard_map/all_gather | solution.py:152
  88.2 9.0 %all-to-all-start.4 = ((bf16[16,3,1024]{2,1,0:T(4,128)(2,1)}), bf16[16,3,1024]{2,1,0:T(4,128)(2,1)S(1)}, u32[]{:S(2)}, u32[]{:S(2)}) async-start(bf16[16,3,1024]{2,1,0:T(4,128)(2,1)} %reshape.275), calls=%async_computation.4 | async-start | bytes 262144 | tf_op jit(solution)/shard_map/all_to_all | solution.py:24
  97.2 1.1 pad_maximum_fusion.1
  98.3 8.1 %all-to-all-done.4 = bf16[16,3,1024]{2,1,0:T(4,128)(2,1)S(1)} async-done(((bf16[16,3,1024]{2,1,0:T(4,128)(2,1)}), bf16[16,3,1024]{2,1,0:T(4,128)(2,1)S(1)}, u32[]{:S(2)}, u32[]{:S(2)}) %all-to-all-start.4) | async-done | bytes 98336 | tf_op jit(solution)/shard_map/all_to_all | solution.py:24
  106.5 5.3 %project.2 = (f32[512,256]{1,0:T(8,128)}, bf16[512,256]{1,0:T(8,128)(2,1)}) custom-call(bf16[512,4096]{1,0:T(8,128)(2,1)} %all-gather.4.cloned.1.call-done.rows_ref, bf16[4096,256]{1,0:T(8,128)(2,1)} %bitcast.61), custom_call_target="tpu_custom_call" | custom-call | flops 1073741824 | bytes 6291456 | tf_op jit(solution)/shard_map/project/pallas_call | solution.py:79
  111.8 1.3 collective-permute-start.3
  113.3 6.4 %collective-permute-done.3 = bf16[512,256]{1,0:T(8,128)(2,1)S(1)} collective-permute-done((bf16[512,256]{1,0:T(8,128)(2,1)}, bf16[512,256]{1,0:T(8,128)(2,1)S(1)}, u32[]{:S(2)}, u32[]{:S(2)}) %collective-permute-start.3) | collective-permute-done | bytes 262176 | tf_op jit(solution)/shard_map/ppermute | solution.py:177
  119.7 1.1 convert_add_fusion.1
  122.2 4.3 %all-to-all-start.5 = ((bf16[16,3,1024]{2,1,0:T(4,128)(2,1)}), bf16[16,3,1024]{2,1,0:T(4,128)(2,1)S(1)}, u32[]{:S(2)}, u32[]{:S(2)}) async-start(bf16[16,3,1024]{2,1,0:T(4,128)(2,1)} %broadcast_in_dim.43), calls=%async_computation.5 | async-start | bytes 262144 | tf_op jit(solution)/shard_map/all_to_all | solution.py:24
  127.2 8.6 %all-to-all-done.5 = bf16[16,3,1024]{2,1,0:T(4,128)(2,1)S(1)} async-done(((bf16[16,3,1024]{2,1,0:T(4,128)(2,1)}), bf16[16,3,1024]{2,1,0:T(4,128)(2,1)S(1)}, u32[]{:S(2)}, u32[]{:S(2)}) %all-to-all-start.5) | async-done | bytes 98336 | tf_op jit(solution)/shard_map/all_to_all | solution.py:24
  136.2 10.7 %all_to_all.56 = bf16[8,12,256]{2,1,0:T(8,128)(2,1)S(1)} all-to-all(bf16[8,12,256]{2,1,0:T(8,128)(2,1)S(1)} %reshape.278), channel_id=1, replica_groups=mesh['far'=4,'row'=4,'core'=2,'section'=2,'tp'=8] {'tp'}, dimensions={0} | all-to-all | bytes 98304 | tf_op jit(solution)/shard_map/all_to_all | solution.py:24
  147.0 10.0 %all_to_all.57 = bf16[16,12,256]{2,1,0:T(8,128)(2,1)S(1)} all-to-all(bf16[16,12,256]{2,1,0:T(8,128)(2,1)S(1)} %broadcast_in_dim.80), channel_id=1, replica_groups=mesh['far'=4,'row'=4,'core'=2,'section'=2,'tp'=8] {'section','tp'}, dimensions={0} | all-to-all | bytes 196608 | tf_op jit(solution)/shard_map/all_to_all | solution.py:24
  157.1 5.3 %project.3 = (f32[512,256]{1,0:T(8,128)}, bf16[512,256]{1,0:T(8,128)(2,1)}) custom-call(bf16[512,4096]{1,0:T(8,128)(2,1)} %all-gather.4.cloned.1.call-done.rows_ref, bf16[4096,256]{1,0:T(8,128)(2,1)} %bitcast.62), custom_call_target="tpu_custom_call" | custom-call | flops 1073741824 | bytes 6291456 | tf_op jit(solution)/shard_map/project/pallas_call | solution.py:79
  163.4 3.5 %all-to-all-start.8 = ((bf16[16,3,1024]{2,1,0:T(4,128)(2,1)}), bf16[16,3,1024]{2,1,0:T(4,128)(2,1)S(1)}, u32[]{:S(2)}, u32[]{:S(2)}) async-start(bf16[16,3,1024]{2,1,0:T(4,128)(2,1)} %reshape.283), calls=%async_computation.8 | async-start | bytes 262144 | tf_op jit(solution)/shard_map/all_to_all | solution.py:24
  166.9 2.3 collective-permute-start.5
  169.2 7.0 %all-to-all-done.8 = bf16[16,3,1024]{2,1,0:T(4,128)(2,1)S(1)} async-done(((bf16[16,3,1024]{2,1,0:T(4,128)(2,1)}), bf16[16,3,1024]{2,1,0:T(4,128)(2,1)S(1)}, u32[]{:S(2)}, u32[]{:S(2)}) %all-to-all-start.8) | async-done | bytes 98336 | tf_op jit(solution)/shard_map/all_to_all | solution.py:24
  177.3 14.4 %all_to_all.58 = bf16[16,3,1024]{2,1,0:T(4,128)(2,1)S(1)} all-to-all(bf16[16,3,1024]{2,1,0:T(4,128)(2,1)S(1)} %broadcast_in_dim.82), channel_id=1, replica_groups=mesh['far'=4,'row'=4,'core'=2,'section'=2,'tp'=8] {'far','row'}, dimensions={0} | all-to-all | bytes 196608 | tf_op jit(solution)/shard_map/all_to_all | solution.py:24
  192.9 12.4 %all-to-all-start.10 = ((bf16[16,48,256]{2,1,0:T(8,128)(2,1)}), bf16[16,48,256]{2,1,0:T(8,128)(2,1)S(1)}, u32[]{:S(2)}, u32[]{:S(2)}) async-start(bf16[16,48,256]{2,1,0:T(8,128)(2,1)} %bitcast.25), calls=%async_computation.10 | async-start | bytes 786432 | tf_op jit(solution)/shard_map/all_to_all | solution.py:24
  205.3 2.1 collective-permute-start.6
  209.9 7.8 %all-to-all-done.10 = bf16[16,48,256]{2,1,0:T(8,128)(2,1)S(1)} async-done(((bf16[16,48,256]{2,1,0:T(8,128)(2,1)}), bf16[16,48,256]{2,1,0:T(8,128)(2,1)S(1)}, u32[]{:S(2)}, u32[]{:S(2)}) %all-to-all-start.10) | async-done | bytes 393248 | tf_op jit(solution)/shard_map/all_to_all | solution.py:24
  (100 shorter events, 16.7 us)
Async XLA Ops:
  7.2 1.0 copy-start
  8.2 4.6 %copy-start.6 = (bf16[1,256,1,256]{3,1,2,0:T(8,128)(2,1)S(1)}, bf16[1,256,1,256]{3,1,2,0:T(8,128)(2,1)}, u32[]{:S(2)}) copy-start(bf16[1,256,1,256]{3,1,2,0:T(8,128)(2,1)} %param.12) | copy-start | bytes 393220
  9.1 21.7 %copy-start.7 = (bf16[32,3,256]{2,0,1:T(8,128)(2,1)S(1)}, bf16[32,3,256]{2,0,1:T(8,128)(2,1)}, u32[]{:S(2)}) copy-start(bf16[32,3,256]{2,0,1:T(8,128)(2,1)} %param.9) | copy-start | bytes 147460
  9.1 10.4 %all-to-all-start = ((bf16[2,32,4096]{2,1,0:T(8,128)(2,1)}), bf16[2,32,4096]{2,1,0:T(8,128)(2,1)S(1)}, u32[]{:S(2)}, u32[]{:S(2)}) async-start(bf16[2,32,4096]{2,1,0:T(8,128)(2,1)} %deal_halves.1), calls=%async_computation | async-start | bytes 1048576 | tf_op jit(solution)/shard_map/all_to_all | solution.py:24
  12.7 74.4 %all-gather.4.cloned.1.call-start = ((), (), s32[]{:S(2)}) async-start(), calls=%async_computation.11 | async-start | bytes 4718592 | tf_op jit(solution)/shard_map/all_gather | solution.py:152
  12.8 6.7 %collective-permute-start = (bf16[128,256]{1,0:T(8,128)(2,1)S(1)}, bf16[128,256]{1,0:T(8,128)(2,1)S(1)}, u32[]{:S(2)}, u32[]{:S(2)}) collective-permute-start(bf16[128,256]{1,0:T(8,128)(2,1)S(1)} %get-tuple-element.46), channel_id=1, source_target_pairs={{0,8},{8,0},{1,9},{9,1},{2,10},{10,2},{3,11},{11,3},{4,12},{12,4},... | collective-permute-start | bytes 196616 | tf_op jit(solution)/shard_map/ppermute | solution.py:151
  19.5 0.8 copy-start.1
  21.2 24.5 %all-to-all-start.1 = ((bf16[4,2,128,256]{3,2,1,0:T(8,128)(2,1)}), bf16[4,2,128,256]{3,2,1,0:T(8,128)(2,1)S(1)}, u32[]{:S(2)}, u32[]{:S(2)}) async-start(bf16[4,2,128,256]{3,2,1,0:T(8,128)(2,1)} %broadcast_in_dim.36), calls=%async_computation.1 | async-start | bytes 1048576 | tf_op jit(solution)/shard_map/all_to_all | solution.py:24
  30.9 20.8 %copy-start.3 = (bf16[1,256,1024]{2,1,0:T(8,128)(2,1)S(1)}, bf16[1,256,1024]{2,1,0:T(8,128)(2,1)}, u32[]{:S(2)}) copy-start(bf16[1,256,1024]{2,1,0:T(8,128)(2,1)} %param.14) | copy-start | bytes 1572868
  46.5 10.7 %copy-start.8 = (bf16[1,128]{1,0:T(2,128)(2,1)S(1)}, bf16[1,128]{1,0:T(2,128)(2,1)}, u32[]{:S(2)}) copy-start(bf16[1,128]{1,0:T(2,128)(2,1)} %param.15) | copy-start | bytes 772
  46.5 10.7 %copy-start.9 = (bf16[1,128]{1,0:T(2,128)(2,1)S(1)}, bf16[1,128]{1,0:T(2,128)(2,1)}, u32[]{:S(2)}) copy-start(bf16[1,128]{1,0:T(2,128)(2,1)} %param.13) | copy-start | bytes 772
  46.5 11.4 %copy-start.4 = (bf16[1,1024,256]{2,1,0:T(8,128)(2,1)S(1)}, bf16[1,1024,256]{2,1,0:T(8,128)(2,1)}, u32[]{:S(2)}) copy-start(bf16[1,1024,256]{2,1,0:T(8,128)(2,1)} %param.16) | copy-start | bytes 1572868
  47.6 17.6 %all-to-all-start.2 = ((bf16[4,4,128,256]{3,2,1,0:T(8,128)(2,1)}), bf16[4,4,128,256]{3,2,1,0:T(8,128)(2,1)S(1)}, u32[]{:S(2)}, u32[]{:S(2)}) async-start(bf16[4,4,128,256]{3,2,1,0:T(8,128)(2,1)} %broadcast_in_dim.38), calls=%async_computation.2 | async-start | bytes 2097152 | tf_op jit(solution)/shard_map/all_to_all | solution.py:24
  51.6 105.5 %all-gather.6.cloned.1.call-start = ((), (), s32[]{:S(2)}) async-start(), calls=%async_computation.12 | async-start | bytes 2359296 | tf_op jit(solution)/shard_map/all_gather | solution.py:190
  51.7 8.7 %collective-permute-start.2 = (bf16[256,1024]{1,0:T(8,128)(2,1)S(1)}, bf16[256,1024]{1,0:T(8,128)(2,1)S(1)}, u32[]{:S(2)}, u32[]{:S(2)}) collective-permute-start(bf16[256,1024]{1,0:T(8,128)(2,1)S(1)} %bitcast.66), channel_id=1, source_target_pairs={{0,16},{16,0},{1,17},{17,1},{2,18},{18,2},{3,19},{19,3},{4,20},{20... | collective-permute-start | bytes 1572872 | tf_op jit(solution)/shard_map/ppermute | solution.py:137
  55.3 5.1 %collective-permute-start.1 = (bf16[48,256]{1,0:T(8,128)(2,1)S(1)}, bf16[48,256]{1,0:T(8,128)(2,1)S(1)}, u32[]{:S(2)}, u32[]{:S(2)}) collective-permute-start(bf16[48,256]{1,0:T(8,128)(2,1)S(1)} %select_n.148), channel_id=1, source_target_pairs={{0,16},{16,0},{1,17},{17,1},{2,18},{18,2},{3,19},{19,3},{4,20},{20... | collective-permute-start | bytes 73736 | tf_op jit(solution)/shard_map/ppermute | solution.py:137
  57.9 39.3 %collective-permute-start.4 = (bf16[1024,256]{1,0:T(8,128)(2,1)S(1)}, bf16[1024,256]{1,0:T(8,128)(2,1)}, u32[]{:S(2)}, u32[]{:S(2)}) collective-permute-start(bf16[1024,256]{1,0:T(8,128)(2,1)S(1)} %bitcast.68), channel_id=1, source_target_pairs={{0,16},{16,0},{1,17},{17,1},{2,18},{18,2},{3,19},{19,3},{4,20},{20... | collective-permute-start | bytes 1572872 | tf_op jit(solution)/shard_map/ppermute | solution.py:137
  60.4 0.8 copy-start.5
  88.2 18.3 %all-to-all-start.4 = ((bf16[16,3,1024]{2,1,0:T(4,128)(2,1)}), bf16[16,3,1024]{2,1,0:T(4,128)(2,1)S(1)}, u32[]{:S(2)}, u32[]{:S(2)}) async-start(bf16[16,3,1024]{2,1,0:T(4,128)(2,1)} %reshape.275), calls=%async_computation.4 | async-start | bytes 262144 | tf_op jit(solution)/shard_map/all_to_all | solution.py:24
  111.8 7.8 %collective-permute-start.3 = (bf16[512,256]{1,0:T(8,128)(2,1)}, bf16[512,256]{1,0:T(8,128)(2,1)S(1)}, u32[]{:S(2)}, u32[]{:S(2)}) collective-permute-start(bf16[512,256]{1,0:T(8,128)(2,1)} %get-tuple-element.26), channel_id=1, source_target_pairs={{8,0},{9,1},{10,2},{11,3},{12,4},{13,5},{14,6},{15,7},{24,16},{25,... | collective-permute-start | bytes 786440 | tf_op jit(solution)/shard_map/ppermute | solution.py:177
  122.2 13.6 %all-to-all-start.5 = ((bf16[16,3,1024]{2,1,0:T(4,128)(2,1)}), bf16[16,3,1024]{2,1,0:T(4,128)(2,1)S(1)}, u32[]{:S(2)}, u32[]{:S(2)}) async-start(bf16[16,3,1024]{2,1,0:T(4,128)(2,1)} %broadcast_in_dim.43), calls=%async_computation.5 | async-start | bytes 262144 | tf_op jit(solution)/shard_map/all_to_all | solution.py:24
  162.4 14.1 %copy-start.2 = (f32[512,256]{1,0:T(8,128)S(1)}, f32[512,256]{1,0:T(8,128)}, u32[]{:S(2)}) copy-start(f32[512,256]{1,0:T(8,128)} %get-tuple-element.34) | copy-start | bytes 1572868
  163.4 12.8 %all-to-all-start.8 = ((bf16[16,3,1024]{2,1,0:T(4,128)(2,1)}), bf16[16,3,1024]{2,1,0:T(4,128)(2,1)S(1)}, u32[]{:S(2)}, u32[]{:S(2)}) async-start(bf16[16,3,1024]{2,1,0:T(4,128)(2,1)} %reshape.283), calls=%async_computation.8 | async-start | bytes 262144 | tf_op jit(solution)/shard_map/all_to_all | solution.py:24
  166.9 9.5 %collective-permute-start.5 = (bf16[512,256]{1,0:T(8,128)(2,1)}, bf16[512,256]{1,0:T(8,128)(2,1)S(1)}, u32[]{:S(2)}, u32[]{:S(2)}) collective-permute-start(bf16[512,256]{1,0:T(8,128)(2,1)} %get-tuple-element.36), channel_id=1, source_target_pairs={{0,8},{1,9},{2,10},{3,11},{4,12},{5,13},{6,14},{7,15},{16,24},{17,... | collective-permute-start | bytes 786440 | tf_op jit(solution)/shard_map/ppermute | solution.py:177
  192.9 24.9 %all-to-all-start.10 = ((bf16[16,48,256]{2,1,0:T(8,128)(2,1)}), bf16[16,48,256]{2,1,0:T(8,128)(2,1)S(1)}, u32[]{:S(2)}, u32[]{:S(2)}) async-start(bf16[16,48,256]{2,1,0:T(8,128)(2,1)} %bitcast.25), calls=%async_computation.10 | async-start | bytes 786432 | tf_op jit(solution)/shard_map/all_to_all | solution.py:24
  205.3 3.1 %collective-permute-start.6 = (bf16[48,256]{1,0:T(8,128)(2,1)S(1)}, bf16[48,256]{1,0:T(8,128)(2,1)S(1)}, u32[]{:S(2)}, u32[]{:S(2)}) collective-permute-start(bf16[48,256]{1,0:T(8,128)(2,1)S(1)} %slice.85), channel_id=1, source_target_pairs={{0,16},{16,0},{1,17},{17,1},{2,18},{18,2},{3,19},{19,3},{4,20},{20... | collective-permute-start | bytes 73736 | tf_op jit(solution)/shard_map/ppermute | solution.py:137
Sparse Core Ops, SparseCore 0:
  20.5 66.5 all-gather.3
  89.3 29.4 all-gather.5

commit v7 on v6

--- a/solution.py
+++ b/solution.py
@@ -54,50 +54,9 @@
     )(rows)
 
 
-def projected(rows, weight, steps=4):
-    count, depth = rows.shape
-    columns = weight.shape[1]
-    part = depth // steps
-
-    def project(rows_ref, weight_ref, sum_ref, rounded_ref):
-        step = pl.program_id(0)
-        product = jnp.dot(rows_ref[...], weight_ref[...], preferred_element_type=F32)
-
-        @pl.when(step == 0)
-        def _():
-            sum_ref[...] = product
-
-        @pl.when(step > 0)
-        def _():
-            sum_ref[...] += product
-
-        @pl.when(step == steps - 1)
-        def _():
-            rounded_ref[...] = sum_ref[...].astype(rounded_ref.dtype)
-
-    whole = pl.BlockSpec((count, columns), lambda step: (0, 0))
-    return pl.pallas_call(
-        project,
-        grid=(steps,),
-        out_shape=(
-            jax.ShapeDtypeStruct((count, columns), F32),
-            jax.ShapeDtypeStruct((count, columns), BF16),
-        ),
-        in_specs=[
-            pl.BlockSpec((count, part), lambda step: (0, step)),
-            pl.BlockSpec((part, columns), lambda step: (step, 0)),
-        ],
-        out_specs=(whole, whole),
-        compiler_params=pltpu.CompilerParams(
-            dimension_semantics=("arbitrary",), vmem_limit_bytes=59 * 1024 * 1024
-        ),
-        cost_estimate=pl.CostEstimate(
-            flops=2 * count * depth * columns,
-            bytes_accessed=2 * (count + columns) * depth,
-            transcendentals=0,
-        ),
-        name="project",
-    )(rows, weight)
+def projected(rows, weight):
+    product = jnp.dot(rows, weight, preferred_element_type=F32)
+    return product, product.astype(BF16)
 
 
 def to_query(state, weight):
@@ -169,8 +128,8 @@
     state, query_weight, first_weight = lax.optimization_barrier(
         (state, query_weight, first_weight)
     )
-    first_query, output_weight = lax.optimization_barrier(
-        (to_query(state, query_weight), output_weight)
+    first_query, output_weight, gathered_tokens = lax.optimization_barrier(
+        (to_query(state, query_weight), output_weight, gathered_tokens)
     )
 
     def handed(partial_sum, direction):

time: 227 us -> 212 us (0.934)
  waiting for transfers between devices: 72.6 us -> 42.3 us
  blocking collectives: 43.5 us -> 70.1 us
  Pallas kernels: 11.5 us -> 0.88 us
  matrix products: 2.33 us -> 11.3 us
  starting transfers between devices: 64 us -> 57 us
    all_to_all x4 -> x5, blocking collectives: 43.5 us -> 70.1 us  [exchange(): return lax.all_to_all(blocks, axis, 0, 0, tiled=True)]
    all_to_all x7 -> x6, waiting for transfers between devices: 49.3 us -> 32.1 us  [exchange(): return lax.all_to_all(blocks, axis, 0, 0, tiled=True)]
    all_gather x1, waiting for transfers between devices: 13.3 us -> 0.01 us  [body(): lax.all_gather(after(pair, got_weight), 'tp', axis=0, tiled=True)]
    pallas_call x2 -> x0, Pallas kernels: 10.6 us -> none  [projected(): pl.pallas_call(project, grid=(steps,), out_shape=(jax.ShapeDtypeStruct((c...]
    dot_general x0 -> x2, matrix products: none -> 8.94 us  [projected(): product = jnp.dot(rows, weight, preferred_element_type=F32)]
    all_to_all x7 -> x6, starting transfers between devices: 46.5 us -> 38 us  [exchange(): return lax.all_to_all(blocks, axis, 0, 0, tiled=True)]
  transfers between devices with their start and end apart: 16 -> 15, of which waited for: 10 -> 8; matrix products, arithmetic and copies ran while one was open for 5% -> 7% of each run, Pallas kernels for 2% -> 0%
where the time goes in v7:
time: 212 us; the launch traced here: 210 us
  blocking collectives  70.1 us (33%)
  starting transfers between devices  57 us (27%)
  waiting for transfers between devices  42.3 us (20%)
  between operations  15.9 us (8%)
  matrix products  11.3 us (5%)
  local copies, waits for them, and re-layouts  9.56 us (5%)
  other arithmetic  3.54 us (2%)
    all_to_all x5, blocking collectives, exchange(): return lax.all_to_all(blocks, axis, 0, 0, tiled=True)  70.1 us
    all_to_all x6, starting transfers between devices, exchange(): return lax.all_to_all(blocks, axis, 0, 0, tiled=True)  38 us
    all_to_all x6, waiting for transfers between devices, exchange(): return lax.all_to_all(blocks, axis, 0, 0, tiled=True)  32.1 us
    ppermute x4, starting transfers between devices, to_other_core(): return lax.ppermute(block, 'core', SWAP)  11.3 us
    dot_general x2, matrix products, projected(): product = jnp.dot(rows, weight, preferred_element_type=F32)  8.94 us
    ppermute x2, waiting for transfers between devices, handed(): return lax.ppermute(partial_sum, 'section', [direction]).astype(F32)  6.45 us
  transfers between devices with their start and end apart: 15, of which 8 were waited for; matrix products, arithmetic and copies ran while one was open for 7% of the time, Pallas kernels for 0%

profile of v7, /device:TPU:1, one launch (start us, length us, event | category | flops | bytes accessed | tf_op | source)
XLA Modules:
  0.0 210.4 jit_solution(8346604330803605301)
XLA Ops:
  7.2 1.0 copy-done
  9.1 3.5 %all-to-all-start = ((bf16[2,32,4096]{2,1,0:T(8,128)(2,1)}), bf16[2,32,4096]{2,1,0:T(8,128)(2,1)S(1)}, u32[]{:S(2)}, u32[]{:S(2)}) async-start(bf16[2,32,4096]{2,1,0:T(8,128)(2,1)} %deal_halves.1), calls=%async_computation | async-start | bytes 1048576 | tf_op jit(solution)/shard_map/all_to_all | solution.py:24
  12.7 4.0 %collective-permute-start.2 = (bf16[128,256]{1,0:T(8,128)(2,1)S(1)}, bf16[128,256]{1,0:T(8,128)(2,1)S(1)}, u32[]{:S(2)}, u32[]{:S(2)}) collective-permute-start(bf16[128,256]{1,0:T(8,128)(2,1)S(1)} %get-tuple-element.40), channel_id=1, source_target_pairs={{0,8},{8,0},{1,9},{9,1},{2,10},{10,2},{3,11},{11,3},{4,12},{12,4},... | collective-permute-start | bytes 196616 | tf_op jit(solution)/shard_map/ppermute | solution.py:110
  16.7 2.7 %collective-permute-done.2 = bf16[128,256]{1,0:T(8,128)(2,1)S(1)} collective-permute-done((bf16[128,256]{1,0:T(8,128)(2,1)S(1)}, bf16[128,256]{1,0:T(8,128)(2,1)S(1)}, u32[]{:S(2)}, u32[]{:S(2)}) %collective-permute-start.2) | collective-permute-done | bytes 65568 | tf_op jit(solution)/shard_map/ppermute | solution.py:110
  20.3 24.0 %all_to_all.55 = bf16[4,2,128,256]{3,2,1,0:T(8,128)(2,1)S(1)} all-to-all(bf16[4,2,128,256]{3,2,1,0:T(8,128)(2,1)S(1)} %broadcast_in_dim.36), channel_id=1, replica_groups=mesh['far'=4,'row'=4,'core'=2,'section'=2,'tp'=8] {'far'}, dimensions={0} | all-to-all | bytes 1048576 | tf_op jit(solution)/shard_map/all_to_all | solution.py:24
  45.0 1.1 broadcast_in_dim.38
  46.1 4.0 %all-to-all-start.2 = ((bf16[4,4,128,256]{3,2,1,0:T(8,128)(2,1)}), bf16[4,4,128,256]{3,2,1,0:T(8,128)(2,1)S(1)}, u32[]{:S(2)}, u32[]{:S(2)}) async-start(bf16[4,4,128,256]{3,2,1,0:T(8,128)(2,1)} %broadcast_in_dim.38), calls=%async_computation.2 | async-start | bytes 2097152 | tf_op jit(solution)/shard_map/all_to_all | solution.py:24
  50.2 4.9 %collective-permute-start.1 = (bf16[256,1024]{1,0:T(8,128)(2,1)S(1)}, bf16[256,1024]{1,0:T(8,128)(2,1)}, u32[]{:S(2)}, u32[]{:S(2)}) collective-permute-start(bf16[256,1024]{1,0:T(8,128)(2,1)S(1)} %bitcast.69), channel_id=1, source_target_pairs={{0,16},{16,0},{1,17},{17,1},{2,18},{18,2},{3,19},{19,3},{4,20},{20... | collective-permute-start | bytes 1572872 | tf_op jit(solution)/shard_map/ppermute | solution.py:96
  55.3 1.9 collective-permute-start
  57.2 2.4 %collective-permute-start.3 = (bf16[1024,256]{1,0:T(8,128)(2,1)S(1)}, bf16[1024,256]{1,0:T(8,128)(2,1)}, u32[]{:S(2)}, u32[]{:S(2)}) collective-permute-start(bf16[1024,256]{1,0:T(8,128)(2,1)S(1)} %bitcast.71), channel_id=1, source_target_pairs={{0,16},{16,0},{1,17},{17,1},{2,18},{18,2},{3,19},{19,3},{4,20},{20... | collective-permute-start | bytes 1572872 | tf_op jit(solution)/shard_map/ppermute | solution.py:96
  59.7 1.1 pad_maximum_fusion
  60.8 1.2 all-to-all-done.2
  62.3 10.1 %all_to_all.56 = bf16[2,4,4,128,256]{4,3,2,1,0:T(8,128)(2,1)} all-to-all(bf16[2,4,4,128,256]{4,3,2,1,0:T(8,128)(2,1)S(1)} %broadcast_in_dim.39), channel_id=1, replica_groups=mesh['far'=4,'row'=4,'core'=2,'section'=2,'tp'=8] {'core'}, dimensions={0} | all-to-all | bytes 4194304 | tf_op jit(solution)/shard_map/all_to_all | solution.py:24
  73.4 5.4 %all-to-all-start.4 = ((bf16[16,3,1024]{2,1,0:T(4,128)(2,1)}), bf16[16,3,1024]{2,1,0:T(4,128)(2,1)S(1)}, u32[]{:S(2)}, u32[]{:S(2)}) async-start(bf16[16,3,1024]{2,1,0:T(4,128)(2,1)} %reshape.274), calls=%async_computation.4 | async-start | bytes 262144 | tf_op jit(solution)/shard_map/all_to_all | solution.py:24
  79.5 1.1 pad_maximum_fusion.1
  80.7 7.4 %all-to-all-done.4 = bf16[16,3,1024]{2,1,0:T(4,128)(2,1)S(1)} async-done(((bf16[16,3,1024]{2,1,0:T(4,128)(2,1)}), bf16[16,3,1024]{2,1,0:T(4,128)(2,1)S(1)}, u32[]{:S(2)}, u32[]{:S(2)}) %all-to-all-start.4) | async-done | bytes 98336 | tf_op jit(solution)/shard_map/all_to_all | solution.py:24
  88.2 4.1 %fusion.36 = (bf16[512,256]{1,0:T(8,128)(2,1)S(1)}, f32[512,256]{1,0:T(8,128)S(1)}) fusion(bf16[512,4096]{1,0:T(8,128)(2,1)} %all-gather.4.cloned.1.call-done, bf16[4096,256]{1,0:T(8,128)(2,1)} %bitcast.65), kind=kOutput, calls=%fused_computation.96 | convolution fusion | flops 1073872896 | bytes 7077888 | tf_op jit(solution)/shard_map/dot_general | solution.py:58
  92.3 1.3 collective-permute-start.4
  93.7 6.5 %collective-permute-done.4 = bf16[512,256]{1,0:T(8,128)(2,1)S(1)} collective-permute-done((bf16[512,256]{1,0:T(8,128)(2,1)S(1)}, bf16[512,256]{1,0:T(8,128)(2,1)S(1)}, u32[]{:S(2)}, u32[]{:S(2)}) %collective-permute-start.4) | collective-permute-done | bytes 262176 | tf_op jit(solution)/shard_map/ppermute | solution.py:136
  101.7 9.0 %all-to-all-start.5 = ((bf16[16,3,1024]{2,1,0:T(4,128)(2,1)}), bf16[16,3,1024]{2,1,0:T(4,128)(2,1)S(1)}, u32[]{:S(2)}, u32[]{:S(2)}) async-start(bf16[16,3,1024]{2,1,0:T(4,128)(2,1)} %broadcast_in_dim.43), calls=%async_computation.5 | async-start | bytes 262144 | tf_op jit(solution)/shard_map/all_to_all | solution.py:24
  111.4 8.7 %all-to-all-done.5 = bf16[16,3,1024]{2,1,0:T(4,128)(2,1)S(1)} async-done(((bf16[16,3,1024]{2,1,0:T(4,128)(2,1)}), bf16[16,3,1024]{2,1,0:T(4,128)(2,1)S(1)}, u32[]{:S(2)}, u32[]{:S(2)}) %all-to-all-start.5) | async-done | bytes 98336 | tf_op jit(solution)/shard_map/all_to_all | solution.py:24
  120.5 11.6 %all_to_all.57 = bf16[8,12,256]{2,1,0:T(8,128)(2,1)S(1)} all-to-all(bf16[8,12,256]{2,1,0:T(8,128)(2,1)S(1)} %reshape.278), channel_id=1, replica_groups=mesh['far'=4,'row'=4,'core'=2,'section'=2,'tp'=8] {'tp'}, dimensions={0} | all-to-all | bytes 98304 | tf_op jit(solution)/shard_map/all_to_all | solution.py:24
  132.2 10.0 %all_to_all.58 = bf16[16,12,256]{2,1,0:T(8,128)(2,1)S(1)} all-to-all(bf16[16,12,256]{2,1,0:T(8,128)(2,1)S(1)} %broadcast_in_dim.80), channel_id=1, replica_groups=mesh['far'=4,'row'=4,'core'=2,'section'=2,'tp'=8] {'section','tp'}, dimensions={0} | all-to-all | bytes 196608 | tf_op jit(solution)/shard_map/all_to_all | solution.py:24
  142.3 4.8 %fusion.38 = (bf16[512,256]{1,0:T(8,128)(2,1)}, f32[512,256]{1,0:T(8,128)S(1)}) fusion(bf16[512,4096]{1,0:T(8,128)(2,1)} %all-gather.4.cloned.1.call-done, bf16[4096,256]{1,0:T(8,128)(2,1)} %bitcast.77), kind=kOutput, calls=%fused_computation.98 | convolution fusion | flops 1073872896 | bytes 7077888 | tf_op jit(solution)/shard_map/dot_general | solution.py:58
  148.1 3.5 %all-to-all-start.8 = ((bf16[16,3,1024]{2,1,0:T(4,128)(2,1)}), bf16[16,3,1024]{2,1,0:T(4,128)(2,1)S(1)}, u32[]{:S(2)}, u32[]{:S(2)}) async-start(bf16[16,3,1024]{2,1,0:T(4,128)(2,1)} %reshape.283), calls=%async_computation.8 | async-start | bytes 262144 | tf_op jit(solution)/shard_map/all_to_all | solution.py:24
  151.7 2.3 %collective-permute-start.5 = (bf16[512,256]{1,0:T(8,128)(2,1)}, bf16[512,256]{1,0:T(8,128)(2,1)S(1)}, u32[]{:S(2)}, u32[]{:S(2)}) collective-permute-start(bf16[512,256]{1,0:T(8,128)(2,1)} %get-tuple-element.30), channel_id=1, source_target_pairs={{0,8},{1,9},{2,10},{3,11},{4,12},{5,13},{6,14},{7,15},{16,24},{17,... | collective-permute-start | bytes 786440 | tf_op jit(solution)/shard_map/ppermute | solution.py:136
  153.9 7.0 %all-to-all-done.8 = bf16[16,3,1024]{2,1,0:T(4,128)(2,1)S(1)} async-done(((bf16[16,3,1024]{2,1,0:T(4,128)(2,1)}), bf16[16,3,1024]{2,1,0:T(4,128)(2,1)S(1)}, u32[]{:S(2)}, u32[]{:S(2)}) %all-to-all-start.8) | async-done | bytes 98336 | tf_op jit(solution)/shard_map/all_to_all | solution.py:24
  162.0 14.4 %all_to_all.59 = bf16[16,3,1024]{2,1,0:T(4,128)(2,1)S(1)} all-to-all(bf16[16,3,1024]{2,1,0:T(4,128)(2,1)S(1)} %broadcast_in_dim.82), channel_id=1, replica_groups=mesh['far'=4,'row'=4,'core'=2,'section'=2,'tp'=8] {'far','row'}, dimensions={0} | all-to-all | bytes 196608 | tf_op jit(solution)/shard_map/all_to_all | solution.py:24
  177.6 12.6 %all-to-all-start.10 = ((bf16[16,48,256]{2,1,0:T(8,128)(2,1)}), bf16[16,48,256]{2,1,0:T(8,128)(2,1)S(1)}, u32[]{:S(2)}, u32[]{:S(2)}) async-start(bf16[16,48,256]{2,1,0:T(8,128)(2,1)} %bitcast.25), calls=%async_computation.10 | async-start | bytes 786432 | tf_op jit(solution)/shard_map/all_to_all | solution.py:24
  190.2 2.1 collective-permute-start.6
  192.4 1.0 collective-permute-done.6
  194.9 7.8 %all-to-all-done.10 = bf16[16,48,256]{2,1,0:T(8,128)(2,1)S(1)} async-done(((bf16[16,48,256]{2,1,0:T(8,128)(2,1)}), bf16[16,48,256]{2,1,0:T(8,128)(2,1)S(1)}, u32[]{:S(2)}, u32[]{:S(2)}) %all-to-all-start.10) | async-done | bytes 393248 | tf_op jit(solution)/shard_map/all_to_all | solution.py:24
  (95 shorter events, 12.1 us)
Async XLA Ops:
  7.2 1.0 copy-start
  8.2 4.4 %copy-start.4 = (bf16[1,256,1,256]{3,1,2,0:T(8,128)(2,1)S(1)}, bf16[1,256,1,256]{3,1,2,0:T(8,128)(2,1)}, u32[]{:S(2)}) copy-start(bf16[1,256,1,256]{3,1,2,0:T(8,128)(2,1)} %param.12) | copy-start | bytes 393220
  9.1 10.3 %all-to-all-start = ((bf16[2,32,4096]{2,1,0:T(8,128)(2,1)}), bf16[2,32,4096]{2,1,0:T(8,128)(2,1)S(1)}, u32[]{:S(2)}, u32[]{:S(2)}) async-start(bf16[2,32,4096]{2,1,0:T(8,128)(2,1)} %deal_halves.1), calls=%async_computation | async-start | bytes 1048576 | tf_op jit(solution)/shard_map/all_to_all | solution.py:24
  12.6 75.5 %all-gather.4.cloned.1.call-start = ((), (), s32[]{:S(2)}) async-start(), calls=%async_computation.11 | async-start | bytes 4718592 | tf_op jit(solution)/shard_map/all_gather | solution.py:111
  12.7 6.7 %collective-permute-start.2 = (bf16[128,256]{1,0:T(8,128)(2,1)S(1)}, bf16[128,256]{1,0:T(8,128)(2,1)S(1)}, u32[]{:S(2)}, u32[]{:S(2)}) collective-permute-start(bf16[128,256]{1,0:T(8,128)(2,1)S(1)} %get-tuple-element.40), channel_id=1, source_target_pairs={{0,8},{8,0},{1,9},{9,1},{2,10},{10,2},{3,11},{11,3},{4,12},{12,4},... | collective-permute-start | bytes 196616 | tf_op jit(solution)/shard_map/ppermute | solution.py:110
  19.4 0.8 copy-start.1
  44.3 5.9 %copy-start.5 = (bf16[32,3,256]{2,0,1:T(8,128)(2,1)S(1)}, bf16[32,3,256]{2,0,1:T(8,128)(2,1)}, u32[]{:S(2)}) copy-start(bf16[32,3,256]{2,0,1:T(8,128)(2,1)} %param.9) | copy-start | bytes 147460
  44.3 5.9 %copy-start.2 = (bf16[1,256,1024]{2,1,0:T(8,128)(2,1)S(1)}, bf16[1,256,1024]{2,1,0:T(8,128)(2,1)}, u32[]{:S(2)}) copy-start(bf16[1,256,1024]{2,1,0:T(8,128)(2,1)} %param.14) | copy-start | bytes 1572868
  45.0 12.2 %copy-start.3 = (bf16[1,1024,256]{2,1,0:T(8,128)(2,1)S(1)}, bf16[1,1024,256]{2,1,0:T(8,128)(2,1)}, u32[]{:S(2)}) copy-start(bf16[1,1024,256]{2,1,0:T(8,128)(2,1)} %param.16) | copy-start | bytes 1572868
  46.1 15.9 %all-to-all-start.2 = ((bf16[4,4,128,256]{3,2,1,0:T(8,128)(2,1)}), bf16[4,4,128,256]{3,2,1,0:T(8,128)(2,1)S(1)}, u32[]{:S(2)}, u32[]{:S(2)}) async-start(bf16[4,4,128,256]{3,2,1,0:T(8,128)(2,1)} %broadcast_in_dim.38), calls=%async_computation.2 | async-start | bytes 2097152 | tf_op jit(solution)/shard_map/all_to_all | solution.py:24
  50.2 9.5 %collective-permute-start.1 = (bf16[256,1024]{1,0:T(8,128)(2,1)S(1)}, bf16[256,1024]{1,0:T(8,128)(2,1)}, u32[]{:S(2)}, u32[]{:S(2)}) collective-permute-start(bf16[256,1024]{1,0:T(8,128)(2,1)S(1)} %bitcast.69), channel_id=1, source_target_pairs={{0,16},{16,0},{1,17},{17,1},{2,18},{18,2},{3,19},{19,3},{4,20},{20... | collective-permute-start | bytes 1572872 | tf_op jit(solution)/shard_map/ppermute | solution.py:96
  55.3 4.4 %collective-permute-start = (bf16[48,256]{1,0:T(8,128)(2,1)S(1)}, bf16[48,256]{1,0:T(8,128)(2,1)S(1)}, u32[]{:S(2)}, u32[]{:S(2)}) collective-permute-start(bf16[48,256]{1,0:T(8,128)(2,1)S(1)} %select_n.145), channel_id=1, source_target_pairs={{0,16},{16,0},{1,17},{17,1},{2,18},{18,2},{3,19},{19,3},{4,20},{20... | collective-permute-start | bytes 73736 | tf_op jit(solution)/shard_map/ppermute | solution.py:96
  57.2 22.3 %collective-permute-start.3 = (bf16[1024,256]{1,0:T(8,128)(2,1)S(1)}, bf16[1024,256]{1,0:T(8,128)(2,1)}, u32[]{:S(2)}, u32[]{:S(2)}) collective-permute-start(bf16[1024,256]{1,0:T(8,128)(2,1)S(1)} %bitcast.71), channel_id=1, source_target_pairs={{0,16},{16,0},{1,17},{17,1},{2,18},{18,2},{3,19},{19,3},{4,20},{20... | collective-permute-start | bytes 1572872 | tf_op jit(solution)/shard_map/ppermute | solution.py:96
  62.3 16.6 %copy-start.6 = (bf16[1,128]{1,0:T(2,128)(2,1)S(1)}, bf16[1,128]{1,0:T(2,128)(2,1)}, u32[]{:S(2)}) copy-start(bf16[1,128]{1,0:T(2,128)(2,1)} %param.15) | copy-start | bytes 772
  62.3 16.6 %copy-start.7 = (bf16[1,128]{1,0:T(2,128)(2,1)S(1)}, bf16[1,128]{1,0:T(2,128)(2,1)}, u32[]{:S(2)}) copy-start(bf16[1,128]{1,0:T(2,128)(2,1)} %param.13) | copy-start | bytes 772
  73.4 14.6 %all-to-all-start.4 = ((bf16[16,3,1024]{2,1,0:T(4,128)(2,1)}), bf16[16,3,1024]{2,1,0:T(4,128)(2,1)S(1)}, u32[]{:S(2)}, u32[]{:S(2)}) async-start(bf16[16,3,1024]{2,1,0:T(4,128)(2,1)} %reshape.274), calls=%async_computation.4 | async-start | bytes 262144 | tf_op jit(solution)/shard_map/all_to_all | solution.py:24
  78.8 63.5 %all-gather.6.cloned.1.call-start = ((), (), s32[]{:S(2)}) async-start(), calls=%async_computation.12 | async-start | bytes 2359296 | tf_op jit(solution)/shard_map/all_gather | solution.py:149
  92.3 7.9 %collective-permute-start.4 = (bf16[512,256]{1,0:T(8,128)(2,1)S(1)}, bf16[512,256]{1,0:T(8,128)(2,1)S(1)}, u32[]{:S(2)}, u32[]{:S(2)}) collective-permute-start(bf16[512,256]{1,0:T(8,128)(2,1)S(1)} %get-tuple-element.49), channel_id=1, source_target_pairs={{8,0},{9,1},{10,2},{11,3},{12,4},{13,5},{14,6},{15,7},{24,16},{25,... | collective-permute-start | bytes 786440 | tf_op jit(solution)/shard_map/ppermute | solution.py:136
  101.7 18.4 %all-to-all-start.5 = ((bf16[16,3,1024]{2,1,0:T(4,128)(2,1)}), bf16[16,3,1024]{2,1,0:T(4,128)(2,1)S(1)}, u32[]{:S(2)}, u32[]{:S(2)}) async-start(bf16[16,3,1024]{2,1,0:T(4,128)(2,1)} %broadcast_in_dim.43), calls=%async_computation.5 | async-start | bytes 262144 | tf_op jit(solution)/shard_map/all_to_all | solution.py:24
  148.1 12.8 %all-to-all-start.8 = ((bf16[16,3,1024]{2,1,0:T(4,128)(2,1)}), bf16[16,3,1024]{2,1,0:T(4,128)(2,1)S(1)}, u32[]{:S(2)}, u32[]{:S(2)}) async-start(bf16[16,3,1024]{2,1,0:T(4,128)(2,1)} %reshape.283), calls=%async_computation.8 | async-start | bytes 262144 | tf_op jit(solution)/shard_map/all_to_all | solution.py:24
  151.7 9.5 %collective-permute-start.5 = (bf16[512,256]{1,0:T(8,128)(2,1)}, bf16[512,256]{1,0:T(8,128)(2,1)S(1)}, u32[]{:S(2)}, u32[]{:S(2)}) collective-permute-start(bf16[512,256]{1,0:T(8,128)(2,1)} %get-tuple-element.30), channel_id=1, source_target_pairs={{0,8},{1,9},{2,10},{3,11},{4,12},{5,13},{6,14},{7,15},{16,24},{17,... | collective-permute-start | bytes 786440 | tf_op jit(solution)/shard_map/ppermute | solution.py:136
  177.6 25.1 %all-to-all-start.10 = ((bf16[16,48,256]{2,1,0:T(8,128)(2,1)}), bf16[16,48,256]{2,1,0:T(8,128)(2,1)S(1)}, u32[]{:S(2)}, u32[]{:S(2)}) async-start(bf16[16,48,256]{2,1,0:T(8,128)(2,1)} %bitcast.25), calls=%async_computation.10 | async-start | bytes 786432 | tf_op jit(solution)/shard_map/all_to_all | solution.py:24
  190.2 3.1 %collective-permute-start.6 = (bf16[48,256]{1,0:T(8,128)(2,1)S(1)}, bf16[48,256]{1,0:T(8,128)(2,1)S(1)}, u32[]{:S(2)}, u32[]{:S(2)}) collective-permute-start(bf16[48,256]{1,0:T(8,128)(2,1)S(1)} %slice.85), channel_id=1, source_target_pairs={{0,16},{16,0},{1,17},{17,1},{2,18},{18,2},{3,19},{19,3},{4,20},{20... | collective-permute-start | bytes 73736 | tf_op jit(solution)/shard_map/ppermute | solution.py:96
Sparse Core Ops, SparseCore 0:
  20.4 66.5 all-gather.3
  89.1 29.7 all-gather.5

commit v8 on v7

--- a/solution.py
+++ b/solution.py
@@ -158,6 +158,7 @@
         output_weight,
         gate,
     )
+    first_sum, second_weight = lax.optimization_barrier((first_sum, second_weight))
     first_sum = jnp.concatenate([first_sum[:, :columns], first_sum[:, columns:]])
     first_sum = first_sum.reshape(tensor_count, -1, columns)
     summed = jnp.sum(exchange(first_sum, "tp").astype(F32), axis=0).astype(BF16)
@@ -166,7 +167,7 @@
     everywhere = jnp.concatenate([everywhere[0], everywhere[1]], axis=1)
     first = (state.astype(F32) + everywhere).astype(BF16)
 
-    second_partial, given = projected(gathered_tokens, after(second_weight, summed))
+    second_partial, given = projected(gathered_tokens, second_weight)
     given, late = lax.optimization_barrier((given, first))
     second_other = handed(given, (0, 1))
     second_query = to_query(late, query_weight)

time: 212 us -> 213 us (level)
  blocking collectives: 70.1 us -> 61.4 us
  starting transfers between devices: 57 us -> 62.4 us
  waiting for transfers between devices: 42.3 us -> 45.6 us
    all_to_all x5 -> x4, blocking collectives: 70.1 us -> 61.4 us  [exchange(): return lax.all_to_all(blocks, axis, 0, 0, tiled=True)]
    all_to_all x6 -> x7, starting transfers between devices: 38 us -> 43.5 us  [exchange(): return lax.all_to_all(blocks, axis, 0, 0, tiled=True)]
    all_to_all x6 -> x7, waiting for transfers between devices: 32.1 us -> 35.4 us  [exchange(): return lax.all_to_all(blocks, axis, 0, 0, tiled=True)]
  transfers between devices with their start and end apart: 15 -> 16, of which waited for: 8 -> 9; matrix products, arithmetic and copies ran while one was open for 7% -> 9% of each run, Pallas kernels for 0% -> 0%
where the time goes in v8:
time: 213 us; the launch traced here: 211 us
  starting transfers between devices  62.4 us (29%)
  blocking collectives  61.4 us (29%)
  waiting for transfers between devices  45.6 us (21%)
  between operations  15.9 us (7%)
  matrix products  11.3 us (5%)
  local copies, waits for them, and re-layouts  10.2 us (5%)
  other arithmetic  3.55 us (2%)
    all_to_all x4, blocking collectives, exchange(): return lax.all_to_all(blocks, axis, 0, 0, tiled=True)  61.4 us
    all_to_all x7, starting transfers between devices, exchange(): return lax.all_to_all(blocks, axis, 0, 0, tiled=True)  43.5 us
    all_to_all x7, waiting for transfers between devices, exchange(): return lax.all_to_all(blocks, axis, 0, 0, tiled=True)  35.4 us
    ppermute x4, starting transfers between devices, to_other_core(): return lax.ppermute(block, 'core', SWAP)  11.2 us
    dot_general x2, matrix products, projected(): product = jnp.dot(rows, weight, preferred_element_type=F32)  8.95 us
    ppermute x2, waiting for transfers between devices, handed(): return lax.ppermute(partial_sum, 'section', [direction]).astype(F32)  6.45 us
  transfers between devices with their start and end apart: 16, of which 9 were waited for; matrix products, arithmetic and copies ran while one was open for 9% of the time, Pallas kernels for 0%

profile of v8, /device:TPU:1, one launch (start us, length us, event | category | flops | bytes accessed | tf_op | source)
XLA Modules:
  0.0 211.3 jit_solution(4480083653225708066)
XLA Ops:
  9.1 3.5 %all-to-all-start = ((bf16[2,32,4096]{2,1,0:T(8,128)(2,1)}), bf16[2,32,4096]{2,1,0:T(8,128)(2,1)S(1)}, u32[]{:S(2)}, u32[]{:S(2)}) async-start(bf16[2,32,4096]{2,1,0:T(8,128)(2,1)} %deal_halves.1), calls=%async_computation | async-start | bytes 1048576 | tf_op jit(solution)/shard_map/all_to_all | solution.py:24
  12.7 4.0 %collective-permute-start.2 = (bf16[128,256]{1,0:T(8,128)(2,1)S(1)}, bf16[128,256]{1,0:T(8,128)(2,1)S(1)}, u32[]{:S(2)}, u32[]{:S(2)}) collective-permute-start(bf16[128,256]{1,0:T(8,128)(2,1)S(1)} %get-tuple-element.42), channel_id=1, source_target_pairs={{0,8},{8,0},{1,9},{9,1},{2,10},{10,2},{3,11},{11,3},{4,12},{12,4},... | collective-permute-start | bytes 196616 | tf_op jit(solution)/shard_map/ppermute | solution.py:110
  16.7 2.7 %collective-permute-done.2 = bf16[128,256]{1,0:T(8,128)(2,1)S(1)} collective-permute-done((bf16[128,256]{1,0:T(8,128)(2,1)S(1)}, bf16[128,256]{1,0:T(8,128)(2,1)S(1)}, u32[]{:S(2)}, u32[]{:S(2)}) %collective-permute-start.2) | collective-permute-done | bytes 65568 | tf_op jit(solution)/shard_map/ppermute | solution.py:110
  20.3 24.0 %all_to_all.55 = bf16[4,2,128,256]{3,2,1,0:T(8,128)(2,1)S(1)} all-to-all(bf16[4,2,128,256]{3,2,1,0:T(8,128)(2,1)S(1)} %broadcast_in_dim.36), channel_id=1, replica_groups=mesh['far'=4,'row'=4,'core'=2,'section'=2,'tp'=8] {'far'}, dimensions={0} | all-to-all | bytes 1048576 | tf_op jit(solution)/shard_map/all_to_all | solution.py:24
  45.0 1.1 broadcast_in_dim.38
  46.1 4.0 %all-to-all-start.2 = ((bf16[4,4,128,256]{3,2,1,0:T(8,128)(2,1)}), bf16[4,4,128,256]{3,2,1,0:T(8,128)(2,1)S(1)}, u32[]{:S(2)}, u32[]{:S(2)}) async-start(bf16[4,4,128,256]{3,2,1,0:T(8,128)(2,1)} %broadcast_in_dim.38), calls=%async_computation.2 | async-start | bytes 2097152 | tf_op jit(solution)/shard_map/all_to_all | solution.py:24
  50.2 4.9 %collective-permute-start.1 = (bf16[256,1024]{1,0:T(8,128)(2,1)S(1)}, bf16[256,1024]{1,0:T(8,128)(2,1)}, u32[]{:S(2)}, u32[]{:S(2)}) collective-permute-start(bf16[256,1024]{1,0:T(8,128)(2,1)S(1)} %bitcast.69), channel_id=1, source_target_pairs={{0,16},{16,0},{1,17},{17,1},{2,18},{18,2},{3,19},{19,3},{4,20},{20... | collective-permute-start | bytes 1572872 | tf_op jit(solution)/shard_map/ppermute | solution.py:96
  55.3 1.9 collective-permute-start
  57.2 2.4 %collective-permute-start.3 = (bf16[1024,256]{1,0:T(8,128)(2,1)S(1)}, bf16[1024,256]{1,0:T(8,128)(2,1)}, u32[]{:S(2)}, u32[]{:S(2)}) collective-permute-start(bf16[1024,256]{1,0:T(8,128)(2,1)S(1)} %bitcast.71), channel_id=1, source_target_pairs={{0,16},{16,0},{1,17},{17,1},{2,18},{18,2},{3,19},{19,3},{4,20},{20... | collective-permute-start | bytes 1572872 | tf_op jit(solution)/shard_map/ppermute | solution.py:96
  59.7 1.1 pad_maximum_fusion
  60.8 1.2 all-to-all-done.2
  62.3 10.1 %all_to_all.56 = bf16[2,4,4,128,256]{4,3,2,1,0:T(8,128)(2,1)} all-to-all(bf16[2,4,4,128,256]{4,3,2,1,0:T(8,128)(2,1)S(1)} %broadcast_in_dim.39), channel_id=1, replica_groups=mesh['far'=4,'row'=4,'core'=2,'section'=2,'tp'=8] {'core'}, dimensions={0} | all-to-all | bytes 4194304 | tf_op jit(solution)/shard_map/all_to_all | solution.py:24
  73.4 5.4 %all-to-all-start.4 = ((bf16[16,3,1024]{2,1,0:T(4,128)(2,1)}), bf16[16,3,1024]{2,1,0:T(4,128)(2,1)S(1)}, u32[]{:S(2)}, u32[]{:S(2)}) async-start(bf16[16,3,1024]{2,1,0:T(4,128)(2,1)} %reshape.274), calls=%async_computation.4 | async-start | bytes 262144 | tf_op jit(solution)/shard_map/all_to_all | solution.py:24
  78.8 1.1 pad_maximum_fusion.1
  80.0 8.0 %all-to-all-done.4 = bf16[16,3,1024]{2,1,0:T(4,128)(2,1)S(1)} async-done(((bf16[16,3,1024]{2,1,0:T(4,128)(2,1)}), bf16[16,3,1024]{2,1,0:T(4,128)(2,1)S(1)}, u32[]{:S(2)}, u32[]{:S(2)}) %all-to-all-start.4) | async-done | bytes 98336 | tf_op jit(solution)/shard_map/all_to_all | solution.py:24
  88.8 4.1 %fusion.36 = (bf16[512,256]{1,0:T(8,128)(2,1)S(1)}, f32[512,256]{1,0:T(8,128)S(1)}) fusion(bf16[512,4096]{1,0:T(8,128)(2,1)} %all-gather.4.cloned.1.call-done, bf16[4096,256]{1,0:T(8,128)(2,1)} %bitcast.65), kind=kOutput, calls=%fused_computation.96 | convolution fusion | flops 1073872896 | bytes 7077888 | tf_op jit(solution)/shard_map/dot_general | solution.py:58
  92.9 1.3 collective-permute-start.4
  94.4 6.5 %collective-permute-done.4 = bf16[512,256]{1,0:T(8,128)(2,1)S(1)} collective-permute-done((bf16[512,256]{1,0:T(8,128)(2,1)S(1)}, bf16[512,256]{1,0:T(8,128)(2,1)S(1)}, u32[]{:S(2)}, u32[]{:S(2)}) %collective-permute-start.4) | collective-permute-done | bytes 262176 | tf_op jit(solution)/shard_map/ppermute | solution.py:136
  102.4 9.1 %all-to-all-start.5 = ((bf16[16,3,1024]{2,1,0:T(4,128)(2,1)}), bf16[16,3,1024]{2,1,0:T(4,128)(2,1)S(1)}, u32[]{:S(2)}, u32[]{:S(2)}) async-start(bf16[16,3,1024]{2,1,0:T(4,128)(2,1)} %broadcast_in_dim.43), calls=%async_computation.5 | async-start | bytes 262144 | tf_op jit(solution)/shard_map/all_to_all | solution.py:24
  112.1 8.7 %all-to-all-done.5 = bf16[16,3,1024]{2,1,0:T(4,128)(2,1)S(1)} async-done(((bf16[16,3,1024]{2,1,0:T(4,128)(2,1)}), bf16[16,3,1024]{2,1,0:T(4,128)(2,1)S(1)}, u32[]{:S(2)}, u32[]{:S(2)}) %all-to-all-start.5) | async-done | bytes 98336 | tf_op jit(solution)/shard_map/all_to_all | solution.py:24
  121.3 11.6 %all_to_all.57 = bf16[8,12,256]{2,1,0:T(8,128)(2,1)S(1)} all-to-all(bf16[8,12,256]{2,1,0:T(8,128)(2,1)S(1)} %reshape.278), channel_id=1, replica_groups=mesh['far'=4,'row'=4,'core'=2,'section'=2,'tp'=8] {'tp'}, dimensions={0} | all-to-all | bytes 98304 | tf_op jit(solution)/shard_map/all_to_all | solution.py:24
  133.5 3.5 %all-to-all-start.7 = ((bf16[16,12,256]{2,1,0:T(8,128)(2,1)}), bf16[16,12,256]{2,1,0:T(8,128)(2,1)S(1)}, u32[]{:S(2)}, u32[]{:S(2)}) async-start(bf16[16,12,256]{2,1,0:T(8,128)(2,1)} %broadcast_in_dim.80), calls=%async_computation.7 | async-start | bytes 262144 | tf_op jit(solution)/shard_map/all_to_all | solution.py:24
  137.1 4.8 %fusion.38 = (bf16[512,256]{1,0:T(8,128)(2,1)}, f32[512,256]{1,0:T(8,128)S(1)}) fusion(bf16[512,4096]{1,0:T(8,128)(2,1)} %all-gather.4.cloned.1.call-done, bf16[4096,256]{1,0:T(8,128)(2,1)} %bitcast.77), kind=kOutput, calls=%fused_computation.98 | convolution fusion | flops 1073872896 | bytes 7077888 | tf_op jit(solution)/shard_map/dot_general | solution.py:58
  141.9 2.5 %all-to-all-done.7 = bf16[16,12,256]{2,1,0:T(8,128)(2,1)S(1)} async-done(((bf16[16,12,256]{2,1,0:T(8,128)(2,1)}), bf16[16,12,256]{2,1,0:T(8,128)(2,1)S(1)}, u32[]{:S(2)}, u32[]{:S(2)}) %all-to-all-start.7) | async-done | bytes 98336 | tf_op jit(solution)/shard_map/all_to_all | solution.py:24
  145.5 8.6 %all-to-all-start.8 = ((bf16[16,3,1024]{2,1,0:T(4,128)(2,1)}), bf16[16,3,1024]{2,1,0:T(4,128)(2,1)S(1)}, u32[]{:S(2)}, u32[]{:S(2)}) async-start(bf16[16,3,1024]{2,1,0:T(4,128)(2,1)} %reshape.283), calls=%async_computation.8 | async-start | bytes 262144 | tf_op jit(solution)/shard_map/all_to_all | solution.py:24
  154.2 2.2 %collective-permute-start.5 = (bf16[512,256]{1,0:T(8,128)(2,1)}, bf16[512,256]{1,0:T(8,128)(2,1)S(1)}, u32[]{:S(2)}, u32[]{:S(2)}) collective-permute-start(bf16[512,256]{1,0:T(8,128)(2,1)} %get-tuple-element.32), channel_id=1, source_target_pairs={{0,8},{1,9},{2,10},{3,11},{4,12},{5,13},{6,14},{7,15},{16,24},{17,... | collective-permute-start | bytes 786440 | tf_op jit(solution)/shard_map/ppermute | solution.py:136
  156.4 7.1 %all-to-all-done.8 = bf16[16,3,1024]{2,1,0:T(4,128)(2,1)S(1)} async-done(((bf16[16,3,1024]{2,1,0:T(4,128)(2,1)}), bf16[16,3,1024]{2,1,0:T(4,128)(2,1)S(1)}, u32[]{:S(2)}, u32[]{:S(2)}) %all-to-all-start.8) | async-done | bytes 98336 | tf_op jit(solution)/shard_map/all_to_all | solution.py:24
  164.7 15.8 %all_to_all.58 = bf16[16,3,1024]{2,1,0:T(4,128)(2,1)S(1)} all-to-all(bf16[16,3,1024]{2,1,0:T(4,128)(2,1)S(1)} %broadcast_in_dim.82), channel_id=1, replica_groups=mesh['far'=4,'row'=4,'core'=2,'section'=2,'tp'=8] {'far','row'}, dimensions={0} | all-to-all | bytes 196608 | tf_op jit(solution)/shard_map/all_to_all | solution.py:24
  181.6 9.4 %all-to-all-start.10 = ((bf16[16,48,256]{2,1,0:T(8,128)(2,1)}), bf16[16,48,256]{2,1,0:T(8,128)(2,1)S(1)}, u32[]{:S(2)}, u32[]{:S(2)}) async-start(bf16[16,48,256]{2,1,0:T(8,128)(2,1)} %bitcast.25), calls=%async_computation.10 | async-start | bytes 786432 | tf_op jit(solution)/shard_map/all_to_all | solution.py:24
  191.0 2.0 collective-permute-start.6
  193.1 1.0 collective-permute-done.6
  195.7 7.8 %all-to-all-done.10 = bf16[16,48,256]{2,1,0:T(8,128)(2,1)S(1)} async-done(((bf16[16,48,256]{2,1,0:T(8,128)(2,1)}), bf16[16,48,256]{2,1,0:T(8,128)(2,1)S(1)}, u32[]{:S(2)}, u32[]{:S(2)}) %all-to-all-start.10) | async-done | bytes 393248 | tf_op jit(solution)/shard_map/all_to_all | solution.py:24
  (96 shorter events, 13.8 us)
Async XLA Ops:
  7.2 1.0 copy-start
  8.2 4.5 %copy-start.4 = (bf16[1,256,1,256]{3,1,2,0:T(8,128)(2,1)S(1)}, bf16[1,256,1,256]{3,1,2,0:T(8,128)(2,1)}, u32[]{:S(2)}) copy-start(bf16[1,256,1,256]{3,1,2,0:T(8,128)(2,1)} %param.12) | copy-start | bytes 393220
  9.1 10.3 %all-to-all-start = ((bf16[2,32,4096]{2,1,0:T(8,128)(2,1)}), bf16[2,32,4096]{2,1,0:T(8,128)(2,1)S(1)}, u32[]{:S(2)}, u32[]{:S(2)}) async-start(bf16[2,32,4096]{2,1,0:T(8,128)(2,1)} %deal_halves.1), calls=%async_computation | async-start | bytes 1048576 | tf_op jit(solution)/shard_map/all_to_all | solution.py:24
  12.6 75.5 %all-gather.4.cloned.1.call-start = ((), (), s32[]{:S(2)}) async-start(), calls=%async_computation.11 | async-start | bytes 4718592 | tf_op jit(solution)/shard_map/all_gather | solution.py:111
  12.7 6.7 %collective-permute-start.2 = (bf16[128,256]{1,0:T(8,128)(2,1)S(1)}, bf16[128,256]{1,0:T(8,128)(2,1)S(1)}, u32[]{:S(2)}, u32[]{:S(2)}) collective-permute-start(bf16[128,256]{1,0:T(8,128)(2,1)S(1)} %get-tuple-element.42), channel_id=1, source_target_pairs={{0,8},{8,0},{1,9},{9,1},{2,10},{10,2},{3,11},{11,3},{4,12},{12,4},... | collective-permute-start | bytes 196616 | tf_op jit(solution)/shard_map/ppermute | solution.py:110
  19.4 0.8 copy-start.1
  44.3 5.9 %copy-start.5 = (bf16[32,3,256]{2,0,1:T(8,128)(2,1)S(1)}, bf16[32,3,256]{2,0,1:T(8,128)(2,1)}, u32[]{:S(2)}) copy-start(bf16[32,3,256]{2,0,1:T(8,128)(2,1)} %param.9) | copy-start | bytes 147460
  44.3 5.9 %copy-start.2 = (bf16[1,256,1024]{2,1,0:T(8,128)(2,1)S(1)}, bf16[1,256,1024]{2,1,0:T(8,128)(2,1)}, u32[]{:S(2)}) copy-start(bf16[1,256,1024]{2,1,0:T(8,128)(2,1)} %param.14) | copy-start | bytes 1572868
  45.0 12.2 %copy-start.3 = (bf16[1,1024,256]{2,1,0:T(8,128)(2,1)S(1)}, bf16[1,1024,256]{2,1,0:T(8,128)(2,1)}, u32[]{:S(2)}) copy-start(bf16[1,1024,256]{2,1,0:T(8,128)(2,1)} %param.16) | copy-start | bytes 1572868
  46.1 15.9 %all-to-all-start.2 = ((bf16[4,4,128,256]{3,2,1,0:T(8,128)(2,1)}), bf16[4,4,128,256]{3,2,1,0:T(8,128)(2,1)S(1)}, u32[]{:S(2)}, u32[]{:S(2)}) async-start(bf16[4,4,128,256]{3,2,1,0:T(8,128)(2,1)} %broadcast_in_dim.38), calls=%async_computation.2 | async-start | bytes 2097152 | tf_op jit(solution)/shard_map/all_to_all | solution.py:24
  50.2 9.5 %collective-permute-start.1 = (bf16[256,1024]{1,0:T(8,128)(2,1)S(1)}, bf16[256,1024]{1,0:T(8,128)(2,1)}, u32[]{:S(2)}, u32[]{:S(2)}) collective-permute-start(bf16[256,1024]{1,0:T(8,128)(2,1)S(1)} %bitcast.69), channel_id=1, source_target_pairs={{0,16},{16,0},{1,17},{17,1},{2,18},{18,2},{3,19},{19,3},{4,20},{20... | collective-permute-start | bytes 1572872 | tf_op jit(solution)/shard_map/ppermute | solution.py:96
  55.3 4.4 %collective-permute-start = (bf16[48,256]{1,0:T(8,128)(2,1)S(1)}, bf16[48,256]{1,0:T(8,128)(2,1)S(1)}, u32[]{:S(2)}, u32[]{:S(2)}) collective-permute-start(bf16[48,256]{1,0:T(8,128)(2,1)S(1)} %select_n.145), channel_id=1, source_target_pairs={{0,16},{16,0},{1,17},{17,1},{2,18},{18,2},{3,19},{19,3},{4,20},{20... | collective-permute-start | bytes 73736 | tf_op jit(solution)/shard_map/ppermute | solution.py:96
  57.2 21.6 %collective-permute-start.3 = (bf16[1024,256]{1,0:T(8,128)(2,1)S(1)}, bf16[1024,256]{1,0:T(8,128)(2,1)}, u32[]{:S(2)}, u32[]{:S(2)}) collective-permute-start(bf16[1024,256]{1,0:T(8,128)(2,1)S(1)} %bitcast.71), channel_id=1, source_target_pairs={{0,16},{16,0},{1,17},{17,1},{2,18},{18,2},{3,19},{19,3},{4,20},{20... | collective-permute-start | bytes 1572872 | tf_op jit(solution)/shard_map/ppermute | solution.py:96
  72.4 16.4 %copy-start.6 = (bf16[1,128]{1,0:T(2,128)(2,1)S(1)}, bf16[1,128]{1,0:T(2,128)(2,1)}, u32[]{:S(2)}) copy-start(bf16[1,128]{1,0:T(2,128)(2,1)} %param.15) | copy-start | bytes 772
  72.4 16.4 %copy-start.7 = (bf16[1,128]{1,0:T(2,128)(2,1)S(1)}, bf16[1,128]{1,0:T(2,128)(2,1)}, u32[]{:S(2)}) copy-start(bf16[1,128]{1,0:T(2,128)(2,1)} %param.13) | copy-start | bytes 772
  73.4 14.6 %all-to-all-start.4 = ((bf16[16,3,1024]{2,1,0:T(4,128)(2,1)}), bf16[16,3,1024]{2,1,0:T(4,128)(2,1)S(1)}, u32[]{:S(2)}, u32[]{:S(2)}) async-start(bf16[16,3,1024]{2,1,0:T(4,128)(2,1)} %reshape.274), calls=%async_computation.4 | async-start | bytes 262144 | tf_op jit(solution)/shard_map/all_to_all | solution.py:24
  78.8 42.4 %all-gather.6.cloned.1.call-start = ((), (), s32[]{:S(2)}) async-start(), calls=%async_computation.12 | async-start | bytes 2359296 | tf_op jit(solution)/shard_map/all_gather | solution.py:149
  92.9 7.9 %collective-permute-start.4 = (bf16[512,256]{1,0:T(8,128)(2,1)S(1)}, bf16[512,256]{1,0:T(8,128)(2,1)S(1)}, u32[]{:S(2)}, u32[]{:S(2)}) collective-permute-start(bf16[512,256]{1,0:T(8,128)(2,1)S(1)} %get-tuple-element.51), channel_id=1, source_target_pairs={{8,0},{9,1},{10,2},{11,3},{12,4},{13,5},{14,6},{15,7},{24,16},{25,... | collective-permute-start | bytes 786440 | tf_op jit(solution)/shard_map/ppermute | solution.py:136
  102.4 18.4 %all-to-all-start.5 = ((bf16[16,3,1024]{2,1,0:T(4,128)(2,1)}), bf16[16,3,1024]{2,1,0:T(4,128)(2,1)S(1)}, u32[]{:S(2)}, u32[]{:S(2)}) async-start(bf16[16,3,1024]{2,1,0:T(4,128)(2,1)} %broadcast_in_dim.43), calls=%async_computation.5 | async-start | bytes 262144 | tf_op jit(solution)/shard_map/all_to_all | solution.py:24
  133.5 10.9 %all-to-all-start.7 = ((bf16[16,12,256]{2,1,0:T(8,128)(2,1)}), bf16[16,12,256]{2,1,0:T(8,128)(2,1)S(1)}, u32[]{:S(2)}, u32[]{:S(2)}) async-start(bf16[16,12,256]{2,1,0:T(8,128)(2,1)} %broadcast_in_dim.80), calls=%async_computation.7 | async-start | bytes 262144 | tf_op jit(solution)/shard_map/all_to_all | solution.py:24
  145.5 18.0 %all-to-all-start.8 = ((bf16[16,3,1024]{2,1,0:T(4,128)(2,1)}), bf16[16,3,1024]{2,1,0:T(4,128)(2,1)S(1)}, u32[]{:S(2)}, u32[]{:S(2)}) async-start(bf16[16,3,1024]{2,1,0:T(4,128)(2,1)} %reshape.283), calls=%async_computation.8 | async-start | bytes 262144 | tf_op jit(solution)/shard_map/all_to_all | solution.py:24
  154.2 9.6 %collective-permute-start.5 = (bf16[512,256]{1,0:T(8,128)(2,1)}, bf16[512,256]{1,0:T(8,128)(2,1)S(1)}, u32[]{:S(2)}, u32[]{:S(2)}) collective-permute-start(bf16[512,256]{1,0:T(8,128)(2,1)} %get-tuple-element.32), channel_id=1, source_target_pairs={{0,8},{1,9},{2,10},{3,11},{4,12},{5,13},{6,14},{7,15},{16,24},{17,... | collective-permute-start | bytes 786440 | tf_op jit(solution)/shard_map/ppermute | solution.py:136
  181.6 21.9 %all-to-all-start.10 = ((bf16[16,48,256]{2,1,0:T(8,128)(2,1)}), bf16[16,48,256]{2,1,0:T(8,128)(2,1)S(1)}, u32[]{:S(2)}, u32[]{:S(2)}) async-start(bf16[16,48,256]{2,1,0:T(8,128)(2,1)} %bitcast.25), calls=%async_computation.10 | async-start | bytes 786432 | tf_op jit(solution)/shard_map/all_to_all | solution.py:24
  191.0 3.1 %collective-permute-start.6 = (bf16[48,256]{1,0:T(8,128)(2,1)S(1)}, bf16[48,256]{1,0:T(8,128)(2,1)S(1)}, u32[]{:S(2)}, u32[]{:S(2)}) collective-permute-start(bf16[48,256]{1,0:T(8,128)(2,1)S(1)} %slice.85), channel_id=1, source_target_pairs={{0,16},{16,0},{1,17},{17,1},{2,18},{18,2},{3,19},{19,3},{4,20},{20... | collective-permute-start | bytes 73736 | tf_op jit(solution)/shard_map/ppermute | solution.py:96
Sparse Core Ops, SparseCore 0:
  20.4 66.5 all-gather.3
  89.1 29.3 all-gather.5

commit v9 on v8

--- a/solution.py
+++ b/solution.py
@@ -52,6 +52,27 @@
         ),
         name="deal_halves",
     )(rows)
+
+
+def turned(parts, place):
+    count = len(parts)
+
+    def turn(place_ref, *refs):
+        for back, part_ref in enumerate(refs[:-1]):
+            refs[-1][lax.rem(place_ref[0] + (count - back), count)] = part_ref[...]
+
+    vmem = pl.BlockSpec(memory_space=pltpu.VMEM)
+    return pl.pallas_call(
+        turn,
+        out_shape=jax.ShapeDtypeStruct((count,) + parts[0].shape, parts[0].dtype),
+        in_specs=[pl.BlockSpec(memory_space=pltpu.SMEM)] + [vmem] * count,
+        out_specs=vmem,
+        compiler_params=pltpu.CompilerParams(vmem_limit_bytes=4 * 1024 * 1024),
+        cost_estimate=pl.CostEstimate(
+            flops=0, bytes_accessed=4 * count * parts[0].size, transcendentals=0
+        ),
+        name="turn_parts",
+    )(place.reshape(1), *parts)
 
 
 def projected(rows, weight):
@@ -109,9 +130,8 @@
     kept_weight = by_index(section, parts[0], parts[1])
     got_weight = lax.ppermute(by_index(section, parts[1], parts[0]), "section", SWAP)
     gathered_tokens = lax.all_gather(after(pair, got_weight), "tp", axis=0, tiled=True)
-    both_parts = by_index(
-        section, jnp.stack([kept_weight, got_weight]), jnp.stack([got_weight, kept_weight])
-    )
+    first_part = by_index(section, kept_weight, got_weight)
+    second_part = by_index(section, got_weight, kept_weight)
 
     positions = hidden.shape[1]
     by_parity = after(hidden, pair).reshape(chips, cores, positions, -1)
@@ -123,11 +143,17 @@
         [o_weight[0], to_other_core(after(o_weight, pair)[0])], axis=1
     )
 
-    by_far = gathered(both_parts, "far")
-    first_weight = gathered(gathered(by_far[:, 0], "row"), "core").reshape(-1, columns)
-    state, query_weight, first_weight = lax.optimization_barrier(
-        (state, query_weight, first_weight)
-    )
+    by_far = gathered(first_part, "far")
+    first_weight = gathered(gathered(by_far, "row"), "core").reshape(-1, columns)
+    early_part = after(second_part, by_far)
+    second_parts = [second_part] + [
+        lax.ppermute(early_part, "far", [(far, (far + step) % fars) for far in range(fars)])
+        for step in range(1, fars)
+    ]
+    state, query_weight, first_weight, second_parts = lax.optimization_barrier(
+        (state, query_weight, first_weight, second_parts)
+    )
+    second_by_far = turned(second_parts, lax.axis_index("far").astype(jnp.int32))
     first_query, output_weight, gathered_tokens = lax.optimization_barrier(
         (to_query(state, query_weight), output_weight, gathered_tokens)
     )
@@ -147,7 +173,7 @@
     first_partial, given = projected(gathered_tokens, first_weight)
     first_keys, first_values = cache(first_partial + handed(given, (1, 0)))
     second_weight = lax.all_gather(
-        after(by_far[:, 1], gathered_tokens), ("core", "row"), axis=0, tiled=False
+        after(second_by_far, gathered_tokens), ("core", "row"), axis=0, tiled=False
     ).reshape(-1, columns)
     first_sum = attend(
         first_query,

time: 213 us -> 220 us (1.033)
  starting transfers between devices: 62.4 us -> 77.4 us
  blocking collectives: 61.4 us -> 48.2 us
  waiting for transfers between devices: 45.6 us -> 49.1 us
    all_to_all x4 -> x3, blocking collectives: 61.4 us -> 48.2 us  [exchange(): return lax.all_to_all(blocks, axis, 0, 0, tiled=True)]
    ppermute x0 -> x3, starting transfers between devices: none -> 10.7 us  [body(): lax.ppermute(early_part, 'far', [(far, (far + step) % fars) for far in ra...]
    all_to_all x7 -> x8, starting transfers between devices: 43.5 us -> 47 us  [exchange(): return lax.all_to_all(blocks, axis, 0, 0, tiled=True)]
    all_gather x1, waiting for transfers between devices: 0.02 us -> 3.16 us  [body(): lax.all_gather(after(second_by_far, gathered_tokens), ('core', 'row'), ax...]
    all_to_all x7 -> x8, waiting for transfers between devices: 35.4 us -> 36.1 us  [exchange(): return lax.all_to_all(blocks, axis, 0, 0, tiled=True)]
  transfers between devices with their start and end apart: 16 -> 20, of which waited for: 9 -> 10; matrix products, arithmetic and copies ran while one was open for 9% -> 9% of each run, Pallas kernels for 0% -> 0%
where the time goes in v9:
time: 220 us; the launch traced here: 218 us
  starting transfers between devices  77.4 us (35%)
  waiting for transfers between devices  49.1 us (22%)
  blocking collectives  48.2 us (22%)
  between operations  15.9 us (7%)
  matrix products  11.3 us (5%)
  local copies, waits for them, and re-layouts  10.9 us (5%)
  other arithmetic  3.53 us (2%)
    all_to_all x3, blocking collectives, exchange(): return lax.all_to_all(blocks, axis, 0, 0, tiled=True)  48.2 us
    all_to_all x8, starting transfers between devices, exchange(): return lax.all_to_all(blocks, axis, 0, 0, tiled=True)  47 us
    all_to_all x8, waiting for transfers between devices, exchange(): return lax.all_to_all(blocks, axis, 0, 0, tiled=True)  36.1 us
    ppermute x4, starting transfers between devices, to_other_core(): return lax.ppermute(block, 'core', SWAP)  12.1 us
    ppermute x3, starting transfers between devices, body(): lax.ppermute(early_part, 'far', [(far, (far + step) % fars) for far in ra...  10.7 us
    dot_general x2, matrix products, projected(): product = jnp.dot(rows, weight, preferred_element_type=F32)  8.96 us
    ppermute x2, waiting for transfers between devices, handed(): return lax.ppermute(partial_sum, 'section', [direction]).astype(F32)  6.16 us
  transfers between devices with their start and end apart: 20, of which 10 were waited for; matrix products, arithmetic and copies ran while one was open for 9% of the time, Pallas kernels for 0%

profile of v9, /device:TPU:1, one launch (start us, length us, event | category | flops | bytes accessed | tf_op | source)
XLA Modules:
  0.0 218.1 jit_solution(1524395873598054837)
XLA Ops:
  9.1 3.5 %all-to-all-start = ((bf16[2,32,4096]{2,1,0:T(8,128)(2,1)}), bf16[2,32,4096]{2,1,0:T(8,128)(2,1)S(1)}, u32[]{:S(2)}, u32[]{:S(2)}) async-start(bf16[2,32,4096]{2,1,0:T(8,128)(2,1)} %deal_halves.1), calls=%async_computation | async-start | bytes 1048576 | tf_op jit(solution)/shard_map/all_to_all | solution.py:24
  12.7 4.0 %collective-permute-start.2 = (bf16[128,256]{1,0:T(8,128)(2,1)S(1)}, bf16[128,256]{1,0:T(8,128)(2,1)S(1)}, u32[]{:S(2)}, u32[]{:S(2)}) collective-permute-start(bf16[128,256]{1,0:T(8,128)(2,1)S(1)} %select_bitcast_fusion), channel_id=1, source_target_pairs={{0,8},{8,0},{1,9},{9,1},{2,10},{10,2},{3,11},{11,3},{4,12},{12,4},... | collective-permute-start | bytes 196616 | tf_op jit(solution)/shard_map/ppermute | solution.py:131
  16.7 2.7 %collective-permute-done.2 = bf16[128,256]{1,0:T(8,128)(2,1)S(1)} collective-permute-done((bf16[128,256]{1,0:T(8,128)(2,1)S(1)}, bf16[128,256]{1,0:T(8,128)(2,1)S(1)}, u32[]{:S(2)}, u32[]{:S(2)}) %collective-permute-start.2) | collective-permute-done | bytes 65568 | tf_op jit(solution)/shard_map/ppermute | solution.py:131
  20.3 18.5 %all_to_all.55 = bf16[4,128,256]{2,1,0:T(8,128)(2,1)S(1)} all-to-all(bf16[4,128,256]{2,1,0:T(8,128)(2,1)S(1)} %broadcast_in_dim.34), channel_id=1, replica_groups=mesh['far'=4,'row'=4,'core'=2,'section'=2,'tp'=8] {'far'}, dimensions={0} | all-to-all | bytes 524288 | tf_op jit(solution)/shard_map/all_to_all | solution.py:24
  40.0 4.0 %all-to-all-start.2 = ((bf16[4,4,128,256]{3,2,1,0:T(8,128)(2,1)}), bf16[4,4,128,256]{3,2,1,0:T(8,128)(2,1)S(1)}, u32[]{:S(2)}, u32[]{:S(2)}) async-start(bf16[4,4,128,256]{3,2,1,0:T(8,128)(2,1)} %broadcast_in_dim.35), calls=%async_computation.2 | async-start | bytes 2097152 | tf_op jit(solution)/shard_map/all_to_all | solution.py:24
  44.0 4.9 %collective-permute-start.1 = (bf16[256,1024]{1,0:T(8,128)(2,1)S(1)}, bf16[256,1024]{1,0:T(8,128)(2,1)}, u32[]{:S(2)}, u32[]{:S(2)}) collective-permute-start(bf16[256,1024]{1,0:T(8,128)(2,1)S(1)} %bitcast.65), channel_id=1, source_target_pairs={{0,16},{16,0},{1,17},{17,1},{2,18},{18,2},{3,19},{19,3},{4,20},{20... | collective-permute-start | bytes 1572872 | tf_op jit(solution)/shard_map/ppermute | solution.py:117
  49.2 1.9 collective-permute-start
  51.1 3.3 %collective-permute-start.3 = (bf16[128,256]{1,0:T(8,128)(2,1)S(1)}, bf16[128,256]{1,0:T(8,128)(2,1)S(1)}, u32[]{:S(2)}, u32[]{:S(2)}) collective-permute-start(bf16[128,256]{1,0:T(8,128)(2,1)S(1)} %get-tuple-element.35.refs_0_), channel_id=1, source_target_pairs={{0,128},{128,256},{256,384},{384,0},{1,129},{129,257},{257,385},{3... | collective-permute-start | bytes 196616 | tf_op jit(solution)/shard_map/ppermute | solution.py:150
  54.4 3.2 %collective-permute-start.4 = (bf16[128,256]{1,0:T(8,128)(2,1)S(1)}, bf16[128,256]{1,0:T(8,128)(2,1)S(1)}, u32[]{:S(2)}, u32[]{:S(2)}) collective-permute-start(bf16[128,256]{1,0:T(8,128)(2,1)S(1)} %get-tuple-element.35.refs_0_), channel_id=1, source_target_pairs={{0,256},{128,384},{256,0},{384,128},{1,257},{129,385},{257,1},{385... | collective-permute-start | bytes 196616 | tf_op jit(solution)/shard_map/ppermute | solution.py:150
  57.7 4.2 %collective-permute-start.5 = (bf16[128,256]{1,0:T(8,128)(2,1)S(1)}, bf16[128,256]{1,0:T(8,128)(2,1)S(1)}, u32[]{:S(2)}, u32[]{:S(2)}) collective-permute-start(bf16[128,256]{1,0:T(8,128)(2,1)S(1)} %get-tuple-element.35.refs_0_), channel_id=1, source_target_pairs={{0,384},{128,0},{256,128},{384,256},{1,385},{129,1},{257,129},{385... | collective-permute-start | bytes 196616 | tf_op jit(solution)/shard_map/ppermute | solution.py:150
  61.9 3.2 %collective-permute-start.6 = (bf16[1024,256]{1,0:T(8,128)(2,1)S(1)}, bf16[1024,256]{1,0:T(8,128)(2,1)}, u32[]{:S(2)}, u32[]{:S(2)}) collective-permute-start(bf16[1024,256]{1,0:T(8,128)(2,1)S(1)} %bitcast.67), channel_id=1, source_target_pairs={{0,16},{16,0},{1,17},{17,1},{2,18},{18,2},{3,19},{19,3},{4,20},{20... | collective-permute-start | bytes 1572872 | tf_op jit(solution)/shard_map/ppermute | solution.py:117
  66.3 1.7 broadcast_in_dim.36
  67.9 4.8 %all-to-all-start.3 = ((bf16[2,4,4,128,256]{4,3,2,1,0:T(8,128)(2,1)}), bf16[2,4,4,128,256]{4,3,2,1,0:T(8,128)(2,1)}, u32[]{:S(2)}, u32[]{:S(2)}) async-start(bf16[2,4,4,128,256]{4,3,2,1,0:T(8,128)(2,1)} %broadcast_in_dim.36), calls=%async_computation.3 | async-start | bytes 4194304 | tf_op jit(solution)/shard_map/all_to_all | solution.py:24
  72.8 2.6 %all-to-all-done.3 = bf16[2,4,4,128,256]{4,3,2,1,0:T(8,128)(2,1)} async-done(((bf16[2,4,4,128,256]{4,3,2,1,0:T(8,128)(2,1)}), bf16[2,4,4,128,256]{4,3,2,1,0:T(8,128)(2,1)}, u32[]{:S(2)}, u32[]{:S(2)}) %all-to-all-start.3) | async-done | bytes 2097184 | tf_op jit(solution)/shard_map/all_to_all | solution.py:24
  76.4 8.3 %all-to-all-start.4 = ((bf16[16,3,1024]{2,1,0:T(4,128)(2,1)}), bf16[16,3,1024]{2,1,0:T(4,128)(2,1)S(1)}, u32[]{:S(2)}, u32[]{:S(2)}) async-start(bf16[16,3,1024]{2,1,0:T(4,128)(2,1)} %reshape.228), calls=%async_computation.4 | async-start | bytes 262144 | tf_op jit(solution)/shard_map/all_to_all | solution.py:24
  86.7 7.5 %all-to-all-done.4 = bf16[16,3,1024]{2,1,0:T(4,128)(2,1)S(1)} async-done(((bf16[16,3,1024]{2,1,0:T(4,128)(2,1)}), bf16[16,3,1024]{2,1,0:T(4,128)(2,1)S(1)}, u32[]{:S(2)}, u32[]{:S(2)}) %all-to-all-start.4) | async-done | bytes 98336 | tf_op jit(solution)/shard_map/all_to_all | solution.py:24
  95.0 4.1 %fusion.36 = (bf16[512,256]{1,0:T(8,128)(2,1)S(1)}, f32[512,256]{1,0:T(8,128)S(1)}) fusion(bf16[512,4096]{1,0:T(8,128)(2,1)} %all-gather.4.cloned.1.call-done, bf16[4096,256]{1,0:T(8,128)(2,1)} %bitcast.6), kind=kOutput, calls=%fused_computation.95 | convolution fusion | flops 1073872896 | bytes 7077888 | tf_op jit(solution)/shard_map/dot_general | solution.py:79
  100.6 6.2 %collective-permute-done.7 = bf16[512,256]{1,0:T(8,128)(2,1)S(1)} collective-permute-done((bf16[512,256]{1,0:T(8,128)(2,1)S(1)}, bf16[512,256]{1,0:T(8,128)(2,1)S(1)}, u32[]{:S(2)}, u32[]{:S(2)}) %collective-permute-start.7) | collective-permute-done | bytes 262176 | tf_op jit(solution)/shard_map/ppermute | solution.py:162
  108.2 5.2 %all-to-all-start.5 = ((bf16[16,3,1024]{2,1,0:T(4,128)(2,1)}), bf16[16,3,1024]{2,1,0:T(4,128)(2,1)S(1)}, u32[]{:S(2)}, u32[]{:S(2)}) async-start(bf16[16,3,1024]{2,1,0:T(4,128)(2,1)} %broadcast_in_dim.40), calls=%async_computation.5 | async-start | bytes 262144 | tf_op jit(solution)/shard_map/all_to_all | solution.py:24
  114.1 8.6 %all-to-all-done.5 = bf16[16,3,1024]{2,1,0:T(4,128)(2,1)S(1)} async-done(((bf16[16,3,1024]{2,1,0:T(4,128)(2,1)}), bf16[16,3,1024]{2,1,0:T(4,128)(2,1)S(1)}, u32[]{:S(2)}, u32[]{:S(2)}) %all-to-all-start.5) | async-done | bytes 98336 | tf_op jit(solution)/shard_map/all_to_all | solution.py:24
  123.1 3.2 %all-gather.6.cloned.1.call-done = bf16[32,128,256]{2,1,0:T(8,128)(2,1)} async-done(((bf16[4,128,256]{2,1,0:T(8,128)(2,1)}), bf16[32,128,256]{2,1,0:T(8,128)(2,1)}) %all-gather.6.cloned.1.call-update) | async-done | bytes 2097168 | tf_op jit(solution)/shard_map/all_gather | solution.py:175
  126.3 13.9 %all_to_all.56 = bf16[8,12,256]{2,1,0:T(8,128)(2,1)S(1)} all-to-all(bf16[8,12,256]{2,1,0:T(8,128)(2,1)S(1)} %reshape.233), channel_id=1, replica_groups=mesh['far'=4,'row'=4,'core'=2,'section'=2,'tp'=8] {'tp'}, dimensions={0} | all-to-all | bytes 98304 | tf_op jit(solution)/shard_map/all_to_all | solution.py:24
  140.9 3.5 %all-to-all-start.7 = ((bf16[16,12,256]{2,1,0:T(8,128)(2,1)}), bf16[16,12,256]{2,1,0:T(8,128)(2,1)S(1)}, u32[]{:S(2)}, u32[]{:S(2)}) async-start(bf16[16,12,256]{2,1,0:T(8,128)(2,1)} %broadcast_in_dim.41), calls=%async_computation.7 | async-start | bytes 262144 | tf_op jit(solution)/shard_map/all_to_all | solution.py:24
  144.4 4.8 %fusion.38 = (bf16[512,256]{1,0:T(8,128)(2,1)}, f32[512,256]{1,0:T(8,128)S(1)}) fusion(bf16[512,4096]{1,0:T(8,128)(2,1)} %all-gather.4.cloned.1.call-done, bf16[4096,256]{1,0:T(8,128)(2,1)} %bitcast.72), kind=kOutput, calls=%fused_computation.97 | convolution fusion | flops 1073872896 | bytes 7077888 | tf_op jit(solution)/shard_map/dot_general | solution.py:79
  149.2 2.5 %all-to-all-done.7 = bf16[16,12,256]{2,1,0:T(8,128)(2,1)S(1)} async-done(((bf16[16,12,256]{2,1,0:T(8,128)(2,1)}), bf16[16,12,256]{2,1,0:T(8,128)(2,1)S(1)}, u32[]{:S(2)}, u32[]{:S(2)}) %all-to-all-start.7) | async-done | bytes 98336 | tf_op jit(solution)/shard_map/all_to_all | solution.py:24
  152.9 8.2 %all-to-all-start.8 = ((bf16[16,3,1024]{2,1,0:T(4,128)(2,1)}), bf16[16,3,1024]{2,1,0:T(4,128)(2,1)S(1)}, u32[]{:S(2)}, u32[]{:S(2)}) async-start(bf16[16,3,1024]{2,1,0:T(4,128)(2,1)} %reshape.238), calls=%async_computation.8 | async-start | bytes 262144 | tf_op jit(solution)/shard_map/all_to_all | solution.py:24
  161.1 2.2 %collective-permute-start.8 = (bf16[512,256]{1,0:T(8,128)(2,1)}, bf16[512,256]{1,0:T(8,128)(2,1)S(1)}, u32[]{:S(2)}, u32[]{:S(2)}) collective-permute-start(bf16[512,256]{1,0:T(8,128)(2,1)} %get-tuple-element.42), channel_id=1, source_target_pairs={{0,8},{1,9},{2,10},{3,11},{4,12},{5,13},{6,14},{7,15},{16,24},{17,... | collective-permute-start | bytes 786440 | tf_op jit(solution)/shard_map/ppermute | solution.py:162
  163.3 7.1 %all-to-all-done.8 = bf16[16,3,1024]{2,1,0:T(4,128)(2,1)S(1)} async-done(((bf16[16,3,1024]{2,1,0:T(4,128)(2,1)}), bf16[16,3,1024]{2,1,0:T(4,128)(2,1)S(1)}, u32[]{:S(2)}, u32[]{:S(2)}) %all-to-all-start.8) | async-done | bytes 98336 | tf_op jit(solution)/shard_map/all_to_all | solution.py:24
  171.5 15.8 %all_to_all.57 = bf16[16,3,1024]{2,1,0:T(4,128)(2,1)S(1)} all-to-all(bf16[16,3,1024]{2,1,0:T(4,128)(2,1)S(1)} %broadcast_in_dim.43), channel_id=1, replica_groups=mesh['far'=4,'row'=4,'core'=2,'section'=2,'tp'=8] {'far','row'}, dimensions={0} | all-to-all | bytes 196608 | tf_op jit(solution)/shard_map/all_to_all | solution.py:24
  188.5 9.5 %all-to-all-start.10 = ((bf16[16,48,256]{2,1,0:T(8,128)(2,1)}), bf16[16,48,256]{2,1,0:T(8,128)(2,1)S(1)}, u32[]{:S(2)}, u32[]{:S(2)}) async-start(bf16[16,48,256]{2,1,0:T(8,128)(2,1)} %bitcast.23), calls=%async_computation.10 | async-start | bytes 786432 | tf_op jit(solution)/shard_map/all_to_all | solution.py:24
  197.9 2.0 collective-permute-start.9
  202.6 7.8 %all-to-all-done.10 = bf16[16,48,256]{2,1,0:T(8,128)(2,1)S(1)} async-done(((bf16[16,48,256]{2,1,0:T(8,128)(2,1)}), bf16[16,48,256]{2,1,0:T(8,128)(2,1)S(1)}, u32[]{:S(2)}, u32[]{:S(2)}) %all-to-all-start.10) | async-done | bytes 393248 | tf_op jit(solution)/shard_map/all_to_all | solution.py:24
  (103 shorter events, 19.3 us)
Async XLA Ops:
  7.2 1.0 copy-start
  8.2 4.5 %copy-start.2 = (bf16[1,256,1,256]{3,1,2,0:T(8,128)(2,1)S(1)}, bf16[1,256,1,256]{3,1,2,0:T(8,128)(2,1)}, u32[]{:S(2)}) copy-start(bf16[1,256,1,256]{3,1,2,0:T(8,128)(2,1)} %param.12) | copy-start | bytes 393220
  9.1 10.3 %all-to-all-start = ((bf16[2,32,4096]{2,1,0:T(8,128)(2,1)}), bf16[2,32,4096]{2,1,0:T(8,128)(2,1)S(1)}, u32[]{:S(2)}, u32[]{:S(2)}) async-start(bf16[2,32,4096]{2,1,0:T(8,128)(2,1)} %deal_halves.1), calls=%async_computation | async-start | bytes 1048576 | tf_op jit(solution)/shard_map/all_to_all | solution.py:24
  12.6 81.7 %all-gather.4.cloned.1.call-start = ((), (), s32[]{:S(2)}) async-start(), calls=%async_computation.11 | async-start | bytes 4718592 | tf_op jit(solution)/shard_map/all_gather | solution.py:132
  12.7 6.7 %collective-permute-start.2 = (bf16[128,256]{1,0:T(8,128)(2,1)S(1)}, bf16[128,256]{1,0:T(8,128)(2,1)S(1)}, u32[]{:S(2)}, u32[]{:S(2)}) collective-permute-start(bf16[128,256]{1,0:T(8,128)(2,1)S(1)} %select_bitcast_fusion), channel_id=1, source_target_pairs={{0,8},{8,0},{1,9},{9,1},{2,10},{10,2},{3,11},{11,3},{4,12},{12,4},... | collective-permute-start | bytes 196616 | tf_op jit(solution)/shard_map/ppermute | solution.py:131
  19.4 0.9 copy-start.1
  20.3 23.7 %copy-start.5 = (bf16[32,3,256]{2,0,1:T(8,128)(2,1)S(1)}, bf16[32,3,256]{2,0,1:T(8,128)(2,1)}, u32[]{:S(2)}) copy-start(bf16[32,3,256]{2,0,1:T(8,128)(2,1)} %param.9) | copy-start | bytes 147460
  20.3 23.7 %copy-start.3 = (bf16[1,256,1024]{2,1,0:T(8,128)(2,1)S(1)}, bf16[1,256,1024]{2,1,0:T(8,128)(2,1)}, u32[]{:S(2)}) copy-start(bf16[1,256,1024]{2,1,0:T(8,128)(2,1)} %param.14) | copy-start | bytes 1572868
  38.9 23.0 %copy-start.4 = (bf16[1,1024,256]{2,1,0:T(8,128)(2,1)S(1)}, bf16[1,1024,256]{2,1,0:T(8,128)(2,1)}, u32[]{:S(2)}) copy-start(bf16[1,1024,256]{2,1,0:T(8,128)(2,1)} %param.16) | copy-start | bytes 1572868
  40.0 26.3 %all-to-all-start.2 = ((bf16[4,4,128,256]{3,2,1,0:T(8,128)(2,1)}), bf16[4,4,128,256]{3,2,1,0:T(8,128)(2,1)S(1)}, u32[]{:S(2)}, u32[]{:S(2)}) async-start(bf16[4,4,128,256]{3,2,1,0:T(8,128)(2,1)} %broadcast_in_dim.35), calls=%async_computation.2 | async-start | bytes 2097152 | tf_op jit(solution)/shard_map/all_to_all | solution.py:24
  44.0 21.1 %collective-permute-start.1 = (bf16[256,1024]{1,0:T(8,128)(2,1)S(1)}, bf16[256,1024]{1,0:T(8,128)(2,1)}, u32[]{:S(2)}, u32[]{:S(2)}) collective-permute-start(bf16[256,1024]{1,0:T(8,128)(2,1)S(1)} %bitcast.65), channel_id=1, source_target_pairs={{0,16},{16,0},{1,17},{17,1},{2,18},{18,2},{3,19},{19,3},{4,20},{20... | collective-permute-start | bytes 1572872 | tf_op jit(solution)/shard_map/ppermute | solution.py:117
  49.2 12.7 %collective-permute-start = (bf16[48,256]{1,0:T(8,128)(2,1)S(1)}, bf16[48,256]{1,0:T(8,128)(2,1)S(1)}, u32[]{:S(2)}, u32[]{:S(2)}) collective-permute-start(bf16[48,256]{1,0:T(8,128)(2,1)S(1)} %select_n.133), channel_id=1, source_target_pairs={{0,16},{16,0},{1,17},{17,1},{2,18},{18,2},{3,19},{19,3},{4,20},{20... | collective-permute-start | bytes 73736 | tf_op jit(solution)/shard_map/ppermute | solution.py:117
  51.1 21.7 %collective-permute-start.3 = (bf16[128,256]{1,0:T(8,128)(2,1)S(1)}, bf16[128,256]{1,0:T(8,128)(2,1)S(1)}, u32[]{:S(2)}, u32[]{:S(2)}) collective-permute-start(bf16[128,256]{1,0:T(8,128)(2,1)S(1)} %get-tuple-element.35.refs_0_), channel_id=1, source_target_pairs={{0,128},{128,256},{256,384},{384,0},{1,129},{129,257},{257,385},{3... | collective-permute-start | bytes 196616 | tf_op jit(solution)/shard_map/ppermute | solution.py:150
  54.4 18.4 %collective-permute-start.4 = (bf16[128,256]{1,0:T(8,128)(2,1)S(1)}, bf16[128,256]{1,0:T(8,128)(2,1)S(1)}, u32[]{:S(2)}, u32[]{:S(2)}) collective-permute-start(bf16[128,256]{1,0:T(8,128)(2,1)S(1)} %get-tuple-element.35.refs_0_), channel_id=1, source_target_pairs={{0,256},{128,384},{256,0},{384,128},{1,257},{129,385},{257,1},{385... | collective-permute-start | bytes 196616 | tf_op jit(solution)/shard_map/ppermute | solution.py:150
  57.7 15.1 %collective-permute-start.5 = (bf16[128,256]{1,0:T(8,128)(2,1)S(1)}, bf16[128,256]{1,0:T(8,128)(2,1)S(1)}, u32[]{:S(2)}, u32[]{:S(2)}) collective-permute-start(bf16[128,256]{1,0:T(8,128)(2,1)S(1)} %get-tuple-element.35.refs_0_), channel_id=1, source_target_pairs={{0,384},{128,0},{256,128},{384,256},{1,385},{129,1},{257,129},{385... | collective-permute-start | bytes 196616 | tf_op jit(solution)/shard_map/ppermute | solution.py:150
  61.9 23.0 %collective-permute-start.6 = (bf16[1024,256]{1,0:T(8,128)(2,1)S(1)}, bf16[1024,256]{1,0:T(8,128)(2,1)}, u32[]{:S(2)}, u32[]{:S(2)}) collective-permute-start(bf16[1024,256]{1,0:T(8,128)(2,1)S(1)} %bitcast.67), channel_id=1, source_target_pairs={{0,16},{16,0},{1,17},{17,1},{2,18},{18,2},{3,19},{19,3},{4,20},{20... | collective-permute-start | bytes 1572872 | tf_op jit(solution)/shard_map/ppermute | solution.py:117
  67.9 7.5 %all-to-all-start.3 = ((bf16[2,4,4,128,256]{4,3,2,1,0:T(8,128)(2,1)}), bf16[2,4,4,128,256]{4,3,2,1,0:T(8,128)(2,1)}, u32[]{:S(2)}, u32[]{:S(2)}) async-start(bf16[2,4,4,128,256]{4,3,2,1,0:T(8,128)(2,1)} %broadcast_in_dim.36), calls=%async_computation.3 | async-start | bytes 4194304 | tf_op jit(solution)/shard_map/all_to_all | solution.py:24
  75.4 19.6 %copy-start.6 = (bf16[1,128]{1,0:T(2,128)(2,1)S(1)}, bf16[1,128]{1,0:T(2,128)(2,1)}, u32[]{:S(2)}) copy-start(bf16[1,128]{1,0:T(2,128)(2,1)} %param.15) | copy-start | bytes 772
  75.4 19.6 %copy-start.7 = (bf16[1,128]{1,0:T(2,128)(2,1)S(1)}, bf16[1,128]{1,0:T(2,128)(2,1)}, u32[]{:S(2)}) copy-start(bf16[1,128]{1,0:T(2,128)(2,1)} %param.13) | copy-start | bytes 772
  76.4 17.7 %all-to-all-start.4 = ((bf16[16,3,1024]{2,1,0:T(4,128)(2,1)}), bf16[16,3,1024]{2,1,0:T(4,128)(2,1)S(1)}, u32[]{:S(2)}, u32[]{:S(2)}) async-start(bf16[16,3,1024]{2,1,0:T(4,128)(2,1)} %reshape.228), calls=%async_computation.4 | async-start | bytes 262144 | tf_op jit(solution)/shard_map/all_to_all | solution.py:24
  84.8 41.4 %all-gather.6.cloned.1.call-start = ((), (), s32[]{:S(2)}) async-start(), calls=%async_computation.12 | async-start | bytes 2359296 | tf_op jit(solution)/shard_map/all_gather | solution.py:175
  99.1 7.6 %collective-permute-start.7 = (bf16[512,256]{1,0:T(8,128)(2,1)S(1)}, bf16[512,256]{1,0:T(8,128)(2,1)S(1)}, u32[]{:S(2)}, u32[]{:S(2)}) collective-permute-start(bf16[512,256]{1,0:T(8,128)(2,1)S(1)} %get-tuple-element.59), channel_id=1, source_target_pairs={{8,0},{9,1},{10,2},{11,3},{12,4},{13,5},{14,6},{15,7},{24,16},{25,... | collective-permute-start | bytes 786440 | tf_op jit(solution)/shard_map/ppermute | solution.py:162
  108.2 14.4 %all-to-all-start.5 = ((bf16[16,3,1024]{2,1,0:T(4,128)(2,1)}), bf16[16,3,1024]{2,1,0:T(4,128)(2,1)S(1)}, u32[]{:S(2)}, u32[]{:S(2)}) async-start(bf16[16,3,1024]{2,1,0:T(4,128)(2,1)} %broadcast_in_dim.40), calls=%async_computation.5 | async-start | bytes 262144 | tf_op jit(solution)/shard_map/all_to_all | solution.py:24
  140.9 10.9 %all-to-all-start.7 = ((bf16[16,12,256]{2,1,0:T(8,128)(2,1)}), bf16[16,12,256]{2,1,0:T(8,128)(2,1)S(1)}, u32[]{:S(2)}, u32[]{:S(2)}) async-start(bf16[16,12,256]{2,1,0:T(8,128)(2,1)} %broadcast_in_dim.41), calls=%async_computation.7 | async-start | bytes 262144 | tf_op jit(solution)/shard_map/all_to_all | solution.py:24
  152.9 17.5 %all-to-all-start.8 = ((bf16[16,3,1024]{2,1,0:T(4,128)(2,1)}), bf16[16,3,1024]{2,1,0:T(4,128)(2,1)S(1)}, u32[]{:S(2)}, u32[]{:S(2)}) async-start(bf16[16,3,1024]{2,1,0:T(4,128)(2,1)} %reshape.238), calls=%async_computation.8 | async-start | bytes 262144 | tf_op jit(solution)/shard_map/all_to_all | solution.py:24
  161.1 9.6 %collective-permute-start.8 = (bf16[512,256]{1,0:T(8,128)(2,1)}, bf16[512,256]{1,0:T(8,128)(2,1)S(1)}, u32[]{:S(2)}, u32[]{:S(2)}) collective-permute-start(bf16[512,256]{1,0:T(8,128)(2,1)} %get-tuple-element.42), channel_id=1, source_target_pairs={{0,8},{1,9},{2,10},{3,11},{4,12},{5,13},{6,14},{7,15},{16,24},{17,... | collective-permute-start | bytes 786440 | tf_op jit(solution)/shard_map/ppermute | solution.py:162
  188.5 21.9 %all-to-all-start.10 = ((bf16[16,48,256]{2,1,0:T(8,128)(2,1)}), bf16[16,48,256]{2,1,0:T(8,128)(2,1)S(1)}, u32[]{:S(2)}, u32[]{:S(2)}) async-start(bf16[16,48,256]{2,1,0:T(8,128)(2,1)} %bitcast.23), calls=%async_computation.10 | async-start | bytes 786432 | tf_op jit(solution)/shard_map/all_to_all | solution.py:24
  197.9 3.1 %collective-permute-start.9 = (bf16[48,256]{1,0:T(8,128)(2,1)S(1)}, bf16[48,256]{1,0:T(8,128)(2,1)S(1)}, u32[]{:S(2)}, u32[]{:S(2)}) collective-permute-start(bf16[48,256]{1,0:T(8,128)(2,1)S(1)} %slice.77), channel_id=1, source_target_pairs={{0,16},{16,0},{1,17},{17,1},{2,18},{18,2},{3,19},{19,3},{4,20},{20... | collective-permute-start | bytes 73736 | tf_op jit(solution)/shard_map/ppermute | solution.py:117
Sparse Core Ops, SparseCore 0:
  20.4 66.5 all-gather.3
  94.4 31.7 all-gather.5

commit v10 on v9

--- a/solution.py
+++ b/solution.py
@@ -145,13 +145,13 @@
 
     by_far = gathered(first_part, "far")
     first_weight = gathered(gathered(by_far, "row"), "core").reshape(-1, columns)
-    early_part = after(second_part, by_far)
+    early_part = after(second_part, first_weight)
     second_parts = [second_part] + [
         lax.ppermute(early_part, "far", [(far, (far + step) % fars) for far in range(fars)])
         for step in range(1, fars)
     ]
-    state, query_weight, first_weight, second_parts = lax.optimization_barrier(
-        (state, query_weight, first_weight, second_parts)
+    state, query_weight, first_weight = lax.optimization_barrier(
+        (state, query_weight, first_weight)
     )
     second_by_far = turned(second_parts, lax.axis_index("far").astype(jnp.int32))
     first_query, output_weight, gathered_tokens = lax.optimization_barrier(
@@ -184,10 +184,10 @@
         output_weight,
         gate,
     )
-    first_sum, second_weight = lax.optimization_barrier((first_sum, second_weight))
     first_sum = jnp.concatenate([first_sum[:, :columns], first_sum[:, columns:]])
     first_sum = first_sum.reshape(tensor_count, -1, columns)
     summed = jnp.sum(exchange(first_sum, "tp").astype(F32), axis=0).astype(BF16)
+    summed, second_weight = lax.optimization_barrier((summed, second_weight))
     everywhere = gathered(summed, ("section", "tp"))[:tensor_count]
     everywhere = everywhere.reshape(2, chips * positions, -1).astype(F32)
     everywhere = jnp.concatenate([everywhere[0], everywhere[1]], axis=1)

time: 220 us -> 216 us (0.982)
  waiting for transfers between devices: 49.1 us -> 37 us
  blocking collectives: 48.2 us -> 60.2 us
  starting transfers between devices: 77.4 us -> 75.1 us
    all_to_all x3 -> x4, blocking collectives: 48.2 us -> 60.2 us  [exchange(): return lax.all_to_all(blocks, axis, 0, 0, tiled=True)]
    all_to_all x8 -> x7, waiting for transfers between devices: 36.1 us -> 27.1 us  [exchange(): return lax.all_to_all(blocks, axis, 0, 0, tiled=True)]
    all_to_all x8 -> x7, starting transfers between devices: 47 us -> 41.5 us  [exchange(): return lax.all_to_all(blocks, axis, 0, 0, tiled=True)]
    ppermute x3, starting transfers between devices: 10.7 us -> 14.6 us  [body(): lax.ppermute(early_part, 'far', [(far, (far + step) % fars) for far in ra...]
    all_gather x1, waiting for transfers between devices: 3.16 us -> 0.02 us  [body(): lax.all_gather(after(second_by_far, gathered_tokens), ('core', 'row'), ax...]
  transfers between devices with their start and end apart: 20 -> 19, of which waited for: 10 -> 9; matrix products, arithmetic and copies ran while one was open for 9% -> 8% of each run, Pallas kernels for 0% -> 0%
where the time goes in v10:
time: 216 us; the launch traced here: 214 us
  starting transfers between devices  75.1 us (35%)
  blocking collectives  60.2 us (28%)
  waiting for transfers between devices  37 us (17%)
  between operations  15.9 us (7%)
  matrix products  11.3 us (5%)
  local copies, waits for them, and re-layouts  9.44 us (4%)
  other arithmetic  3.54 us (2%)
    all_to_all x4, blocking collectives, exchange(): return lax.all_to_all(blocks, axis, 0, 0, tiled=True)  60.2 us
    all_to_all x7, starting transfers between devices, exchange(): return lax.all_to_all(blocks, axis, 0, 0, tiled=True)  41.5 us
    all_to_all x7, waiting for transfers between devices, exchange(): return lax.all_to_all(blocks, axis, 0, 0, tiled=True)  27.1 us
    ppermute x3, starting transfers between devices, body(): lax.ppermute(early_part, 'far', [(far, (far + step) % fars) for far in ra...  14.6 us
    ppermute x4, starting transfers between devices, to_other_core(): return lax.ppermute(block, 'core', SWAP)  11.3 us
    dot_general x2, matrix products, projected(): product = jnp.dot(rows, weight, preferred_element_type=F32)  8.96 us
    ppermute x2, waiting for transfers between devices, handed(): return lax.ppermute(partial_sum, 'section', [direction]).astype(F32)  5.68 us
  transfers between devices with their start and end apart: 19, of which 9 were waited for; matrix products, arithmetic and copies ran while one was open for 8% of the time, Pallas kernels for 0%

profile of v10, /device:TPU:1, one launch (start us, length us, event | category | flops | bytes accessed | tf_op | source)
XLA Modules:
  0.0 214.1 jit_solution(11794483747262834000)
XLA Ops:
  9.1 3.5 %all-to-all-start = ((bf16[2,32,4096]{2,1,0:T(8,128)(2,1)}), bf16[2,32,4096]{2,1,0:T(8,128)(2,1)S(1)}, u32[]{:S(2)}, u32[]{:S(2)}) async-start(bf16[2,32,4096]{2,1,0:T(8,128)(2,1)} %deal_halves.1), calls=%async_computation | async-start | bytes 1048576 | tf_op jit(solution)/shard_map/all_to_all | solution.py:24
  12.7 4.0 %collective-permute-start.2 = (bf16[128,256]{1,0:T(8,128)(2,1)S(1)}, bf16[128,256]{1,0:T(8,128)(2,1)S(1)}, u32[]{:S(2)}, u32[]{:S(2)}) collective-permute-start(bf16[128,256]{1,0:T(8,128)(2,1)S(1)} %select_bitcast_fusion), channel_id=1, source_target_pairs={{0,8},{8,0},{1,9},{9,1},{2,10},{10,2},{3,11},{11,3},{4,12},{12,4},... | collective-permute-start | bytes 196616 | tf_op jit(solution)/shard_map/ppermute | solution.py:131
  16.7 2.7 %collective-permute-done.2 = bf16[128,256]{1,0:T(8,128)(2,1)S(1)} collective-permute-done((bf16[128,256]{1,0:T(8,128)(2,1)S(1)}, bf16[128,256]{1,0:T(8,128)(2,1)S(1)}, u32[]{:S(2)}, u32[]{:S(2)}) %collective-permute-start.2) | collective-permute-done | bytes 65568 | tf_op jit(solution)/shard_map/ppermute | solution.py:131
  20.3 18.5 %all_to_all.55 = bf16[4,128,256]{2,1,0:T(8,128)(2,1)S(1)} all-to-all(bf16[4,128,256]{2,1,0:T(8,128)(2,1)S(1)} %broadcast_in_dim.34), channel_id=1, replica_groups=mesh['far'=4,'row'=4,'core'=2,'section'=2,'tp'=8] {'far'}, dimensions={0} | all-to-all | bytes 524288 | tf_op jit(solution)/shard_map/all_to_all | solution.py:24
  39.9 4.0 %all-to-all-start.2 = ((bf16[4,4,128,256]{3,2,1,0:T(8,128)(2,1)}), bf16[4,4,128,256]{3,2,1,0:T(8,128)(2,1)S(1)}, u32[]{:S(2)}, u32[]{:S(2)}) async-start(bf16[4,4,128,256]{3,2,1,0:T(8,128)(2,1)} %broadcast_in_dim.35), calls=%async_computation.2 | async-start | bytes 2097152 | tf_op jit(solution)/shard_map/all_to_all | solution.py:24
  44.0 4.9 %collective-permute-start.1 = (bf16[256,1024]{1,0:T(8,128)(2,1)S(1)}, bf16[256,1024]{1,0:T(8,128)(2,1)}, u32[]{:S(2)}, u32[]{:S(2)}) collective-permute-start(bf16[256,1024]{1,0:T(8,128)(2,1)S(1)} %bitcast.66), channel_id=1, source_target_pairs={{0,16},{16,0},{1,17},{17,1},{2,18},{18,2},{3,19},{19,3},{4,20},{20... | collective-permute-start | bytes 1572872 | tf_op jit(solution)/shard_map/ppermute | solution.py:117
  49.1 1.9 collective-permute-start
  51.1 2.4 %collective-permute-start.3 = (bf16[1024,256]{1,0:T(8,128)(2,1)S(1)}, bf16[1024,256]{1,0:T(8,128)(2,1)}, u32[]{:S(2)}, u32[]{:S(2)}) collective-permute-start(bf16[1024,256]{1,0:T(8,128)(2,1)S(1)} %bitcast.68), channel_id=1, source_target_pairs={{0,16},{16,0},{1,17},{17,1},{2,18},{18,2},{3,19},{19,3},{4,20},{20... | collective-permute-start | bytes 1572872 | tf_op jit(solution)/shard_map/ppermute | solution.py:117
  53.5 1.1 pad_maximum_fusion
  54.7 1.1 all-to-all-done.2
  56.0 10.1 %all_to_all.56 = bf16[2,4,4,128,256]{4,3,2,1,0:T(8,128)(2,1)} all-to-all(bf16[2,4,4,128,256]{4,3,2,1,0:T(8,128)(2,1)S(1)} %broadcast_in_dim.36), channel_id=1, replica_groups=mesh['far'=4,'row'=4,'core'=2,'section'=2,'tp'=8] {'core'}, dimensions={0} | all-to-all | bytes 4194304 | tf_op jit(solution)/shard_map/all_to_all | solution.py:24
  67.2 4.1 %all-to-all-start.4 = ((bf16[16,3,1024]{2,1,0:T(4,128)(2,1)}), bf16[16,3,1024]{2,1,0:T(4,128)(2,1)S(1)}, u32[]{:S(2)}, u32[]{:S(2)}) async-start(bf16[16,3,1024]{2,1,0:T(4,128)(2,1)} %reshape.228), calls=%async_computation.4 | async-start | bytes 262144 | tf_op jit(solution)/shard_map/all_to_all | solution.py:24
  71.4 4.2 %collective-permute-start.5 = (bf16[128,256]{1,0:T(8,128)(2,1)S(1)}, bf16[128,256]{1,0:T(8,128)(2,1)S(1)}, u32[]{:S(2)}, u32[]{:S(2)}) collective-permute-start(bf16[128,256]{1,0:T(8,128)(2,1)S(1)} %get-tuple-element.30.refs_0_), channel_id=1, source_target_pairs={{0,128},{128,256},{256,384},{384,0},{1,129},{129,257},{257,385},{3... | collective-permute-start | bytes 196616 | tf_op jit(solution)/shard_map/ppermute | solution.py:150
  75.6 5.2 %collective-permute-start.6 = (bf16[128,256]{1,0:T(8,128)(2,1)S(1)}, bf16[128,256]{1,0:T(8,128)(2,1)S(1)}, u32[]{:S(2)}, u32[]{:S(2)}) collective-permute-start(bf16[128,256]{1,0:T(8,128)(2,1)S(1)} %get-tuple-element.30.refs_0_), channel_id=1, source_target_pairs={{0,256},{128,384},{256,0},{384,128},{1,257},{129,385},{257,1},{385... | collective-permute-start | bytes 196616 | tf_op jit(solution)/shard_map/ppermute | solution.py:150
  80.8 5.2 %collective-permute-start.7 = (bf16[128,256]{1,0:T(8,128)(2,1)S(1)}, bf16[128,256]{1,0:T(8,128)(2,1)S(1)}, u32[]{:S(2)}, u32[]{:S(2)}) collective-permute-start(bf16[128,256]{1,0:T(8,128)(2,1)S(1)} %get-tuple-element.30.refs_0_), channel_id=1, source_target_pairs={{0,384},{128,0},{256,128},{384,256},{1,385},{129,1},{257,129},{385... | collective-permute-start | bytes 196616 | tf_op jit(solution)/shard_map/ppermute | solution.py:150
  86.0 1.1 pad_maximum_fusion.1
  89.2 4.1 %fusion.36 = (bf16[512,256]{1,0:T(8,128)(2,1)S(1)}, f32[512,256]{1,0:T(8,128)S(1)}) fusion(bf16[512,4096]{1,0:T(8,128)(2,1)} %all-gather.4.cloned.1.call-done, bf16[4096,256]{1,0:T(8,128)(2,1)} %bitcast.62), kind=kOutput, calls=%fused_computation.95 | convolution fusion | flops 1073872896 | bytes 7077888 | tf_op jit(solution)/shard_map/dot_general | solution.py:79
  93.3 1.3 collective-permute-start.4
  94.7 5.7 %collective-permute-done.4 = bf16[512,256]{1,0:T(8,128)(2,1)S(1)} collective-permute-done((bf16[512,256]{1,0:T(8,128)(2,1)S(1)}, bf16[512,256]{1,0:T(8,128)(2,1)S(1)}, u32[]{:S(2)}, u32[]{:S(2)}) %collective-permute-start.4) | collective-permute-done | bytes 262176 | tf_op jit(solution)/shard_map/ppermute | solution.py:162
  101.9 10.9 %all-to-all-start.5 = ((bf16[16,3,1024]{2,1,0:T(4,128)(2,1)}), bf16[16,3,1024]{2,1,0:T(4,128)(2,1)S(1)}, u32[]{:S(2)}, u32[]{:S(2)}) async-start(bf16[16,3,1024]{2,1,0:T(4,128)(2,1)} %broadcast_in_dim.40), calls=%async_computation.5 | async-start | bytes 262144 | tf_op jit(solution)/shard_map/all_to_all | solution.py:24
  113.5 8.6 %all-to-all-done.5 = bf16[16,3,1024]{2,1,0:T(4,128)(2,1)S(1)} async-done(((bf16[16,3,1024]{2,1,0:T(4,128)(2,1)}), bf16[16,3,1024]{2,1,0:T(4,128)(2,1)S(1)}, u32[]{:S(2)}, u32[]{:S(2)}) %all-to-all-start.5) | async-done | bytes 98336 | tf_op jit(solution)/shard_map/all_to_all | solution.py:24
  122.5 17.1 %all_to_all.57 = bf16[8,12,256]{2,1,0:T(8,128)(2,1)S(1)} all-to-all(bf16[8,12,256]{2,1,0:T(8,128)(2,1)S(1)} %reshape.231), channel_id=1, replica_groups=mesh['far'=4,'row'=4,'core'=2,'section'=2,'tp'=8] {'tp'}, dimensions={0} | all-to-all | bytes 98304 | tf_op jit(solution)/shard_map/all_to_all | solution.py:24
  140.3 3.5 %all-to-all-start.7 = ((bf16[16,12,256]{2,1,0:T(8,128)(2,1)}), bf16[16,12,256]{2,1,0:T(8,128)(2,1)S(1)}, u32[]{:S(2)}, u32[]{:S(2)}) async-start(bf16[16,12,256]{2,1,0:T(8,128)(2,1)} %broadcast_in_dim.41), calls=%async_computation.7 | async-start | bytes 262144 | tf_op jit(solution)/shard_map/all_to_all | solution.py:24
  143.8 4.8 %fusion.38 = (bf16[512,256]{1,0:T(8,128)(2,1)}, f32[512,256]{1,0:T(8,128)S(1)}) fusion(bf16[512,4096]{1,0:T(8,128)(2,1)} %all-gather.4.cloned.1.call-done, bf16[4096,256]{1,0:T(8,128)(2,1)} %bitcast.73), kind=kOutput, calls=%fused_computation.97 | convolution fusion | flops 1073872896 | bytes 7077888 | tf_op jit(solution)/shard_map/dot_general | solution.py:79
  148.7 2.5 %all-to-all-done.7 = bf16[16,12,256]{2,1,0:T(8,128)(2,1)S(1)} async-done(((bf16[16,12,256]{2,1,0:T(8,128)(2,1)}), bf16[16,12,256]{2,1,0:T(8,128)(2,1)S(1)}, u32[]{:S(2)}, u32[]{:S(2)}) %all-to-all-start.7) | async-done | bytes 98336 | tf_op jit(solution)/shard_map/all_to_all | solution.py:24
  152.3 3.5 %all-to-all-start.8 = ((bf16[16,3,1024]{2,1,0:T(4,128)(2,1)}), bf16[16,3,1024]{2,1,0:T(4,128)(2,1)S(1)}, u32[]{:S(2)}, u32[]{:S(2)}) async-start(bf16[16,3,1024]{2,1,0:T(4,128)(2,1)} %reshape.238), calls=%async_computation.8 | async-start | bytes 262144 | tf_op jit(solution)/shard_map/all_to_all | solution.py:24
  155.8 2.3 %collective-permute-start.8 = (bf16[512,256]{1,0:T(8,128)(2,1)}, bf16[512,256]{1,0:T(8,128)(2,1)S(1)}, u32[]{:S(2)}, u32[]{:S(2)}) collective-permute-start(bf16[512,256]{1,0:T(8,128)(2,1)} %get-tuple-element.34), channel_id=1, source_target_pairs={{0,8},{1,9},{2,10},{3,11},{4,12},{5,13},{6,14},{7,15},{16,24},{17,... | collective-permute-start | bytes 786440 | tf_op jit(solution)/shard_map/ppermute | solution.py:162
  158.1 7.0 %all-to-all-done.8 = bf16[16,3,1024]{2,1,0:T(4,128)(2,1)S(1)} async-done(((bf16[16,3,1024]{2,1,0:T(4,128)(2,1)}), bf16[16,3,1024]{2,1,0:T(4,128)(2,1)S(1)}, u32[]{:S(2)}, u32[]{:S(2)}) %all-to-all-start.8) | async-done | bytes 98336 | tf_op jit(solution)/shard_map/all_to_all | solution.py:24
  166.2 14.5 %all_to_all.58 = bf16[16,3,1024]{2,1,0:T(4,128)(2,1)S(1)} all-to-all(bf16[16,3,1024]{2,1,0:T(4,128)(2,1)S(1)} %broadcast_in_dim.43), channel_id=1, replica_groups=mesh['far'=4,'row'=4,'core'=2,'section'=2,'tp'=8] {'far','row'}, dimensions={0} | all-to-all | bytes 196608 | tf_op jit(solution)/shard_map/all_to_all | solution.py:24
  181.9 12.0 %all-to-all-start.10 = ((bf16[16,48,256]{2,1,0:T(8,128)(2,1)}), bf16[16,48,256]{2,1,0:T(8,128)(2,1)S(1)}, u32[]{:S(2)}, u32[]{:S(2)}) async-start(bf16[16,48,256]{2,1,0:T(8,128)(2,1)} %bitcast.23), calls=%async_computation.10 | async-start | bytes 786432 | tf_op jit(solution)/shard_map/all_to_all | solution.py:24
  193.9 2.0 collective-permute-start.9
  198.5 7.8 %all-to-all-done.10 = bf16[16,48,256]{2,1,0:T(8,128)(2,1)S(1)} async-done(((bf16[16,48,256]{2,1,0:T(8,128)(2,1)}), bf16[16,48,256]{2,1,0:T(8,128)(2,1)S(1)}, u32[]{:S(2)}, u32[]{:S(2)}) %all-to-all-start.10) | async-done | bytes 393248 | tf_op jit(solution)/shard_map/all_to_all | solution.py:24
  (102 shorter events, 16.4 us)
Async XLA Ops:
  7.2 1.0 copy-start
  8.2 4.4 %copy-start.2 = (bf16[1,256,1,256]{3,1,2,0:T(8,128)(2,1)S(1)}, bf16[1,256,1,256]{3,1,2,0:T(8,128)(2,1)}, u32[]{:S(2)}) copy-start(bf16[1,256,1,256]{3,1,2,0:T(8,128)(2,1)} %param.12) | copy-start | bytes 393220
  9.1 10.3 %all-to-all-start = ((bf16[2,32,4096]{2,1,0:T(8,128)(2,1)}), bf16[2,32,4096]{2,1,0:T(8,128)(2,1)S(1)}, u32[]{:S(2)}, u32[]{:S(2)}) async-start(bf16[2,32,4096]{2,1,0:T(8,128)(2,1)} %deal_halves.1), calls=%async_computation | async-start | bytes 1048576 | tf_op jit(solution)/shard_map/all_to_all | solution.py:24
  12.6 75.8 %all-gather.4.cloned.1.call-start = ((), (), s32[]{:S(2)}) async-start(), calls=%async_computation.11 | async-start | bytes 4718592 | tf_op jit(solution)/shard_map/all_gather | solution.py:132
  12.7 6.7 %collective-permute-start.2 = (bf16[128,256]{1,0:T(8,128)(2,1)S(1)}, bf16[128,256]{1,0:T(8,128)(2,1)S(1)}, u32[]{:S(2)}, u32[]{:S(2)}) collective-permute-start(bf16[128,256]{1,0:T(8,128)(2,1)S(1)} %select_bitcast_fusion), channel_id=1, source_target_pairs={{0,8},{8,0},{1,9},{9,1},{2,10},{10,2},{3,11},{11,3},{4,12},{12,4},... | collective-permute-start | bytes 196616 | tf_op jit(solution)/shard_map/ppermute | solution.py:131
  19.4 0.8 copy-start.1
  20.2 23.7 %copy-start.5 = (bf16[32,3,256]{2,0,1:T(8,128)(2,1)S(1)}, bf16[32,3,256]{2,0,1:T(8,128)(2,1)}, u32[]{:S(2)}) copy-start(bf16[32,3,256]{2,0,1:T(8,128)(2,1)} %param.9) | copy-start | bytes 147460
  20.3 23.7 %copy-start.3 = (bf16[1,256,1024]{2,1,0:T(8,128)(2,1)S(1)}, bf16[1,256,1024]{2,1,0:T(8,128)(2,1)}, u32[]{:S(2)}) copy-start(bf16[1,256,1024]{2,1,0:T(8,128)(2,1)} %param.14) | copy-start | bytes 1572868
  38.8 12.2 %copy-start.4 = (bf16[1,1024,256]{2,1,0:T(8,128)(2,1)S(1)}, bf16[1,1024,256]{2,1,0:T(8,128)(2,1)}, u32[]{:S(2)}) copy-start(bf16[1,1024,256]{2,1,0:T(8,128)(2,1)} %param.16) | copy-start | bytes 1572868
  39.9 15.9 %all-to-all-start.2 = ((bf16[4,4,128,256]{3,2,1,0:T(8,128)(2,1)}), bf16[4,4,128,256]{3,2,1,0:T(8,128)(2,1)S(1)}, u32[]{:S(2)}, u32[]{:S(2)}) async-start(bf16[4,4,128,256]{3,2,1,0:T(8,128)(2,1)} %broadcast_in_dim.35), calls=%async_computation.2 | async-start | bytes 2097152 | tf_op jit(solution)/shard_map/all_to_all | solution.py:24
  44.0 9.6 %collective-permute-start.1 = (bf16[256,1024]{1,0:T(8,128)(2,1)S(1)}, bf16[256,1024]{1,0:T(8,128)(2,1)}, u32[]{:S(2)}, u32[]{:S(2)}) collective-permute-start(bf16[256,1024]{1,0:T(8,128)(2,1)S(1)} %bitcast.66), channel_id=1, source_target_pairs={{0,16},{16,0},{1,17},{17,1},{2,18},{18,2},{3,19},{19,3},{4,20},{20... | collective-permute-start | bytes 1572872 | tf_op jit(solution)/shard_map/ppermute | solution.py:117
  49.1 4.4 %collective-permute-start = (bf16[48,256]{1,0:T(8,128)(2,1)S(1)}, bf16[48,256]{1,0:T(8,128)(2,1)S(1)}, u32[]{:S(2)}, u32[]{:S(2)}) collective-permute-start(bf16[48,256]{1,0:T(8,128)(2,1)S(1)} %select_n.133), channel_id=1, source_target_pairs={{0,16},{16,0},{1,17},{17,1},{2,18},{18,2},{3,19},{19,3},{4,20},{20... | collective-permute-start | bytes 73736 | tf_op jit(solution)/shard_map/ppermute | solution.py:117
  51.1 34.9 %collective-permute-start.3 = (bf16[1024,256]{1,0:T(8,128)(2,1)S(1)}, bf16[1024,256]{1,0:T(8,128)(2,1)}, u32[]{:S(2)}, u32[]{:S(2)}) collective-permute-start(bf16[1024,256]{1,0:T(8,128)(2,1)S(1)} %bitcast.68), channel_id=1, source_target_pairs={{0,16},{16,0},{1,17},{17,1},{2,18},{18,2},{3,19},{19,3},{4,20},{20... | collective-permute-start | bytes 1572872 | tf_op jit(solution)/shard_map/ppermute | solution.py:117
  66.1 23.0 %copy-start.6 = (bf16[1,128]{1,0:T(2,128)(2,1)S(1)}, bf16[1,128]{1,0:T(2,128)(2,1)}, u32[]{:S(2)}) copy-start(bf16[1,128]{1,0:T(2,128)(2,1)} %param.15) | copy-start | bytes 772
  66.1 23.0 %copy-start.7 = (bf16[1,128]{1,0:T(2,128)(2,1)S(1)}, bf16[1,128]{1,0:T(2,128)(2,1)}, u32[]{:S(2)}) copy-start(bf16[1,128]{1,0:T(2,128)(2,1)} %param.13) | copy-start | bytes 772
  67.2 21.2 %all-to-all-start.4 = ((bf16[16,3,1024]{2,1,0:T(4,128)(2,1)}), bf16[16,3,1024]{2,1,0:T(4,128)(2,1)S(1)}, u32[]{:S(2)}, u32[]{:S(2)}) async-start(bf16[16,3,1024]{2,1,0:T(4,128)(2,1)} %reshape.228), calls=%async_computation.4 | async-start | bytes 262144 | tf_op jit(solution)/shard_map/all_to_all | solution.py:24
  71.3 68.3 %all-gather.6.cloned.1.call-start = ((), (), s32[]{:S(2)}) async-start(), calls=%async_computation.12 | async-start | bytes 2359296 | tf_op jit(solution)/shard_map/all_gather | solution.py:175
  71.4 15.7 %collective-permute-start.5 = (bf16[128,256]{1,0:T(8,128)(2,1)S(1)}, bf16[128,256]{1,0:T(8,128)(2,1)S(1)}, u32[]{:S(2)}, u32[]{:S(2)}) collective-permute-start(bf16[128,256]{1,0:T(8,128)(2,1)S(1)} %get-tuple-element.30.refs_0_), channel_id=1, source_target_pairs={{0,128},{128,256},{256,384},{384,0},{1,129},{129,257},{257,385},{3... | collective-permute-start | bytes 196616 | tf_op jit(solution)/shard_map/ppermute | solution.py:150
  75.6 11.6 %collective-permute-start.6 = (bf16[128,256]{1,0:T(8,128)(2,1)S(1)}, bf16[128,256]{1,0:T(8,128)(2,1)S(1)}, u32[]{:S(2)}, u32[]{:S(2)}) collective-permute-start(bf16[128,256]{1,0:T(8,128)(2,1)S(1)} %get-tuple-element.30.refs_0_), channel_id=1, source_target_pairs={{0,256},{128,384},{256,0},{384,128},{1,257},{129,385},{257,1},{385... | collective-permute-start | bytes 196616 | tf_op jit(solution)/shard_map/ppermute | solution.py:150
  80.8 6.8 %collective-permute-start.7 = (bf16[128,256]{1,0:T(8,128)(2,1)S(1)}, bf16[128,256]{1,0:T(8,128)(2,1)S(1)}, u32[]{:S(2)}, u32[]{:S(2)}) collective-permute-start(bf16[128,256]{1,0:T(8,128)(2,1)S(1)} %get-tuple-element.30.refs_0_), channel_id=1, source_target_pairs={{0,384},{128,0},{256,128},{384,256},{1,385},{129,1},{257,129},{385... | collective-permute-start | bytes 196616 | tf_op jit(solution)/shard_map/ppermute | solution.py:150
  93.3 7.1 %collective-permute-start.4 = (bf16[512,256]{1,0:T(8,128)(2,1)S(1)}, bf16[512,256]{1,0:T(8,128)(2,1)S(1)}, u32[]{:S(2)}, u32[]{:S(2)}) collective-permute-start(bf16[512,256]{1,0:T(8,128)(2,1)S(1)} %get-tuple-element.51), channel_id=1, source_target_pairs={{8,0},{9,1},{10,2},{11,3},{12,4},{13,5},{14,6},{15,7},{24,16},{25,... | collective-permute-start | bytes 786440 | tf_op jit(solution)/shard_map/ppermute | solution.py:162
  101.9 20.2 %all-to-all-start.5 = ((bf16[16,3,1024]{2,1,0:T(4,128)(2,1)}), bf16[16,3,1024]{2,1,0:T(4,128)(2,1)S(1)}, u32[]{:S(2)}, u32[]{:S(2)}) async-start(bf16[16,3,1024]{2,1,0:T(4,128)(2,1)} %broadcast_in_dim.40), calls=%async_computation.5 | async-start | bytes 262144 | tf_op jit(solution)/shard_map/all_to_all | solution.py:24
  140.3 10.9 %all-to-all-start.7 = ((bf16[16,12,256]{2,1,0:T(8,128)(2,1)}), bf16[16,12,256]{2,1,0:T(8,128)(2,1)S(1)}, u32[]{:S(2)}, u32[]{:S(2)}) async-start(bf16[16,12,256]{2,1,0:T(8,128)(2,1)} %broadcast_in_dim.41), calls=%async_computation.7 | async-start | bytes 262144 | tf_op jit(solution)/shard_map/all_to_all | solution.py:24
  152.3 12.8 %all-to-all-start.8 = ((bf16[16,3,1024]{2,1,0:T(4,128)(2,1)}), bf16[16,3,1024]{2,1,0:T(4,128)(2,1)S(1)}, u32[]{:S(2)}, u32[]{:S(2)}) async-start(bf16[16,3,1024]{2,1,0:T(4,128)(2,1)} %reshape.238), calls=%async_computation.8 | async-start | bytes 262144 | tf_op jit(solution)/shard_map/all_to_all | solution.py:24
  155.8 9.5 %collective-permute-start.8 = (bf16[512,256]{1,0:T(8,128)(2,1)}, bf16[512,256]{1,0:T(8,128)(2,1)S(1)}, u32[]{:S(2)}, u32[]{:S(2)}) collective-permute-start(bf16[512,256]{1,0:T(8,128)(2,1)} %get-tuple-element.34), channel_id=1, source_target_pairs={{0,8},{1,9},{2,10},{3,11},{4,12},{5,13},{6,14},{7,15},{16,24},{17,... | collective-permute-start | bytes 786440 | tf_op jit(solution)/shard_map/ppermute | solution.py:162
  181.9 24.5 %all-to-all-start.10 = ((bf16[16,48,256]{2,1,0:T(8,128)(2,1)}), bf16[16,48,256]{2,1,0:T(8,128)(2,1)S(1)}, u32[]{:S(2)}, u32[]{:S(2)}) async-start(bf16[16,48,256]{2,1,0:T(8,128)(2,1)} %bitcast.23), calls=%async_computation.10 | async-start | bytes 786432 | tf_op jit(solution)/shard_map/all_to_all | solution.py:24
  193.9 3.1 %collective-permute-start.9 = (bf16[48,256]{1,0:T(8,128)(2,1)S(1)}, bf16[48,256]{1,0:T(8,128)(2,1)S(1)}, u32[]{:S(2)}, u32[]{:S(2)}) collective-permute-start(bf16[48,256]{1,0:T(8,128)(2,1)S(1)} %slice.77), channel_id=1, source_target_pairs={{0,16},{16,0},{1,17},{17,1},{2,18},{18,2},{3,19},{19,3},{4,20},{20... | collective-permute-start | bytes 73736 | tf_op jit(solution)/shard_map/ppermute | solution.py:117
Sparse Core Ops, SparseCore 0:
  20.3 66.5 all-gather.3
  89.1 35.7 all-gather.5

commit v11 on v8

--- a/solution.py
+++ b/solution.py
@@ -160,10 +160,9 @@
     )
     first_sum, second_weight = lax.optimization_barrier((first_sum, second_weight))
     first_sum = jnp.concatenate([first_sum[:, :columns], first_sum[:, columns:]])
-    first_sum = first_sum.reshape(tensor_count, -1, columns)
-    summed = jnp.sum(exchange(first_sum, "tp").astype(F32), axis=0).astype(BF16)
-    everywhere = gathered(summed, ("section", "tp"))[:tensor_count]
-    everywhere = everywhere.reshape(2, chips * positions, -1).astype(F32)
+    everywhere = gathered(first_sum, ("section", "tp"))[:tensor_count]
+    everywhere = jnp.sum(everywhere.astype(F32), axis=0)
+    everywhere = everywhere.reshape(2, chips * positions, -1)
     everywhere = jnp.concatenate([everywhere[0], everywhere[1]], axis=1)
     first = (state.astype(F32) + everywhere).astype(BF16)
 

time: 213 us -> 215 us (level)
  blocking collectives: 61.4 us -> 50.7 us
  waiting for transfers between devices: 45.6 us -> 55 us
  starting transfers between devices: 62.4 us -> 66 us
    all_to_all x4 -> x3, blocking collectives: 61.4 us -> 50.7 us  [exchange(): return lax.all_to_all(blocks, axis, 0, 0, tiled=True)]
    all_to_all x7, waiting for transfers between devices: 35.4 us -> 44.7 us  [exchange(): return lax.all_to_all(blocks, axis, 0, 0, tiled=True)]
    all_to_all x7, starting transfers between devices: 43.5 us -> 46.3 us  [exchange(): return lax.all_to_all(blocks, axis, 0, 0, tiled=True)]
where the time goes in v11:
time: 215 us; the launch traced here: 214 us
  starting transfers between devices  66 us (31%)
  waiting for transfers between devices  55 us (26%)
  blocking collectives  50.7 us (24%)
  between operations  15.9 us (7%)
  matrix products  11.4 us (5%)
  local copies, waits for them, and re-layouts  10.5 us (5%)
  other arithmetic  3.57 us (2%)
    all_to_all x3, blocking collectives, exchange(): return lax.all_to_all(blocks, axis, 0, 0, tiled=True)  50.7 us
    all_to_all x7, starting transfers between devices, exchange(): return lax.all_to_all(blocks, axis, 0, 0, tiled=True)  46.3 us
    all_to_all x7, waiting for transfers between devices, exchange(): return lax.all_to_all(blocks, axis, 0, 0, tiled=True)  44.7 us
    ppermute x4, starting transfers between devices, to_other_core(): return lax.ppermute(block, 'core', SWAP)  11.2 us
    dot_general x2, matrix products, projected(): product = jnp.dot(rows, weight, preferred_element_type=F32)  9.12 us
    ppermute x2, waiting for transfers between devices, handed(): return lax.ppermute(partial_sum, 'section', [direction]).astype(F32)  6.45 us
    ppermute x2, starting transfers between devices, handed(): return lax.ppermute(partial_sum, 'section', [direction]).astype(F32)  4.36 us
  transfers between devices with their start and end apart: 16, of which 9 were waited for; matrix products, arithmetic and copies ran while one was open for 9% of the time, Pallas kernels for 0%

profile of v11, /device:TPU:1, one launch (start us, length us, event | category | flops | bytes accessed | tf_op | source)
XLA Modules:
  0.0 214.0 jit_solution(17607427286293422630)
XLA Ops:
  7.2 1.0 copy-done
  9.1 3.5 %all-to-all-start = ((bf16[2,32,4096]{2,1,0:T(8,128)(2,1)}), bf16[2,32,4096]{2,1,0:T(8,128)(2,1)S(1)}, u32[]{:S(2)}, u32[]{:S(2)}) async-start(bf16[2,32,4096]{2,1,0:T(8,128)(2,1)} %deal_halves.1), calls=%async_computation | async-start | bytes 1048576 | tf_op jit(solution)/shard_map/all_to_all | solution.py:24
  12.7 4.0 %collective-permute-start.2 = (bf16[128,256]{1,0:T(8,128)(2,1)S(1)}, bf16[128,256]{1,0:T(8,128)(2,1)S(1)}, u32[]{:S(2)}, u32[]{:S(2)}) collective-permute-start(bf16[128,256]{1,0:T(8,128)(2,1)S(1)} %get-tuple-element.40), channel_id=1, source_target_pairs={{0,8},{8,0},{1,9},{9,1},{2,10},{10,2},{3,11},{11,3},{4,12},{12,4},... | collective-permute-start | bytes 196616 | tf_op jit(solution)/shard_map/ppermute | solution.py:110
  16.7 2.7 %collective-permute-done.2 = bf16[128,256]{1,0:T(8,128)(2,1)S(1)} collective-permute-done((bf16[128,256]{1,0:T(8,128)(2,1)S(1)}, bf16[128,256]{1,0:T(8,128)(2,1)S(1)}, u32[]{:S(2)}, u32[]{:S(2)}) %collective-permute-start.2) | collective-permute-done | bytes 65568 | tf_op jit(solution)/shard_map/ppermute | solution.py:110
  20.3 24.0 %all_to_all.50 = bf16[4,2,128,256]{3,2,1,0:T(8,128)(2,1)S(1)} all-to-all(bf16[4,2,128,256]{3,2,1,0:T(8,128)(2,1)S(1)} %broadcast_in_dim.36), channel_id=1, replica_groups=mesh['far'=4,'row'=4,'core'=2,'section'=2,'tp'=8] {'far'}, dimensions={0} | all-to-all | bytes 1048576 | tf_op jit(solution)/shard_map/all_to_all | solution.py:24
  45.0 1.1 broadcast_in_dim.38
  46.1 4.0 %all-to-all-start.2 = ((bf16[4,4,128,256]{3,2,1,0:T(8,128)(2,1)}), bf16[4,4,128,256]{3,2,1,0:T(8,128)(2,1)S(1)}, u32[]{:S(2)}, u32[]{:S(2)}) async-start(bf16[4,4,128,256]{3,2,1,0:T(8,128)(2,1)} %broadcast_in_dim.38), calls=%async_computation.2 | async-start | bytes 2097152 | tf_op jit(solution)/shard_map/all_to_all | solution.py:24
  50.2 4.9 %collective-permute-start.1 = (bf16[256,1024]{1,0:T(8,128)(2,1)S(1)}, bf16[256,1024]{1,0:T(8,128)(2,1)}, u32[]{:S(2)}, u32[]{:S(2)}) collective-permute-start(bf16[256,1024]{1,0:T(8,128)(2,1)S(1)} %bitcast.69), channel_id=1, source_target_pairs={{0,16},{16,0},{1,17},{17,1},{2,18},{18,2},{3,19},{19,3},{4,20},{20... | collective-permute-start | bytes 1572872 | tf_op jit(solution)/shard_map/ppermute | solution.py:96
  55.3 1.9 collective-permute-start
  57.2 2.4 %collective-permute-start.3 = (bf16[1024,256]{1,0:T(8,128)(2,1)S(1)}, bf16[1024,256]{1,0:T(8,128)(2,1)}, u32[]{:S(2)}, u32[]{:S(2)}) collective-permute-start(bf16[1024,256]{1,0:T(8,128)(2,1)S(1)} %bitcast.71), channel_id=1, source_target_pairs={{0,16},{16,0},{1,17},{17,1},{2,18},{18,2},{3,19},{19,3},{4,20},{20... | collective-permute-start | bytes 1572872 | tf_op jit(solution)/shard_map/ppermute | solution.py:96
  59.7 1.1 pad_maximum_fusion
  60.8 1.2 all-to-all-done.2
  62.3 10.1 %all_to_all.51 = bf16[2,4,4,128,256]{4,3,2,1,0:T(8,128)(2,1)} all-to-all(bf16[2,4,4,128,256]{4,3,2,1,0:T(8,128)(2,1)S(1)} %broadcast_in_dim.39), channel_id=1, replica_groups=mesh['far'=4,'row'=4,'core'=2,'section'=2,'tp'=8] {'core'}, dimensions={0} | all-to-all | bytes 4194304 | tf_op jit(solution)/shard_map/all_to_all | solution.py:24
  73.4 5.4 %all-to-all-start.4 = ((bf16[16,3,1024]{2,1,0:T(4,128)(2,1)}), bf16[16,3,1024]{2,1,0:T(4,128)(2,1)S(1)}, u32[]{:S(2)}, u32[]{:S(2)}) async-start(bf16[16,3,1024]{2,1,0:T(4,128)(2,1)} %reshape.270), calls=%async_computation.4 | async-start | bytes 262144 | tf_op jit(solution)/shard_map/all_to_all | solution.py:24
  78.8 1.1 pad_maximum_fusion.1
  79.9 8.0 %all-to-all-done.4 = bf16[16,3,1024]{2,1,0:T(4,128)(2,1)S(1)} async-done(((bf16[16,3,1024]{2,1,0:T(4,128)(2,1)}), bf16[16,3,1024]{2,1,0:T(4,128)(2,1)S(1)}, u32[]{:S(2)}, u32[]{:S(2)}) %all-to-all-start.4) | async-done | bytes 98336 | tf_op jit(solution)/shard_map/all_to_all | solution.py:24
  88.8 4.1 %fusion.36 = (bf16[512,256]{1,0:T(8,128)(2,1)S(1)}, f32[512,256]{1,0:T(8,128)S(1)}) fusion(bf16[512,4096]{1,0:T(8,128)(2,1)} %all-gather.4.cloned.1.call-done, bf16[4096,256]{1,0:T(8,128)(2,1)} %bitcast.65), kind=kOutput, calls=%fused_computation.96 | convolution fusion | flops 1073872896 | bytes 7077888 | tf_op jit(solution)/shard_map/dot_general | solution.py:58
  92.9 1.3 collective-permute-start.4
  94.4 6.5 %collective-permute-done.4 = bf16[512,256]{1,0:T(8,128)(2,1)S(1)} collective-permute-done((bf16[512,256]{1,0:T(8,128)(2,1)S(1)}, bf16[512,256]{1,0:T(8,128)(2,1)S(1)}, u32[]{:S(2)}, u32[]{:S(2)}) %collective-permute-start.4) | collective-permute-done | bytes 262176 | tf_op jit(solution)/shard_map/ppermute | solution.py:136
  102.3 9.1 %all-to-all-start.5 = ((bf16[16,3,1024]{2,1,0:T(4,128)(2,1)}), bf16[16,3,1024]{2,1,0:T(4,128)(2,1)S(1)}, u32[]{:S(2)}, u32[]{:S(2)}) async-start(bf16[16,3,1024]{2,1,0:T(4,128)(2,1)} %broadcast_in_dim.43), calls=%async_computation.5 | async-start | bytes 262144 | tf_op jit(solution)/shard_map/all_to_all | solution.py:24
  112.1 8.7 %all-to-all-done.5 = bf16[16,3,1024]{2,1,0:T(4,128)(2,1)S(1)} async-done(((bf16[16,3,1024]{2,1,0:T(4,128)(2,1)}), bf16[16,3,1024]{2,1,0:T(4,128)(2,1)S(1)}, u32[]{:S(2)}, u32[]{:S(2)}) %all-to-all-start.5) | async-done | bytes 98336 | tf_op jit(solution)/shard_map/all_to_all | solution.py:24
  122.2 5.9 %all-to-all-start.6 = ((bf16[16,96,256]{2,1,0:T(8,128)(2,1)}), bf16[16,96,256]{2,1,0:T(8,128)(2,1)S(1)}, u32[]{:S(2)}, u32[]{:S(2)}) async-start(bf16[16,96,256]{2,1,0:T(8,128)(2,1)} %broadcast_in_dim.80), calls=%async_computation.6 | async-start | bytes 1572864 | tf_op jit(solution)/shard_map/all_to_all | solution.py:24
  128.2 5.0 %fusion.38 = (bf16[512,256]{1,0:T(8,128)(2,1)}, f32[512,256]{1,0:T(8,128)}) fusion(bf16[512,4096]{1,0:T(8,128)(2,1)} %all-gather.4.cloned.1.call-done, bf16[4096,256]{1,0:T(8,128)(2,1)} %bitcast.77), kind=kOutput, calls=%fused_computation.98 | convolution fusion | flops 1073872896 | bytes 7077888 | tf_op jit(solution)/shard_map/dot_general | solution.py:58
  133.2 12.7 %all-to-all-done.6 = bf16[16,96,256]{2,1,0:T(8,128)(2,1)S(1)} async-done(((bf16[16,96,256]{2,1,0:T(8,128)(2,1)}), bf16[16,96,256]{2,1,0:T(8,128)(2,1)S(1)}, u32[]{:S(2)}, u32[]{:S(2)}) %all-to-all-start.6) | async-done | bytes 786464 | tf_op jit(solution)/shard_map/all_to_all | solution.py:24
  147.0 8.1 %all-to-all-start.7 = ((bf16[16,3,1024]{2,1,0:T(4,128)(2,1)}), bf16[16,3,1024]{2,1,0:T(4,128)(2,1)S(1)}, u32[]{:S(2)}, u32[]{:S(2)}) async-start(bf16[16,3,1024]{2,1,0:T(4,128)(2,1)} %reshape.278), calls=%async_computation.7 | async-start | bytes 262144 | tf_op jit(solution)/shard_map/all_to_all | solution.py:24
  155.1 3.1 %collective-permute-start.5 = (bf16[512,256]{1,0:T(8,128)(2,1)}, bf16[512,256]{1,0:T(8,128)(2,1)S(1)}, u32[]{:S(2)}, u32[]{:S(2)}) collective-permute-start(bf16[512,256]{1,0:T(8,128)(2,1)} %get-tuple-element.32), channel_id=1, source_target_pairs={{0,8},{1,9},{2,10},{3,11},{4,12},{5,13},{6,14},{7,15},{16,24},{17,... | collective-permute-start | bytes 786440 | tf_op jit(solution)/shard_map/ppermute | solution.py:136
  158.2 6.3 %all-to-all-done.7 = bf16[16,3,1024]{2,1,0:T(4,128)(2,1)S(1)} async-done(((bf16[16,3,1024]{2,1,0:T(4,128)(2,1)}), bf16[16,3,1024]{2,1,0:T(4,128)(2,1)S(1)}, u32[]{:S(2)}, u32[]{:S(2)}) %all-to-all-start.7) | async-done | bytes 98336 | tf_op jit(solution)/shard_map/all_to_all | solution.py:24
  165.6 16.6 %all_to_all.52 = bf16[16,3,1024]{2,1,0:T(4,128)(2,1)S(1)} all-to-all(bf16[16,3,1024]{2,1,0:T(4,128)(2,1)S(1)} %broadcast_in_dim.82), channel_id=1, replica_groups=mesh['far'=4,'row'=4,'core'=2,'section'=2,'tp'=8] {'far','row'}, dimensions={0} | all-to-all | bytes 196608 | tf_op jit(solution)/shard_map/all_to_all | solution.py:24
  183.3 10.4 %all-to-all-start.9 = ((bf16[16,48,256]{2,1,0:T(8,128)(2,1)}), bf16[16,48,256]{2,1,0:T(8,128)(2,1)S(1)}, u32[]{:S(2)}, u32[]{:S(2)}) async-start(bf16[16,48,256]{2,1,0:T(8,128)(2,1)} %bitcast.25), calls=%async_computation.9 | async-start | bytes 786432 | tf_op jit(solution)/shard_map/all_to_all | solution.py:24
  193.7 2.0 collective-permute-start.6
  195.8 1.0 collective-permute-done.6
  198.4 7.8 %all-to-all-done.9 = bf16[16,48,256]{2,1,0:T(8,128)(2,1)S(1)} async-done(((bf16[16,48,256]{2,1,0:T(8,128)(2,1)}), bf16[16,48,256]{2,1,0:T(8,128)(2,1)S(1)}, u32[]{:S(2)}, u32[]{:S(2)}) %all-to-all-start.9) | async-done | bytes 393248 | tf_op jit(solution)/shard_map/all_to_all | solution.py:24
  (93 shorter events, 13.1 us)
Async XLA Ops:
  7.2 1.0 copy-start
  8.2 4.4 %copy-start.5 = (bf16[1,256,1,256]{3,1,2,0:T(8,128)(2,1)S(1)}, bf16[1,256,1,256]{3,1,2,0:T(8,128)(2,1)}, u32[]{:S(2)}) copy-start(bf16[1,256,1,256]{3,1,2,0:T(8,128)(2,1)} %param.12) | copy-start | bytes 393220
  9.1 10.3 %all-to-all-start = ((bf16[2,32,4096]{2,1,0:T(8,128)(2,1)}), bf16[2,32,4096]{2,1,0:T(8,128)(2,1)S(1)}, u32[]{:S(2)}, u32[]{:S(2)}) async-start(bf16[2,32,4096]{2,1,0:T(8,128)(2,1)} %deal_halves.1), calls=%async_computation | async-start | bytes 1048576 | tf_op jit(solution)/shard_map/all_to_all | solution.py:24
  12.6 75.5 %all-gather.4.cloned.1.call-start = ((), (), s32[]{:S(2)}) async-start(), calls=%async_computation.10 | async-start | bytes 4718592 | tf_op jit(solution)/shard_map/all_gather | solution.py:111
  12.7 6.7 %collective-permute-start.2 = (bf16[128,256]{1,0:T(8,128)(2,1)S(1)}, bf16[128,256]{1,0:T(8,128)(2,1)S(1)}, u32[]{:S(2)}, u32[]{:S(2)}) collective-permute-start(bf16[128,256]{1,0:T(8,128)(2,1)S(1)} %get-tuple-element.40), channel_id=1, source_target_pairs={{0,8},{8,0},{1,9},{9,1},{2,10},{10,2},{3,11},{11,3},{4,12},{12,4},... | collective-permute-start | bytes 196616 | tf_op jit(solution)/shard_map/ppermute | solution.py:110
  19.4 0.8 copy-start.1
  44.3 5.8 %copy-start.6 = (bf16[32,3,256]{2,0,1:T(8,128)(2,1)S(1)}, bf16[32,3,256]{2,0,1:T(8,128)(2,1)}, u32[]{:S(2)}) copy-start(bf16[32,3,256]{2,0,1:T(8,128)(2,1)} %param.9) | copy-start | bytes 147460
  44.3 5.9 %copy-start.3 = (bf16[1,256,1024]{2,1,0:T(8,128)(2,1)S(1)}, bf16[1,256,1024]{2,1,0:T(8,128)(2,1)}, u32[]{:S(2)}) copy-start(bf16[1,256,1024]{2,1,0:T(8,128)(2,1)} %param.14) | copy-start | bytes 1572868
  45.0 12.2 %copy-start.4 = (bf16[1,1024,256]{2,1,0:T(8,128)(2,1)S(1)}, bf16[1,1024,256]{2,1,0:T(8,128)(2,1)}, u32[]{:S(2)}) copy-start(bf16[1,1024,256]{2,1,0:T(8,128)(2,1)} %param.16) | copy-start | bytes 1572868
  46.1 15.9 %all-to-all-start.2 = ((bf16[4,4,128,256]{3,2,1,0:T(8,128)(2,1)}), bf16[4,4,128,256]{3,2,1,0:T(8,128)(2,1)S(1)}, u32[]{:S(2)}, u32[]{:S(2)}) async-start(bf16[4,4,128,256]{3,2,1,0:T(8,128)(2,1)} %broadcast_in_dim.38), calls=%async_computation.2 | async-start | bytes 2097152 | tf_op jit(solution)/shard_map/all_to_all | solution.py:24
  50.2 9.5 %collective-permute-start.1 = (bf16[256,1024]{1,0:T(8,128)(2,1)S(1)}, bf16[256,1024]{1,0:T(8,128)(2,1)}, u32[]{:S(2)}, u32[]{:S(2)}) collective-permute-start(bf16[256,1024]{1,0:T(8,128)(2,1)S(1)} %bitcast.69), channel_id=1, source_target_pairs={{0,16},{16,0},{1,17},{17,1},{2,18},{18,2},{3,19},{19,3},{4,20},{20... | collective-permute-start | bytes 1572872 | tf_op jit(solution)/shard_map/ppermute | solution.py:96
  55.3 4.4 %collective-permute-start = (bf16[48,256]{1,0:T(8,128)(2,1)S(1)}, bf16[48,256]{1,0:T(8,128)(2,1)S(1)}, u32[]{:S(2)}, u32[]{:S(2)}) collective-permute-start(bf16[48,256]{1,0:T(8,128)(2,1)S(1)} %select_n.145), channel_id=1, source_target_pairs={{0,16},{16,0},{1,17},{17,1},{2,18},{18,2},{3,19},{19,3},{4,20},{20... | collective-permute-start | bytes 73736 | tf_op jit(solution)/shard_map/ppermute | solution.py:96
  57.2 21.6 %collective-permute-start.3 = (bf16[1024,256]{1,0:T(8,128)(2,1)S(1)}, bf16[1024,256]{1,0:T(8,128)(2,1)}, u32[]{:S(2)}, u32[]{:S(2)}) collective-permute-start(bf16[1024,256]{1,0:T(8,128)(2,1)S(1)} %bitcast.71), channel_id=1, source_target_pairs={{0,16},{16,0},{1,17},{17,1},{2,18},{18,2},{3,19},{19,3},{4,20},{20... | collective-permute-start | bytes 1572872 | tf_op jit(solution)/shard_map/ppermute | solution.py:96
  72.3 16.4 %copy-start.7 = (bf16[1,128]{1,0:T(2,128)(2,1)S(1)}, bf16[1,128]{1,0:T(2,128)(2,1)}, u32[]{:S(2)}) copy-start(bf16[1,128]{1,0:T(2,128)(2,1)} %param.15) | copy-start | bytes 772
  72.3 16.4 %copy-start.8 = (bf16[1,128]{1,0:T(2,128)(2,1)S(1)}, bf16[1,128]{1,0:T(2,128)(2,1)}, u32[]{:S(2)}) copy-start(bf16[1,128]{1,0:T(2,128)(2,1)} %param.13) | copy-start | bytes 772
  73.4 14.6 %all-to-all-start.4 = ((bf16[16,3,1024]{2,1,0:T(4,128)(2,1)}), bf16[16,3,1024]{2,1,0:T(4,128)(2,1)S(1)}, u32[]{:S(2)}, u32[]{:S(2)}) async-start(bf16[16,3,1024]{2,1,0:T(4,128)(2,1)} %reshape.270), calls=%async_computation.4 | async-start | bytes 262144 | tf_op jit(solution)/shard_map/all_to_all | solution.py:24
  78.7 42.4 %all-gather.6.cloned.1.call-start = ((), (), s32[]{:S(2)}) async-start(), calls=%async_computation.11 | async-start | bytes 2359296 | tf_op jit(solution)/shard_map/all_gather | solution.py:149
  92.9 7.9 %collective-permute-start.4 = (bf16[512,256]{1,0:T(8,128)(2,1)S(1)}, bf16[512,256]{1,0:T(8,128)(2,1)S(1)}, u32[]{:S(2)}, u32[]{:S(2)}) collective-permute-start(bf16[512,256]{1,0:T(8,128)(2,1)S(1)} %get-tuple-element.51), channel_id=1, source_target_pairs={{8,0},{9,1},{10,2},{11,3},{12,4},{13,5},{14,6},{15,7},{24,16},{25,... | collective-permute-start | bytes 786440 | tf_op jit(solution)/shard_map/ppermute | solution.py:136
  102.3 18.5 %all-to-all-start.5 = ((bf16[16,3,1024]{2,1,0:T(4,128)(2,1)}), bf16[16,3,1024]{2,1,0:T(4,128)(2,1)S(1)}, u32[]{:S(2)}, u32[]{:S(2)}) async-start(bf16[16,3,1024]{2,1,0:T(4,128)(2,1)} %broadcast_in_dim.43), calls=%async_computation.5 | async-start | bytes 262144 | tf_op jit(solution)/shard_map/all_to_all | solution.py:24
  122.2 23.7 %all-to-all-start.6 = ((bf16[16,96,256]{2,1,0:T(8,128)(2,1)}), bf16[16,96,256]{2,1,0:T(8,128)(2,1)S(1)}, u32[]{:S(2)}, u32[]{:S(2)}) async-start(bf16[16,96,256]{2,1,0:T(8,128)(2,1)} %broadcast_in_dim.80), calls=%async_computation.6 | async-start | bytes 1572864 | tf_op jit(solution)/shard_map/all_to_all | solution.py:24
  145.9 18.7 %copy-start.2 = (f32[512,256]{1,0:T(8,128)S(1)}, f32[512,256]{1,0:T(8,128)}, u32[]{:S(2)}) copy-start(f32[512,256]{1,0:T(8,128)} %get-tuple-element.56) | copy-start | bytes 1572868
  147.0 17.4 %all-to-all-start.7 = ((bf16[16,3,1024]{2,1,0:T(4,128)(2,1)}), bf16[16,3,1024]{2,1,0:T(4,128)(2,1)S(1)}, u32[]{:S(2)}, u32[]{:S(2)}) async-start(bf16[16,3,1024]{2,1,0:T(4,128)(2,1)} %reshape.278), calls=%async_computation.7 | async-start | bytes 262144 | tf_op jit(solution)/shard_map/all_to_all | solution.py:24
  155.1 9.6 %collective-permute-start.5 = (bf16[512,256]{1,0:T(8,128)(2,1)}, bf16[512,256]{1,0:T(8,128)(2,1)S(1)}, u32[]{:S(2)}, u32[]{:S(2)}) collective-permute-start(bf16[512,256]{1,0:T(8,128)(2,1)} %get-tuple-element.32), channel_id=1, source_target_pairs={{0,8},{1,9},{2,10},{3,11},{4,12},{5,13},{6,14},{7,15},{16,24},{17,... | collective-permute-start | bytes 786440 | tf_op jit(solution)/shard_map/ppermute | solution.py:136
  183.3 22.8 %all-to-all-start.9 = ((bf16[16,48,256]{2,1,0:T(8,128)(2,1)}), bf16[16,48,256]{2,1,0:T(8,128)(2,1)S(1)}, u32[]{:S(2)}, u32[]{:S(2)}) async-start(bf16[16,48,256]{2,1,0:T(8,128)(2,1)} %bitcast.25), calls=%async_computation.9 | async-start | bytes 786432 | tf_op jit(solution)/shard_map/all_to_all | solution.py:24
  193.7 3.1 %collective-permute-start.6 = (bf16[48,256]{1,0:T(8,128)(2,1)S(1)}, bf16[48,256]{1,0:T(8,128)(2,1)S(1)}, u32[]{:S(2)}, u32[]{:S(2)}) collective-permute-start(bf16[48,256]{1,0:T(8,128)(2,1)S(1)} %slice.85), channel_id=1, source_target_pairs={{0,16},{16,0},{1,17},{17,1},{2,18},{18,2},{3,19},{19,3},{4,20},{20... | collective-permute-start | bytes 73736 | tf_op jit(solution)/shard_map/ppermute | solution.py:96
Sparse Core Ops, SparseCore 0:
  20.4 66.5 all-gather.3
  89.1 29.3 all-gather.5

commit v12 on v8

--- a/solution.py
+++ b/solution.py
@@ -158,10 +158,10 @@
         output_weight,
         gate,
     )
-    first_sum, second_weight = lax.optimization_barrier((first_sum, second_weight))
     first_sum = jnp.concatenate([first_sum[:, :columns], first_sum[:, columns:]])
     first_sum = first_sum.reshape(tensor_count, -1, columns)
     summed = jnp.sum(exchange(first_sum, "tp").astype(F32), axis=0).astype(BF16)
+    summed, second_weight = lax.optimization_barrier((summed, second_weight))
     everywhere = gathered(summed, ("section", "tp"))[:tensor_count]
     everywhere = everywhere.reshape(2, chips * positions, -1).astype(F32)
     everywhere = jnp.concatenate([everywhere[0], everywhere[1]], axis=1)

time: 213 us -> 210 us (0.986)
  no operation moved by 1% of the time
where the time goes in v12:
time: 210 us; the launch traced here: 208 us
  starting transfers between devices  61.1 us (29%)
  blocking collectives  60 us (29%)
  waiting for transfers between devices  45.5 us (22%)
  between operations  15.9 us (8%)
  matrix products  11.3 us (5%)
  local copies, waits for them, and re-layouts  10.2 us (5%)
  other arithmetic  3.55 us (2%)
    all_to_all x4, blocking collectives, exchange(): return lax.all_to_all(blocks, axis, 0, 0, tiled=True)  60 us
    all_to_all x7, starting transfers between devices, exchange(): return lax.all_to_all(blocks, axis, 0, 0, tiled=True)  42.3 us
    all_to_all x7, waiting for transfers between devices, exchange(): return lax.all_to_all(blocks, axis, 0, 0, tiled=True)  35.3 us
    ppermute x4, starting transfers between devices, to_other_core(): return lax.ppermute(block, 'core', SWAP)  11.2 us
    dot_general x2, matrix products, projected(): product = jnp.dot(rows, weight, preferred_element_type=F32)  8.95 us
    ppermute x2, waiting for transfers between devices, handed(): return lax.ppermute(partial_sum, 'section', [direction]).astype(F32)  6.45 us
  transfers between devices with their start and end apart: 16, of which 9 were waited for; matrix products, arithmetic and copies ran while one was open for 9% of the time, Pallas kernels for 0%

profile of v12, /device:TPU:1, one launch (start us, length us, event | category | flops | bytes accessed | tf_op | source)
XLA Modules:
  0.0 208.5 jit_solution(6494588956027623885)
XLA Ops:
  9.1 3.5 %all-to-all-start = ((bf16[2,32,4096]{2,1,0:T(8,128)(2,1)}), bf16[2,32,4096]{2,1,0:T(8,128)(2,1)S(1)}, u32[]{:S(2)}, u32[]{:S(2)}) async-start(bf16[2,32,4096]{2,1,0:T(8,128)(2,1)} %deal_halves.1), calls=%async_computation | async-start | bytes 1048576 | tf_op jit(solution)/shard_map/all_to_all | solution.py:24
  12.7 4.0 %collective-permute-start.2 = (bf16[128,256]{1,0:T(8,128)(2,1)S(1)}, bf16[128,256]{1,0:T(8,128)(2,1)S(1)}, u32[]{:S(2)}, u32[]{:S(2)}) collective-permute-start(bf16[128,256]{1,0:T(8,128)(2,1)S(1)} %get-tuple-element.42), channel_id=1, source_target_pairs={{0,8},{8,0},{1,9},{9,1},{2,10},{10,2},{3,11},{11,3},{4,12},{12,4},... | collective-permute-start | bytes 196616 | tf_op jit(solution)/shard_map/ppermute | solution.py:110
  16.7 2.7 %collective-permute-done.2 = bf16[128,256]{1,0:T(8,128)(2,1)S(1)} collective-permute-done((bf16[128,256]{1,0:T(8,128)(2,1)S(1)}, bf16[128,256]{1,0:T(8,128)(2,1)S(1)}, u32[]{:S(2)}, u32[]{:S(2)}) %collective-permute-start.2) | collective-permute-done | bytes 65568 | tf_op jit(solution)/shard_map/ppermute | solution.py:110
  20.3 24.0 %all_to_all.55 = bf16[4,2,128,256]{3,2,1,0:T(8,128)(2,1)S(1)} all-to-all(bf16[4,2,128,256]{3,2,1,0:T(8,128)(2,1)S(1)} %broadcast_in_dim.36), channel_id=1, replica_groups=mesh['far'=4,'row'=4,'core'=2,'section'=2,'tp'=8] {'far'}, dimensions={0} | all-to-all | bytes 1048576 | tf_op jit(solution)/shard_map/all_to_all | solution.py:24
  45.0 1.1 broadcast_in_dim.38
  46.1 4.0 %all-to-all-start.2 = ((bf16[4,4,128,256]{3,2,1,0:T(8,128)(2,1)}), bf16[4,4,128,256]{3,2,1,0:T(8,128)(2,1)S(1)}, u32[]{:S(2)}, u32[]{:S(2)}) async-start(bf16[4,4,128,256]{3,2,1,0:T(8,128)(2,1)} %broadcast_in_dim.38), calls=%async_computation.2 | async-start | bytes 2097152 | tf_op jit(solution)/shard_map/all_to_all | solution.py:24
  50.2 4.9 %collective-permute-start.1 = (bf16[256,1024]{1,0:T(8,128)(2,1)S(1)}, bf16[256,1024]{1,0:T(8,128)(2,1)}, u32[]{:S(2)}, u32[]{:S(2)}) collective-permute-start(bf16[256,1024]{1,0:T(8,128)(2,1)S(1)} %bitcast.69), channel_id=1, source_target_pairs={{0,16},{16,0},{1,17},{17,1},{2,18},{18,2},{3,19},{19,3},{4,20},{20... | collective-permute-start | bytes 1572872 | tf_op jit(solution)/shard_map/ppermute | solution.py:96
  55.3 1.9 collective-permute-start
  57.2 2.4 %collective-permute-start.3 = (bf16[1024,256]{1,0:T(8,128)(2,1)S(1)}, bf16[1024,256]{1,0:T(8,128)(2,1)}, u32[]{:S(2)}, u32[]{:S(2)}) collective-permute-start(bf16[1024,256]{1,0:T(8,128)(2,1)S(1)} %bitcast.71), channel_id=1, source_target_pairs={{0,16},{16,0},{1,17},{17,1},{2,18},{18,2},{3,19},{19,3},{4,20},{20... | collective-permute-start | bytes 1572872 | tf_op jit(solution)/shard_map/ppermute | solution.py:96
  59.7 1.1 pad_maximum_fusion
  60.8 1.2 all-to-all-done.2
  62.3 10.1 %all_to_all.56 = bf16[2,4,4,128,256]{4,3,2,1,0:T(8,128)(2,1)} all-to-all(bf16[2,4,4,128,256]{4,3,2,1,0:T(8,128)(2,1)S(1)} %broadcast_in_dim.39), channel_id=1, replica_groups=mesh['far'=4,'row'=4,'core'=2,'section'=2,'tp'=8] {'core'}, dimensions={0} | all-to-all | bytes 4194304 | tf_op jit(solution)/shard_map/all_to_all | solution.py:24
  73.4 5.4 %all-to-all-start.4 = ((bf16[16,3,1024]{2,1,0:T(4,128)(2,1)}), bf16[16,3,1024]{2,1,0:T(4,128)(2,1)S(1)}, u32[]{:S(2)}, u32[]{:S(2)}) async-start(bf16[16,3,1024]{2,1,0:T(4,128)(2,1)} %reshape.274), calls=%async_computation.4 | async-start | bytes 262144 | tf_op jit(solution)/shard_map/all_to_all | solution.py:24
  78.8 1.1 pad_maximum_fusion.1
  80.0 8.0 %all-to-all-done.4 = bf16[16,3,1024]{2,1,0:T(4,128)(2,1)S(1)} async-done(((bf16[16,3,1024]{2,1,0:T(4,128)(2,1)}), bf16[16,3,1024]{2,1,0:T(4,128)(2,1)S(1)}, u32[]{:S(2)}, u32[]{:S(2)}) %all-to-all-start.4) | async-done | bytes 98336 | tf_op jit(solution)/shard_map/all_to_all | solution.py:24
  88.8 4.1 %fusion.36 = (bf16[512,256]{1,0:T(8,128)(2,1)S(1)}, f32[512,256]{1,0:T(8,128)S(1)}) fusion(bf16[512,4096]{1,0:T(8,128)(2,1)} %all-gather.4.cloned.1.call-done, bf16[4096,256]{1,0:T(8,128)(2,1)} %bitcast.65), kind=kOutput, calls=%fused_computation.96 | convolution fusion | flops 1073872896 | bytes 7077888 | tf_op jit(solution)/shard_map/dot_general | solution.py:58
  92.9 1.3 collective-permute-start.4
  94.4 6.5 %collective-permute-done.4 = bf16[512,256]{1,0:T(8,128)(2,1)S(1)} collective-permute-done((bf16[512,256]{1,0:T(8,128)(2,1)S(1)}, bf16[512,256]{1,0:T(8,128)(2,1)S(1)}, u32[]{:S(2)}, u32[]{:S(2)}) %collective-permute-start.4) | collective-permute-done | bytes 262176 | tf_op jit(solution)/shard_map/ppermute | solution.py:136
  102.4 9.1 %all-to-all-start.5 = ((bf16[16,3,1024]{2,1,0:T(4,128)(2,1)}), bf16[16,3,1024]{2,1,0:T(4,128)(2,1)S(1)}, u32[]{:S(2)}, u32[]{:S(2)}) async-start(bf16[16,3,1024]{2,1,0:T(4,128)(2,1)} %broadcast_in_dim.43), calls=%async_computation.5 | async-start | bytes 262144 | tf_op jit(solution)/shard_map/all_to_all | solution.py:24
  112.1 8.7 %all-to-all-done.5 = bf16[16,3,1024]{2,1,0:T(4,128)(2,1)S(1)} async-done(((bf16[16,3,1024]{2,1,0:T(4,128)(2,1)}), bf16[16,3,1024]{2,1,0:T(4,128)(2,1)S(1)}, u32[]{:S(2)}, u32[]{:S(2)}) %all-to-all-start.5) | async-done | bytes 98336 | tf_op jit(solution)/shard_map/all_to_all | solution.py:24
  121.2 11.5 %all_to_all.57 = bf16[8,12,256]{2,1,0:T(8,128)(2,1)S(1)} all-to-all(bf16[8,12,256]{2,1,0:T(8,128)(2,1)S(1)} %reshape.277), channel_id=1, replica_groups=mesh['far'=4,'row'=4,'core'=2,'section'=2,'tp'=8] {'tp'}, dimensions={0} | all-to-all | bytes 98304 | tf_op jit(solution)/shard_map/all_to_all | solution.py:24
  133.5 3.5 %all-to-all-start.7 = ((bf16[16,12,256]{2,1,0:T(8,128)(2,1)}), bf16[16,12,256]{2,1,0:T(8,128)(2,1)S(1)}, u32[]{:S(2)}, u32[]{:S(2)}) async-start(bf16[16,12,256]{2,1,0:T(8,128)(2,1)} %broadcast_in_dim.80), calls=%async_computation.7 | async-start | bytes 262144 | tf_op jit(solution)/shard_map/all_to_all | solution.py:24
  137.0 4.8 %fusion.38 = (bf16[512,256]{1,0:T(8,128)(2,1)}, f32[512,256]{1,0:T(8,128)S(1)}) fusion(bf16[512,4096]{1,0:T(8,128)(2,1)} %all-gather.4.cloned.1.call-done, bf16[4096,256]{1,0:T(8,128)(2,1)} %bitcast.77), kind=kOutput, calls=%fused_computation.98 | convolution fusion | flops 1073872896 | bytes 7077888 | tf_op jit(solution)/shard_map/dot_general | solution.py:58
  141.8 2.5 %all-to-all-done.7 = bf16[16,12,256]{2,1,0:T(8,128)(2,1)S(1)} async-done(((bf16[16,12,256]{2,1,0:T(8,128)(2,1)}), bf16[16,12,256]{2,1,0:T(8,128)(2,1)S(1)}, u32[]{:S(2)}, u32[]{:S(2)}) %all-to-all-start.7) | async-done | bytes 98336 | tf_op jit(solution)/shard_map/all_to_all | solution.py:24
  145.5 3.5 %all-to-all-start.8 = ((bf16[16,3,1024]{2,1,0:T(4,128)(2,1)}), bf16[16,3,1024]{2,1,0:T(4,128)(2,1)S(1)}, u32[]{:S(2)}, u32[]{:S(2)}) async-start(bf16[16,3,1024]{2,1,0:T(4,128)(2,1)} %reshape.283), calls=%async_computation.8 | async-start | bytes 262144 | tf_op jit(solution)/shard_map/all_to_all | solution.py:24
  149.0 2.3 %collective-permute-start.5 = (bf16[512,256]{1,0:T(8,128)(2,1)}, bf16[512,256]{1,0:T(8,128)(2,1)S(1)}, u32[]{:S(2)}, u32[]{:S(2)}) collective-permute-start(bf16[512,256]{1,0:T(8,128)(2,1)} %get-tuple-element.32), channel_id=1, source_target_pairs={{0,8},{1,9},{2,10},{3,11},{4,12},{5,13},{6,14},{7,15},{16,24},{17,... | collective-permute-start | bytes 786440 | tf_op jit(solution)/shard_map/ppermute | solution.py:136
  151.3 7.0 %all-to-all-done.8 = bf16[16,3,1024]{2,1,0:T(4,128)(2,1)S(1)} async-done(((bf16[16,3,1024]{2,1,0:T(4,128)(2,1)}), bf16[16,3,1024]{2,1,0:T(4,128)(2,1)S(1)}, u32[]{:S(2)}, u32[]{:S(2)}) %all-to-all-start.8) | async-done | bytes 98336 | tf_op jit(solution)/shard_map/all_to_all | solution.py:24
  159.4 14.4 %all_to_all.58 = bf16[16,3,1024]{2,1,0:T(4,128)(2,1)S(1)} all-to-all(bf16[16,3,1024]{2,1,0:T(4,128)(2,1)S(1)} %broadcast_in_dim.82), channel_id=1, replica_groups=mesh['far'=4,'row'=4,'core'=2,'section'=2,'tp'=8] {'far','row'}, dimensions={0} | all-to-all | bytes 196608 | tf_op jit(solution)/shard_map/all_to_all | solution.py:24
  175.0 13.3 %all-to-all-start.10 = ((bf16[16,48,256]{2,1,0:T(8,128)(2,1)}), bf16[16,48,256]{2,1,0:T(8,128)(2,1)S(1)}, u32[]{:S(2)}, u32[]{:S(2)}) async-start(bf16[16,48,256]{2,1,0:T(8,128)(2,1)} %bitcast.25), calls=%async_computation.10 | async-start | bytes 786432 | tf_op jit(solution)/shard_map/all_to_all | solution.py:24
  188.3 2.0 collective-permute-start.6
  190.3 1.0 collective-permute-done.6
  192.9 7.8 %all-to-all-done.10 = bf16[16,48,256]{2,1,0:T(8,128)(2,1)S(1)} async-done(((bf16[16,48,256]{2,1,0:T(8,128)(2,1)}), bf16[16,48,256]{2,1,0:T(8,128)(2,1)S(1)}, u32[]{:S(2)}, u32[]{:S(2)}) %all-to-all-start.10) | async-done | bytes 393248 | tf_op jit(solution)/shard_map/all_to_all | solution.py:24
  (96 shorter events, 13.8 us)
Async XLA Ops:
  7.2 1.0 copy-start
  8.2 4.5 %copy-start.4 = (bf16[1,256,1,256]{3,1,2,0:T(8,128)(2,1)S(1)}, bf16[1,256,1,256]{3,1,2,0:T(8,128)(2,1)}, u32[]{:S(2)}) copy-start(bf16[1,256,1,256]{3,1,2,0:T(8,128)(2,1)} %param.12) | copy-start | bytes 393220
  9.1 10.3 %all-to-all-start = ((bf16[2,32,4096]{2,1,0:T(8,128)(2,1)}), bf16[2,32,4096]{2,1,0:T(8,128)(2,1)S(1)}, u32[]{:S(2)}, u32[]{:S(2)}) async-start(bf16[2,32,4096]{2,1,0:T(8,128)(2,1)} %deal_halves.1), calls=%async_computation | async-start | bytes 1048576 | tf_op jit(solution)/shard_map/all_to_all | solution.py:24
  12.6 75.5 %all-gather.4.cloned.1.call-start = ((), (), s32[]{:S(2)}) async-start(), calls=%async_computation.11 | async-start | bytes 4718592 | tf_op jit(solution)/shard_map/all_gather | solution.py:111
  12.7 6.7 %collective-permute-start.2 = (bf16[128,256]{1,0:T(8,128)(2,1)S(1)}, bf16[128,256]{1,0:T(8,128)(2,1)S(1)}, u32[]{:S(2)}, u32[]{:S(2)}) collective-permute-start(bf16[128,256]{1,0:T(8,128)(2,1)S(1)} %get-tuple-element.42), channel_id=1, source_target_pairs={{0,8},{8,0},{1,9},{9,1},{2,10},{10,2},{3,11},{11,3},{4,12},{12,4},... | collective-permute-start | bytes 196616 | tf_op jit(solution)/shard_map/ppermute | solution.py:110
  19.4 0.8 copy-start.1
  44.3 5.9 %copy-start.5 = (bf16[32,3,256]{2,0,1:T(8,128)(2,1)S(1)}, bf16[32,3,256]{2,0,1:T(8,128)(2,1)}, u32[]{:S(2)}) copy-start(bf16[32,3,256]{2,0,1:T(8,128)(2,1)} %param.9) | copy-start | bytes 147460
  44.3 5.9 %copy-start.2 = (bf16[1,256,1024]{2,1,0:T(8,128)(2,1)S(1)}, bf16[1,256,1024]{2,1,0:T(8,128)(2,1)}, u32[]{:S(2)}) copy-start(bf16[1,256,1024]{2,1,0:T(8,128)(2,1)} %param.14) | copy-start | bytes 1572868
  45.0 12.2 %copy-start.3 = (bf16[1,1024,256]{2,1,0:T(8,128)(2,1)S(1)}, bf16[1,1024,256]{2,1,0:T(8,128)(2,1)}, u32[]{:S(2)}) copy-start(bf16[1,1024,256]{2,1,0:T(8,128)(2,1)} %param.16) | copy-start | bytes 1572868
  46.1 15.9 %all-to-all-start.2 = ((bf16[4,4,128,256]{3,2,1,0:T(8,128)(2,1)}), bf16[4,4,128,256]{3,2,1,0:T(8,128)(2,1)S(1)}, u32[]{:S(2)}, u32[]{:S(2)}) async-start(bf16[4,4,128,256]{3,2,1,0:T(8,128)(2,1)} %broadcast_in_dim.38), calls=%async_computation.2 | async-start | bytes 2097152 | tf_op jit(solution)/shard_map/all_to_all | solution.py:24
  50.2 9.5 %collective-permute-start.1 = (bf16[256,1024]{1,0:T(8,128)(2,1)S(1)}, bf16[256,1024]{1,0:T(8,128)(2,1)}, u32[]{:S(2)}, u32[]{:S(2)}) collective-permute-start(bf16[256,1024]{1,0:T(8,128)(2,1)S(1)} %bitcast.69), channel_id=1, source_target_pairs={{0,16},{16,0},{1,17},{17,1},{2,18},{18,2},{3,19},{19,3},{4,20},{20... | collective-permute-start | bytes 1572872 | tf_op jit(solution)/shard_map/ppermute | solution.py:96
  55.3 4.4 %collective-permute-start = (bf16[48,256]{1,0:T(8,128)(2,1)S(1)}, bf16[48,256]{1,0:T(8,128)(2,1)S(1)}, u32[]{:S(2)}, u32[]{:S(2)}) collective-permute-start(bf16[48,256]{1,0:T(8,128)(2,1)S(1)} %select_n.145), channel_id=1, source_target_pairs={{0,16},{16,0},{1,17},{17,1},{2,18},{18,2},{3,19},{19,3},{4,20},{20... | collective-permute-start | bytes 73736 | tf_op jit(solution)/shard_map/ppermute | solution.py:96
  57.2 21.6 %collective-permute-start.3 = (bf16[1024,256]{1,0:T(8,128)(2,1)S(1)}, bf16[1024,256]{1,0:T(8,128)(2,1)}, u32[]{:S(2)}, u32[]{:S(2)}) collective-permute-start(bf16[1024,256]{1,0:T(8,128)(2,1)S(1)} %bitcast.71), channel_id=1, source_target_pairs={{0,16},{16,0},{1,17},{17,1},{2,18},{18,2},{3,19},{19,3},{4,20},{20... | collective-permute-start | bytes 1572872 | tf_op jit(solution)/shard_map/ppermute | solution.py:96
  72.4 16.4 %copy-start.6 = (bf16[1,128]{1,0:T(2,128)(2,1)S(1)}, bf16[1,128]{1,0:T(2,128)(2,1)}, u32[]{:S(2)}) copy-start(bf16[1,128]{1,0:T(2,128)(2,1)} %param.15) | copy-start | bytes 772
  72.4 16.4 %copy-start.7 = (bf16[1,128]{1,0:T(2,128)(2,1)S(1)}, bf16[1,128]{1,0:T(2,128)(2,1)}, u32[]{:S(2)}) copy-start(bf16[1,128]{1,0:T(2,128)(2,1)} %param.13) | copy-start | bytes 772
  73.4 14.6 %all-to-all-start.4 = ((bf16[16,3,1024]{2,1,0:T(4,128)(2,1)}), bf16[16,3,1024]{2,1,0:T(4,128)(2,1)S(1)}, u32[]{:S(2)}, u32[]{:S(2)}) async-start(bf16[16,3,1024]{2,1,0:T(4,128)(2,1)} %reshape.274), calls=%async_computation.4 | async-start | bytes 262144 | tf_op jit(solution)/shard_map/all_to_all | solution.py:24
  78.8 54.0 %all-gather.6.cloned.1.call-start = ((), (), s32[]{:S(2)}) async-start(), calls=%async_computation.12 | async-start | bytes 2359296 | tf_op jit(solution)/shard_map/all_gather | solution.py:149
  92.9 7.9 %collective-permute-start.4 = (bf16[512,256]{1,0:T(8,128)(2,1)S(1)}, bf16[512,256]{1,0:T(8,128)(2,1)S(1)}, u32[]{:S(2)}, u32[]{:S(2)}) collective-permute-start(bf16[512,256]{1,0:T(8,128)(2,1)S(1)} %get-tuple-element.51), channel_id=1, source_target_pairs={{8,0},{9,1},{10,2},{11,3},{12,4},{13,5},{14,6},{15,7},{24,16},{25,... | collective-permute-start | bytes 786440 | tf_op jit(solution)/shard_map/ppermute | solution.py:136
  102.4 18.4 %all-to-all-start.5 = ((bf16[16,3,1024]{2,1,0:T(4,128)(2,1)}), bf16[16,3,1024]{2,1,0:T(4,128)(2,1)S(1)}, u32[]{:S(2)}, u32[]{:S(2)}) async-start(bf16[16,3,1024]{2,1,0:T(4,128)(2,1)} %broadcast_in_dim.43), calls=%async_computation.5 | async-start | bytes 262144 | tf_op jit(solution)/shard_map/all_to_all | solution.py:24
  133.5 10.9 %all-to-all-start.7 = ((bf16[16,12,256]{2,1,0:T(8,128)(2,1)}), bf16[16,12,256]{2,1,0:T(8,128)(2,1)S(1)}, u32[]{:S(2)}, u32[]{:S(2)}) async-start(bf16[16,12,256]{2,1,0:T(8,128)(2,1)} %broadcast_in_dim.80), calls=%async_computation.7 | async-start | bytes 262144 | tf_op jit(solution)/shard_map/all_to_all | solution.py:24
  145.5 12.8 %all-to-all-start.8 = ((bf16[16,3,1024]{2,1,0:T(4,128)(2,1)}), bf16[16,3,1024]{2,1,0:T(4,128)(2,1)S(1)}, u32[]{:S(2)}, u32[]{:S(2)}) async-start(bf16[16,3,1024]{2,1,0:T(4,128)(2,1)} %reshape.283), calls=%async_computation.8 | async-start | bytes 262144 | tf_op jit(solution)/shard_map/all_to_all | solution.py:24
  149.0 9.5 %collective-permute-start.5 = (bf16[512,256]{1,0:T(8,128)(2,1)}, bf16[512,256]{1,0:T(8,128)(2,1)S(1)}, u32[]{:S(2)}, u32[]{:S(2)}) collective-permute-start(bf16[512,256]{1,0:T(8,128)(2,1)} %get-tuple-element.32), channel_id=1, source_target_pairs={{0,8},{1,9},{2,10},{3,11},{4,12},{5,13},{6,14},{7,15},{16,24},{17,... | collective-permute-start | bytes 786440 | tf_op jit(solution)/shard_map/ppermute | solution.py:136
  175.0 25.7 %all-to-all-start.10 = ((bf16[16,48,256]{2,1,0:T(8,128)(2,1)}), bf16[16,48,256]{2,1,0:T(8,128)(2,1)S(1)}, u32[]{:S(2)}, u32[]{:S(2)}) async-start(bf16[16,48,256]{2,1,0:T(8,128)(2,1)} %bitcast.25), calls=%async_computation.10 | async-start | bytes 786432 | tf_op jit(solution)/shard_map/all_to_all | solution.py:24
  188.3 3.1 %collective-permute-start.6 = (bf16[48,256]{1,0:T(8,128)(2,1)S(1)}, bf16[48,256]{1,0:T(8,128)(2,1)S(1)}, u32[]{:S(2)}, u32[]{:S(2)}) collective-permute-start(bf16[48,256]{1,0:T(8,128)(2,1)S(1)} %slice.85), channel_id=1, source_target_pairs={{0,16},{16,0},{1,17},{17,1},{2,18},{18,2},{3,19},{19,3},{4,20},{20... | collective-permute-start | bytes 73736 | tf_op jit(solution)/shard_map/ppermute | solution.py:96
Sparse Core Ops, SparseCore 0:
  20.4 66.5 all-gather.3
  89.1 29.3 all-gather.5
